TPU v7x, 128 devices: a whole 4x4x4 slice. The times are simulated.
128 devices in a mesh: ka: 4 (over z_hi, core), ga: 32 (over y, z_lo, x).
Axes of the slice: x: 4, y: 4, z: 4 (z_hi: 2, z_lo: 2; z = z_hi * 2 + z_lo), core: 2. Of those that a mesh axis runs over, the one named last changes fastest.
Arguments:
- pair_vc: bfloat16 [384, 2048, 128], P('ka', 'ga'), may hold values from -6 to 6
- coulomb: float32 [2048], P('ga'), may hold values from 0.01 to 0.1
- dens_cc: bfloat16 [2, 384, 2048, 128], P(None, 'ka', 'ga'), may hold values from -1.5 to 1.5
- dens_vv: bfloat16 [2, 384, 2048, 128], P(None, 'ka', 'ga'), may hold values from -1.5 to 1.5
- screen: bfloat16 [2, 2048, 2048], P(None, 'ga'), may hold values from -0.125 to 0.125
- offsets: int32 [2, 2], replicated, may hold values from 0 to 23, as said below
Outputs:
- kernel: float32 [2, 2, 384, 4096], P(None, None, ('ka', 'ga'))
Inputs may be any that keep to these rules, and one draw needn't show every extreme that they name: offsets[o, 0] is 1 to 4; one offset, which one drawn from the seed, has offsets[o, 0] = 4 and offsets[o, 1] = 23, the other has offsets[o, 1] = 0.
All inputs are finite; a program needn't handle non-finite values.
Results may differ from a plain program's by a relative error of at most 0.0029.
Values may be sent and summed in bfloat16 or wider, within the bound.
No kernel may reach another device: no remote copies, remote signals or barrier semaphores. Data moves between devices by JAX's collectives and lax.ppermute only.
A program may use at most 192 MiB of HBM per device.

v0:
```python
import jax
import jax.numpy as jnp
from jax import lax
from jax.sharding import PartitionSpec as P

NV = 8
NC = 8
NKY = 24
KX_DEV = 4
NOFF = 2


def from_behind(array, axis, by):
    length = lax.axis_size(axis)
    return lax.ppermute(array, axis, [(i, (i + by) % length) for i in range(length)])


def shifted_rows(joined, step_x, step_y):
    picked = lax.dynamic_slice_in_dim(joined, step_x, KX_DEV, 0)
    twice = jnp.concatenate([picked, picked], axis=1)
    return lax.dynamic_slice_in_dim(twice, step_y, NKY, 1)


def pair_products(left_side, right_side):
    left_half = left_side.shape[-1] // 2
    right_half = right_side.shape[-1] // 2
    full = jnp.einsum("kgp,kgq->kpq", left_side, right_side, preferred_element_type=jnp.float32)
    real_part = full[:, :left_half, :right_half] + full[:, left_half:, right_half:]
    imag_part = full[:, :left_half, right_half:] - full[:, left_half:, :right_half]
    return jnp.stack([real_part, imag_part])


def summed_exchange(scaled, moved):
    partial_terms = jnp.stack(
        [pair_products(scaled, moved[offset_index]) for offset_index in range(NOFF)]
    )
    return lax.psum_scatter(partial_terms, "ga", scatter_dimension=2, tiled=True)


def local(pair_vc, coulomb, dens_cc, dens_vv, screen, offsets):
    local_k = pair_vc.shape[0]
    slab = pair_vc.shape[1]
    width = pair_vc.shape[2]
    pairs = width // 2
    shards = lax.axis_size("ga")
    few_k = local_k // shards
    scaled = (coulomb[None, :, None] * pair_vc.astype(jnp.float32)).astype(jnp.bfloat16)
    ahead = from_behind(pair_vc, "ka", -1)
    joined = jnp.concatenate([pair_vc, ahead], axis=0).reshape(2 * KX_DEV, NKY, slab, width)
    moved = jnp.stack(
        [
            shifted_rows(joined, offsets[offset_index, 0], offsets[offset_index, 1]).reshape(
                local_k, slab, width
            )
            for offset_index in range(NOFF)
        ]
    )
    cc_x, vv_x = (
        lax.all_to_all(dens_cc, "ga", split_axis=1, concat_axis=2, tiled=True),
        lax.all_to_all(dens_vv, "ga", split_axis=1, concat_axis=2, tiled=True),
    )
    exch = summed_exchange(scaled, moved)
    blocks = []
    for offset_index in range(NOFF):
        mc_here = cc_x[offset_index]
        mv_here = vv_x[offset_index]

        def add_one(carry, piece, start, mc_here=mc_here, mv_here=mv_here):
            image = jnp.einsum(
                "gh,khq->kgq", piece, mv_here, preferred_element_type=jnp.float32
            ).astype(jnp.bfloat16)
            return pair_products(mc_here, image)

        zeros_one = jnp.zeros((2, few_k, NC * NC, NV * NV), jnp.float32)
        blocks.append(
            add_one(
                zeros_one,
                lax.all_gather(screen[offset_index], "ga", axis=0, tiled=True),
                jnp.int32(0),
            )
        )
    direct = jnp.stack(blocks)
    shaped = direct.reshape(NOFF, 2, few_k, NC, NC, NV, NV)
    shaped = jnp.transpose(shaped, (0, 1, 2, 5, 3, 6, 4)).reshape(NOFF, 2, few_k, pairs * pairs)
    return 2.0 * exch.reshape(NOFF, 2, few_k, pairs * pairs) - shaped


def solution(mesh):
    placed = (
        P("ka", "ga", None),
        P("ga"),
        P(None, "ka", "ga", None),
        P(None, "ka", "ga", None),
        P(None, "ga", None),
        P(),
    )
    return jax.shard_map(
        local,
        mesh=mesh,
        in_specs=placed,
        out_specs=P(None, None, ("ka", "ga"), None),
        check_vma=False,
    )
```

profile of v0, /device:TPU:2, one launch (start us, length us, event | category | flops | bytes accessed | tf_op | source)
XLA Modules:
  0.0 841.1 jit_solution(16399707312251802117)
XLA Ops:
  6.5 0.0 all-reduce.3.cloned.1.call-start
  6.5 3.3 collective-permute-start
  9.9 1.5 fusion.25
  19.0 9.1 %collective-permute-done = bf16[96,64,128]{2,1,0:T(8,128)(2,1)S(1)} collective-permute-done((bf16[96,64,128]{2,1,0:T(8,128)(2,1)}, bf16[96,64,128]{2,1,0:T(8,128)(2,1)S(1)}, u32[]{:S(2)}, u32[]{:S(2)}) %collective-permute-start) | collective-permute-done | bytes 1572896 | tf_op jit(solution)/shard_map/ppermute | solution.py:15
  28.1 1.7 pad_maximum_fusion.1
  29.8 0.7 constant_dynamic-slice_fusion.1
  30.5 0.0 copy-start
  30.5 0.0 copy-start.8
  30.5 1.4 fusion.14
  31.9 0.0 copy-done
  31.9 0.0 copy-done.8
  31.9 1.1 fusion.21
  33.0 3.4 fusion.7
  36.4 1.1 fusion.20
  37.5 4.3 fusion.5
  41.8 2.7 maximum_bitcast_fusion
  44.6 0.1 copy-done.2
  44.7 1.0 copy-done.3
  45.6 3.3 maximum_bitcast_fusion.1
  48.9 9.5 %pad_maximum_fusion = f32[2,2,96,64,64]{4,3,2,1,0:T(8,128)} fusion(f32[1,2,96,64,64]{4,3,2,1,0:T(8,128)} %maximum_bitcast_fusion.1, f32[1,2,96,64,64]{4,3,2,1,0:T(8,128)S(1)} %maximum_bitcast_fusion), kind=kLoop, calls=%fused_computation | loop fusion | flops 1572864 | bytes 12582912 | tf_op jit(solution)/shard_map/stack | solution.py:34
  58.4 0.0 all-reduce.3.cloned.1.call-update
  58.5 0.0 all-gather.5.cloned.1.call-start
  58.5 2.0 fusion.24
  60.6 0.0 all-gather.5.cloned.1.call-update
  60.6 0.2 all-gather.7.cloned.1.call-start
  60.8 0.5 all-gather.7.cloned.1.call-update
  61.3 0.0 copy-done.5
  61.3 2.7 copy.21
  64.0 8.1 all-to-all-start
  72.1 4.6 copy.25
  76.6 53.4 %all-to-all-done = bf16[2,96,64,128]{3,2,0,1:T(8,128)(2,1)S(1)} async-done(((bf16[2,96,64,128]{3,2,0,1:T(8,128)(2,1)}), bf16[2,96,64,128]{3,2,0,1:T(8,128)(2,1)S(1)}, u32[]{:S(2)}, u32[]{:S(2)}) %all-to-all-start) | async-done | bytes 3145760 | tf_op jit(solution)/shard_map/all_to_all | solution.py:60
  130.1 1.7 copy-done.1
  131.7 21.2 %all-to-all-start.1 = ((bf16[2,96,64,128]{3,2,0,1:T(8,128)(2,1)}), bf16[2,96,64,128]{3,2,0,1:T(8,128)(2,1)S(1)}, u32[]{:S(2)}, u32[]{:S(2)}) async-start(bf16[2,96,64,128]{3,2,0,1:T(8,128)(2,1)} %copy.25), calls=%async_computation.1 | async-start | bytes 6291456 | tf_op jit(solution)/shard_map/all_to_all | solution.py:59
  152.9 0.0 copy-done.9
  152.9 0.6 dynamic-slice
  154.2 2.7 copy.22
  156.9 1.9 fusion.22
  158.8 1.3 copy.23
  160.1 49.5 %all-to-all-done.1 = bf16[2,96,64,128]{3,2,0,1:T(8,128)(2,1)S(1)} async-done(((bf16[2,96,64,128]{3,2,0,1:T(8,128)(2,1)}), bf16[2,96,64,128]{3,2,0,1:T(8,128)(2,1)S(1)}, u32[]{:S(2)}, u32[]{:S(2)}) %all-to-all-start.1) | async-done | bytes 3145760 | tf_op jit(solution)/shard_map/all_to_all | solution.py:59
  209.6 0.9 copy.37
  210.6 0.5 copy-done.4
  211.0 0.1 copy.27
  211.2 0.0 copy-start.6
  211.2 3.0 fusion.23
  214.2 267.3 %all-reduce.3.cloned.1.call-done = f32[2,2,96,64,64]{4,3,2,1,0:T(8,128)} async-done(((f32[2,2,96,64,64]{4,3,2,1,0:T(8,128)}), f32[2,2,96,64,64]{4,3,2,1,0:T(8,128)}) %all-reduce.3.cloned.1.call-update) | async-done | bytes 6291472
  481.5 1.0 dynamic-slice_multiply_fusion
  482.5 0.9 reshape.37
  483.4 167.6 %all-gather.5.cloned.1.call-done = bf16[1,2048,2048]{2,1,0:T(8,128)(2,1)} async-done(((bf16[1,64,2048]{2,1,0:T(8,128)(2,1)}), bf16[1,2048,2048]{2,1,0:T(8,128)(2,1)}) %all-gather.5.cloned.1.call-update) | async-done | bytes 8388624 | tf_op jit(solution)/shard_map/all_gather | solution.py:78
  651.0 0.0 copy-done.6
  651.0 7.7 convolution_bitcast_fusion.1
  658.6 0.1 slice_add_fusion.3
  658.7 0.2 stack.59
  659.0 0.2 stack.60
  659.3 161.6 %all-gather.7.cloned.1.call-done = bf16[1,2048,2048]{2,1,0:T(8,128)(2,1)} async-done(((bf16[1,64,2048]{2,1,0:T(8,128)(2,1)}), bf16[1,2048,2048]{2,1,0:T(8,128)(2,1)}) %all-gather.7.cloned.1.call-update) | async-done | bytes 8388624 | tf_op jit(solution)/shard_map/all_gather | solution.py:78
  820.9 7.7 convolution_bitcast_fusion
  828.5 0.1 slice_add_fusion.2
  828.7 0.5 stack.62
  829.1 0.2 stack.63
  829.4 0.3 maximum_bitcast_fusion.2
  829.7 0.7 copy.29
  830.4 0.0 copy-start.7
  830.4 2.3 reshape.32
  832.7 0.0 copy-done.7
  832.7 1.8 copy_subtract_fusion
  (6 shorter events, 0.0 us)
Async XLA Ops:
  6.5 474.9 %all-reduce.3.cloned.1.call-start = ((), (), s32[]{:S(2)}) async-start(), calls=%async_computation.4 | async-start | bytes 25165824
  6.5 21.6 %collective-permute-start = (bf16[96,64,128]{2,1,0:T(8,128)(2,1)}, bf16[96,64,128]{2,1,0:T(8,128)(2,1)S(1)}, u32[]{:S(2)}, u32[]{:S(2)}) collective-permute-start(bf16[96,64,128]{2,1,0:T(8,128)(2,1)} %param.6), channel_id=1, source_target_pairs={{0,96},{32,0},{64,32},{96,64},{1,97},{33,1},{65,33},{97,65},{2,98}... | collective-permute-start | bytes 4718600 | tf_op jit(solution)/shard_map/ppermute | solution.py:15
  30.5 1.4 copy-start
  30.5 1.4 copy-start.8
  41.8 2.8 copy-start.2
  41.8 3.8 copy-start.3
  58.4 2.9 copy-start.5
  58.5 592.5 %all-gather.5.cloned.1.call-start = ((), (), s32[]{:S(2)}) async-start(), calls=%async_computation.2 | async-start | bytes 8650752 | tf_op jit(solution)/shard_map/all_gather | solution.py:78
  60.6 760.3 %all-gather.7.cloned.1.call-start = ((), (), s32[]{:S(2)}) async-start(), calls=%async_computation.3 | async-start | bytes 8650752 | tf_op jit(solution)/shard_map/all_gather | solution.py:78
  64.0 66.0 %all-to-all-start = ((bf16[2,96,64,128]{3,2,0,1:T(8,128)(2,1)}), bf16[2,96,64,128]{3,2,0,1:T(8,128)(2,1)S(1)}, u32[]{:S(2)}, u32[]{:S(2)}) async-start(bf16[2,96,64,128]{3,2,0,1:T(8,128)(2,1)} %copy.21), calls=%async_computation | async-start | bytes 6291456 | tf_op jit(solution)/shard_map/all_to_all | solution.py:60
  76.6 76.3 %copy-start.9 = (u32[128]{0:T(128)S(1)}, u32[128]{0:T(128)}, u32[]{:S(2)}) copy-start(u32[128]{0:T(128)} %constant.10) | copy-start | bytes 1540
  130.1 1.7 copy-start.1
  131.7 77.9 %all-to-all-start.1 = ((bf16[2,96,64,128]{3,2,0,1:T(8,128)(2,1)}), bf16[2,96,64,128]{3,2,0,1:T(8,128)(2,1)S(1)}, u32[]{:S(2)}, u32[]{:S(2)}) async-start(bf16[2,96,64,128]{3,2,0,1:T(8,128)(2,1)} %copy.25), calls=%async_computation.1 | async-start | bytes 6291456 | tf_op jit(solution)/shard_map/all_to_all | solution.py:59
  209.6 1.4 copy-start.4
  211.2 439.8 %copy-start.6 = (bf16[1,3,32,64,128]{4,3,2,1,0:T(8,128)(2,1)S(1)}, bf16[1,3,32,64,128]{4,3,2,1,0:T(8,128)(2,1)}, u32[]{:S(2)}) copy-start(bf16[1,3,32,64,128]{4,3,2,1,0:T(8,128)(2,1)} %copy.23) | copy-start | bytes 4718596
  830.4 2.3 copy-start.7
Sparse Core Ops, SparseCore 0:
  58.6 422.8 all-reduce.2
  483.1 167.8 all-gather.4
  652.6 168.2 all-gather.6
where the time goes:
time: 842 us; the launch traced here: 841 us
  waiting for transfers between devices  709 us (84%)
  starting transfers between devices  32.9 us (4%)
  local copies, waits for them, and re-layouts  30.4 us (4%)
  other arithmetic  29.7 us (4%)
  between operations  21.6 us (3%)
  matrix products  17.5 us (2%)
    all_gather x2, waiting for transfers between devices, local(): lax.all_gather(screen[offset_index], 'ga', axis=0, tiled=True)  329 us
    unnamed x4, waiting for transfers between devices  268 us
    all_to_all x1, waiting for transfers between devices, local(): lax.all_to_all(dens_vv, 'ga', split_axis=1, concat_axis=2, tiled=True)  53.4 us
    all_to_all x1, waiting for transfers between devices, local(): lax.all_to_all(dens_cc, 'ga', split_axis=1, concat_axis=2, tiled=True)  49.5 us
    all_to_all x1, starting transfers between devices, local(): lax.all_to_all(dens_cc, 'ga', split_axis=1, concat_axis=2, tiled=True)  21.2 us
    dot_general x4, matrix products, pair_products(): jnp.einsum('kgp,kgq->kpq', left_side, right_side, preferred_element_type=...  17.5 us
  transfers between devices with their start and end apart: 6, of which 6 were waited for; matrix products, arithmetic and copies ran while one was open for 4% of the time, Pallas kernels for 0%

commit v1 on v0

v1 whole, which is shorter than its diff:
```python
import functools

import jax
import jax.numpy as jnp
from jax import lax
from jax.experimental import pallas as pl
from jax.experimental.pallas import tpu as pltpu
from jax.sharding import PartitionSpec as P

NV = 8
NC = 8
NKY = 24
KX_DEV = 4
NOFF = 2
AXES = ("ka", "ga")
A_STEPS = (0, 0, -1, -1, 1, 1, 2, 2)
Z_STEPS = (0, 1, 0, 1, 0, 1, 0, 1)


def index_of(x, y, z_hi, z_lo, core):
    return (z_hi * 2 + core) * 32 + (y % 4) * 8 + (z_lo % 2) * 4 + x % 4


def route(move):
    pairs = []
    for source in range(128):
        ka, ga = divmod(source, 32)
        z_hi, core = divmod(ka, 2)
        y, rest = divmod(ga, 8)
        z_lo, x = divmod(rest, 4)
        pairs.append((source, move(x, y, z_hi, z_lo, core)))
    return pairs


def along_first(step):
    return route(
        lambda x, y, h, l, c: index_of(x + step, y, h, l, c) if c == 0 else index_of(x, y + step, h, l, c)
    )


def along_second(step):
    return route(
        lambda x, y, h, l, c: index_of(x, y + step, h, l, c) if c == 0 else index_of(x + step, y, h, l, c)
    )


def along_y(step):
    return route(lambda x, y, h, l, c: index_of(x, y + step, h, l, c))


def along_z():
    return route(lambda x, y, h, l, c: index_of(x, y, h, l + 1, c))


def other_core():
    return route(lambda x, y, h, l, c: index_of(x, y, h, l, 1 - c))


def ka_back():
    return [(i, (i - 32) % 128) for i in range(128)]


def ka_back_j_ahead():
    pairs = []
    for source in range(128):
        ka, ga = divmod(source, 32)
        y, j = divmod(ga, 8)
        pairs.append((source, ((ka - 1) % 4) * 32 + y * 8 + (j + 1) % 8))
    return pairs


def send(array, pairs):
    return lax.ppermute(array, AXES, pairs)


def ring_of_four(held, along):
    half = held.shape[0] // 2
    behind = send(held, along(1))
    ahead = send(held, along(-1))
    far_low = send(behind[:half], along(1))
    far_high = send(ahead[half:], along(-1))
    return behind, ahead, far_low, far_high


def direct_kernel(step, first, pos_ref, rows_ref, valence_ref, conduction_ref, sum_ref, out_ref):
    blocks = rows_ref.shape[0]
    x, y, z_lo, core = pos_ref[0], pos_ref[1], pos_ref[2], pos_ref[3]
    along_a = jnp.where(core == 0, x, y)
    along_b = lax.rem(jnp.where(core == 0, y, x) + (step + 4), 4)
    places = []
    for block in range(first, first + blocks):
        a_now = lax.rem(along_a + (A_STEPS[block] + 4), 4)
        z_now = lax.rem(z_lo + Z_STEPS[block], 2)
        x_now = jnp.where(core == 0, a_now, along_b)
        y_now = jnp.where(core == 0, along_b, a_now)
        places.append(y_now * 8 + z_now * 4 + x_now)
    rows = rows_ref[...].reshape(blocks * rows_ref.shape[1], rows_ref.shape[2])
    image = jnp.dot(rows, valence_ref[...], preferred_element_type=jnp.float32).astype(jnp.bfloat16)
    for k in range(conduction_ref.shape[1]):
        left = jnp.concatenate([conduction_ref[place, k] for place in places], axis=0)
        out_ref[k] = sum_ref[k] + lax.dot_general(
            left,
            image[:, k * 128 : (k + 1) * 128],
            (((0,), (0,)), ((), ())),
            preferred_element_type=jnp.float32,
        )


def add_direct(step, first, pos, rows, valence, conduction, total):
    vmem = pl.BlockSpec(memory_space=pltpu.VMEM)
    count = rows.shape[0] * rows.shape[1]
    return pl.pallas_call(
        functools.partial(direct_kernel, step, first),
        out_shape=jax.ShapeDtypeStruct(total.shape, total.dtype),
        in_specs=[pl.BlockSpec(memory_space=pltpu.SMEM), vmem, vmem, vmem, vmem],
        out_specs=vmem,
        input_output_aliases={4: 0},
        compiler_params=pltpu.CompilerParams(vmem_limit_bytes=40 * 1024 * 1024),
        cost_estimate=pl.CostEstimate(
            flops=2 * count * 2048 * 768 + 2 * count * 128 * 768,
            bytes_accessed=8 * 1024 * 1024,
            transcendentals=0,
        ),
    )(pos, rows, valence, conduction, total)


def parts_of(full):
    half = full.shape[-1] // 2
    real_part = full[..., :half, :half] + full[..., half:, half:]
    imag_part = full[..., :half, half:] - full[..., half:, :half]
    return real_part, imag_part


def exchange_sums(pair_vc, coulomb, offsets, y):
    groups = [[b * 8 + i for i in range(8)] for b in range(4)]
    sent = jnp.transpose(pair_vc.reshape(KX_DEV, 8, 3, 64, 128), (1, 0, 2, 3, 4))
    here = lax.all_to_all(
        sent, "ga", split_axis=0, concat_axis=0, tiled=True, axis_index_groups=groups
    )
    all_coulomb = lax.all_gather(coulomb, "ga", axis=0, tiled=True)
    near_coulomb = lax.dynamic_slice_in_dim(all_coulomb, y * 512, 512, 0)
    ahead = send(here, ka_back())
    before = send(here[:, :, 2:], ka_back_j_ahead())
    scaled = (near_coulomb.reshape(8, 1, 1, 64, 1) * here.astype(jnp.float32)).astype(jnp.bfloat16)
    special = jnp.where(offsets[0, 1] == NKY - 1, 0, 1)
    plain_x = offsets[1 - special, 0]
    shifted = jnp.concatenate([before, ahead[:, :, :2]], axis=2)
    joined = jnp.concatenate([here, ahead], axis=1)
    plain = lax.dynamic_slice_in_dim(joined, plain_x, KX_DEV, 1)

    def products(right):
        full = jnp.einsum("sabgp,sabgq->abpq", scaled, right, preferred_element_type=jnp.float32)
        return jnp.stack(parts_of(full), axis=1)

    of_special = products(shifted)
    of_plain = products(plain)
    terms = jnp.stack(
        [jnp.where(special == 0, of_special, of_plain), jnp.where(special == 0, of_plain, of_special)],
        axis=1,
    )
    total = lax.dynamic_index_in_dim(terms, y, 0, keepdims=False)
    for step in (1, 2, 3):
        piece = lax.dynamic_index_in_dim(terms, lax.rem(y + step, 4), 0, keepdims=False)
        total = total + send(piece, along_y(step))
    return total


def own_offset(dens, core):
    mine = lax.dynamic_index_in_dim(dens, core, 0, keepdims=False)
    theirs = lax.dynamic_index_in_dim(dens, 1 - core, 0, keepdims=False)
    got = send(theirs, other_core())
    packed = jnp.concatenate([mine.reshape(32, 3, 64, 128), got.reshape(32, 3, 64, 128)], axis=1)
    return lax.all_to_all(packed, "ga", split_axis=0, concat_axis=0, tiled=True)


def local(pair_vc, coulomb, dens_cc, dens_vv, screen, offsets):
    ka = lax.axis_index("ka")
    ga = lax.axis_index("ga")
    core = lax.rem(ka, 2)
    y, z_lo, x = ga // 8, lax.rem(ga // 4, 2), lax.rem(ga, 4)
    pos = jnp.stack([x, y, z_lo, core]).astype(jnp.int32)

    rows = lax.dynamic_index_in_dim(screen, core, 0, keepdims=True)
    rows = jnp.concatenate([rows, send(rows, along_z())], axis=0)
    rows = jnp.concatenate([rows, *ring_of_four(rows, along_first)], axis=0)
    behind, ahead, far_low, far_high = ring_of_four(rows, along_second)

    valence = own_offset(dens_vv, core)
    conduction = own_offset(dens_cc, core)
    exch = exchange_sums(pair_vc, coulomb, offsets, y)

    valence = jnp.transpose(valence, (0, 2, 1, 3)).reshape(2048, 768)
    total = jnp.zeros((6, 128, 128), jnp.float32)
    total = add_direct(0, 0, pos, rows, valence, conduction, total)
    total = add_direct(-1, 0, pos, behind, valence, conduction, total)
    total = add_direct(1, 0, pos, ahead, valence, conduction, total)
    total = add_direct(2, 0, pos, far_low, valence, conduction, total)
    total = add_direct(2, 4, pos, far_high, valence, conduction, total)

    direct = jnp.stack(parts_of(total))
    mine = direct[:, :3]
    theirs = send(direct[:, 3:], other_core())
    direct = jnp.stack(
        [jnp.where(core == 0, mine, theirs), jnp.where(core == 0, theirs, mine)]
    )
    shaped = direct.reshape(NOFF, 2, 3, NC, NC, NV, NV)
    shaped = jnp.transpose(shaped, (0, 1, 2, 5, 3, 6, 4)).reshape(NOFF, 2, 3, 4096)
    return 2.0 * exch.reshape(NOFF, 2, 3, 4096) - shaped


def solution(mesh):
    placed = (
        P("ka", "ga", None),
        P("ga"),
        P(None, "ka", "ga", None),
        P(None, "ka", "ga", None),
        P(None, "ga", None),
        P(),
    )
    return jax.shard_map(
        local,
        mesh=mesh,
        in_specs=placed,
        out_specs=P(None, None, ("ka", "ga"), None),
        check_vma=False,
    )
```

time: 842 us -> 308 us (0.37)
  the two profiles are of different devices: /device:TPU:2 before, /device:TPU:65 now
where the time goes in v1:
time: 308 us; the launch traced here: 307 us
  blocking collectives  124 us (40%)
  waiting for transfers between devices  60.2 us (20%)
  local copies, waits for them, and re-layouts  45.6 us (15%)
  starting transfers between devices  38.4 us (12%)
  Pallas kernels  16.5 us (5%)
  other arithmetic  14.1 us (5%)
  matrix products  4.21 us (1%)
  between operations  3.86 us (1%)
    unnamed x1, blocking collectives  124 us
    ppermute x17, waiting for transfers between devices, send(): return lax.ppermute(array, AXES, pairs)  42 us
    ppermute x17, starting transfers between devices, send(): return lax.ppermute(array, AXES, pairs)  21.5 us
    all_to_all x1, waiting for transfers between devices, exchange_sums(): lax.all_to_all(sent, 'ga', split_axis=0, concat_axis=0, tiled=True, axis_...  18.1 us
    pallas_call x5, Pallas kernels, add_direct(): pl.pallas_call(functools.partial(direct_kernel, step, first), out_shape=j...  16.5 us
    all_to_all x2, starting transfers between devices, own_offset(): return lax.all_to_all(packed, 'ga', split_axis=0, concat_axis=0, tiled=True)  11.9 us
    unnamed x33, local copies, waits for them, and re-layouts  10.2 us
    dynamic_slice x2, local copies, waits for them, and re-layouts, own_offset(): mine = lax.dynamic_index_in_dim(dens, core, 0, keepdims=False)  6.46 us
  transfers between devices with their start and end apart: 20, of which 3 were waited for; matrix products, arithmetic and copies ran while one was open for 15% of the time, Pallas kernels for 5%

profile of v1, /device:TPU:65, one launch (start us, length us, event | category | flops | bytes accessed | tf_op | source)
XLA Modules:
  0.0 306.9 jit_solution(10619700042447520286)
XLA Ops:
  0.0 3.8 %constant_dynamic-slice_fusion.1 = (bf16[1,96,64,128]{3,2,1,0:T(8,128)(2,1)S(1)}, bf16[96,64,128]{2,1,0:T(8,128)(2,1)}) fusion(bf16[2,96,64,128]{3,2,1,0:T(8,128)(2,1)} %param.9, s32[]{:T(128)S(6)} %select_n.98, s32[]{:T(128)S(6)} %select_n.99), kind=kLoop, calls=%fused_computation.70 | loop fusion | bytes 6291464 | tf_op jit(solution)/shard_map/jit(dynamic_index_in_dim)/dynamic_slice | solution.py:169
  3.8 0.7 collective-permute-start.12
  4.5 1.3 copy.22
  5.8 5.1 %all-to-all-start = ((bf16[8,4,3,64,128]{4,3,2,1,0:T(8,128)(2,1)}), bf16[8,4,3,64,128]{4,3,2,1,0:T(8,128)(2,1)S(1)}, u32[]{:S(2)}, u32[]{:S(2)}) async-start(bf16[8,4,3,64,128]{4,3,2,1,0:T(8,128)(2,1)} %copy.22), calls=%async_computation | async-start | bytes 3145728 | tf_op jit(solution)/shard_map/all_to_all | solution.py:137
  10.9 3.4 %pad_maximum_fusion = bf16[32,6,64,128]{3,2,1,0:T(8,128)(2,1)} fusion(bf16[32,3,64,128]{3,2,1,0:T(8,128)(2,1)} %bitcast.23, bf16[32,3,64,128]{3,2,1,0:T(8,128)(2,1)S(1)} %bitcast.81), kind=kLoop, calls=%fused_computation.3 | loop fusion | flops 1572864 | bytes 6291456 | tf_op jit(solution)/shard_map/concatenate | solution.py:172
  14.3 18.1 %all-to-all-done = bf16[8,4,3,64,128]{4,3,2,1,0:T(8,128)(2,1)S(1)} async-done(((bf16[8,4,3,64,128]{4,3,2,1,0:T(8,128)(2,1)}), bf16[8,4,3,64,128]{4,3,2,1,0:T(8,128)(2,1)S(1)}, u32[]{:S(2)}, u32[]{:S(2)}) %all-to-all-start) | async-done | bytes 1572896 | tf_op jit(solution)/shard_map/all_to_all | solution.py:137
  32.4 7.8 %all-to-all-start.1 = ((bf16[32,6,64,128]{3,2,1,0:T(8,128)(2,1)}), bf16[32,6,64,128]{3,2,1,0:T(8,128)(2,1)}, u32[]{:S(2)}, u32[]{:S(2)}) async-start(bf16[32,6,64,128]{3,2,1,0:T(8,128)(2,1)} %pad_maximum_fusion), calls=%async_computation.1 | async-start | bytes 6291456 | tf_op jit(solution)/shard_map/all_to_all | solution.py:173
  40.2 2.6 constant_dynamic-slice_fusion
  42.9 1.5 collective-permute-start.13
  44.4 0.7 constant_dynamic-update-slice_fusion.5
  45.1 1.4 collective-permute-start.5
  46.6 35.8 %collective-permute-done.5 = bf16[1,64,2048]{2,1,0:T(8,128)(2,1)S(1)} collective-permute-done((bf16[1,64,2048]{2,1,0:T(8,128)(2,1)S(1)}, bf16[1,64,2048]{2,1,0:T(8,128)(2,1)S(1)}, u32[]{:S(2)}, u32[]{:S(2)}) %collective-permute-start.5) | collective-permute-done | bytes 262176 | tf_op jit(solution)/shard_map/ppermute | solution.py:73
  82.6 2.7 collective-permute-start.7
  85.2 0.7 constant_dynamic-update-slice_fusion.4
  86.0 6.1 %collective-permute-done.6 = bf16[2,64,2048]{2,1,0:T(8,128)(2,1)S(1)} collective-permute-done((bf16[2,64,2048]{2,1,0:T(8,128)(2,1)S(1)}, bf16[2,64,2048]{2,1,0:T(8,128)(2,1)S(1)}, u32[]{:S(2)}, u32[]{:S(2)}) %collective-permute-start.6) | collective-permute-done | bytes 524320 | tf_op jit(solution)/shard_map/ppermute | solution.py:73
  92.1 0.7 slice.94
  92.8 0.7 slice.95
  93.6 2.7 collective-permute-start.9
  96.2 0.8 constant_dynamic-update-slice_fusion.3
  97.1 0.8 constant_dynamic-update-slice_fusion.2
  97.9 1.3 copy.23
  99.2 2.3 collective-permute-start.1
  101.5 2.0 pad_maximum_fusion.1
  103.5 4.1 %all-to-all-start.2 = ((bf16[32,6,64,128]{3,2,1,0:T(8,128)(2,1)}), bf16[32,6,64,128]{3,2,1,0:T(8,128)(2,1)S(1)}, u32[]{:S(2)}, u32[]{:S(2)}) async-start(bf16[32,6,64,128]{3,2,1,0:T(8,128)(2,1)} %pad_maximum_fusion.1), calls=%async_computation.2 | async-start | bytes 6291456 | tf_op jit(solution)/shard_map/all_to_all | solution.py:173
  107.6 0.7 constant_dynamic-update-slice_fusion.1
  108.3 1.7 constant_dynamic-update-slice_fusion.rows_ref
  110.0 1.1 collective-permute-start.14
  111.1 1.6 collective-permute-start.10
  112.7 1.9 slice.84
  114.5 1.8 collective-permute-start
  116.4 0.6 slice.63
  117.7 0.6 dynamic-slice
  119.1 0.3 dynamic-update-slice
  119.4 124.1 %all-reduce = f32[2048]{0:T(1024)S(1)} all-reduce(f32[2048]{0:T(1024)S(1)} %dynamic-update-slice), channel_id=1, replica_groups=mesh['ka'=4,'ga'=32] {'ga'}, use_global_device_ids=true, to_apply=%add | all-reduce | flops 2048 | bytes 16384
  243.6 0.6 constant_dynamic-slice_fusion.3
  246.3 2.0 multiply_convert_fusion
  248.3 1.4 slice.85
  249.7 0.3 copy-done.2
  250.0 1.9 fusion.3
  252.0 2.3 fusion.1
  254.4 2.3 slice.97
  256.7 0.3 collective-permute-start.15
  257.0 2.3 slice.96
  259.3 2.3 collective-permute-start.11
  261.7 0.5 fusion.22
  262.4 1.1 fusion.18
  263.6 2.7 collective-permute-start.4
  266.2 4.8 %copy.29 = bf16[32,64,6,128]{3,2,1,0:T(8,128)(2,1)S(1)} copy(bf16[32,64,6,128]{3,1,2,0:T(8,128)(2,1)} %bitcast.24) | data formatting | bytes 6291456 | tf_op jit(solution)/shard_map/transpose | solution.py:192
  271.0 2.4 copy.57
  273.5 1.9 copy-done
  275.4 3.8 %shard_map.64.sum_ref = f32[6,128,128]{2,1,0:T(8,128)S(1)} custom-call(s32[4]{0:T(128)S(1)} %pad_add_fusion.pos_ref, bf16[8,64,2048]{2,1,0:T(8,128)(2,1)} %constant_dynamic-update-slice_fusion.rows_ref, bf16[2048,768]{1,0:T(8,128)(2,1)S(1)} %bitcast.72, bf16[32,6,64,128]{3,2,1,0:T(8,128)(2,1)S(1)} %all-to-all-done.2.conduction_ref, ...), custom_call_target="tpu_custom_call", output_to_operand_aliasing={{}: (4, {})} | custom-call | flops 1711276032 | bytes 8388608 | tf_op jit(solution)/shard_map/pallas_call | solution.py:112
  279.2 3.8 %shard_map.65.sum_ref = f32[6,128,128]{2,1,0:T(8,128)S(1)} custom-call(s32[4]{0:T(128)S(1)} %pad_add_fusion.pos_ref, bf16[8,64,2048]{2,1,0:T(8,128)(2,1)} %collective-permute-done.14.rows_ref, bf16[2048,768]{1,0:T(8,128)(2,1)S(1)} %bitcast.73, bf16[32,6,64,128]{3,2,1,0:T(8,128)(2,1)S(1)} %all-to-all-done.2.conduction_ref, ...), custom_call_target="tpu_custom_call", output_to_operand_aliasing={{}: (4, {})} | custom-call | flops 1711276032 | bytes 8388608 | tf_op jit(solution)/shard_map/pallas_call | solution.py:112
  283.0 3.8 %shard_map.66.sum_ref = f32[6,128,128]{2,1,0:T(8,128)S(1)} custom-call(s32[4]{0:T(128)S(1)} %pad_add_fusion.pos_ref, bf16[8,64,2048]{2,1,0:T(8,128)(2,1)} %collective-permute-done.10.rows_ref, bf16[2048,768]{1,0:T(8,128)(2,1)S(1)} %bitcast.74, bf16[32,6,64,128]{3,2,1,0:T(8,128)(2,1)S(1)} %all-to-all-done.2.conduction_ref, ...), custom_call_target="tpu_custom_call", output_to_operand_aliasing={{}: (4, {})} | custom-call | flops 1711276032 | bytes 8388608 | tf_op jit(solution)/shard_map/pallas_call | solution.py:112
  286.9 2.5 shard_map.67.sum_ref
  289.4 2.5 shard_map.68
  292.1 0.3 collective-permute-start.16
  292.5 0.6 copy-done.4
  293.3 1.2 fusion.16
  294.8 1.6 stack.71
  296.4 1.6 stack.72
  298.0 2.4 maximum_bitcast_fusion
  300.4 2.3 copy.30
  302.8 3.3 %reshape.168 = f32[2,2,3,4096]{3,1,2,0:T(2,128)S(1)} reshape(f32[2,2,3,8,8,8,8]{6,5,4,3,1,2,0:T(8,128)} %copy.30) | data formatting | bytes 393216 | tf_op jit(solution)/shard_map/reshape | solution.py:207
  306.1 0.9 copy_subtract_fusion
  (55 shorter events, 1.5 us)
Async XLA Ops:
  0.0 4.5 %copy-start.7 = (bf16[96,64,128]{2,1,0:T(8,128)(2,1)S(1)}, bf16[96,64,128]{2,1,0:T(8,128)(2,1)}, u32[]{:S(2)}) copy-start(bf16[96,64,128]{2,1,0:T(8,128)(2,1)} %param.6) | copy-start | bytes 4718596
  3.8 7.1 %collective-permute-start.12 = (bf16[96,64,128]{2,1,0:T(8,128)(2,1)}, bf16[96,64,128]{2,1,0:T(8,128)(2,1)}, u32[]{:S(2)}, u32[]{:S(2)}) collective-permute-start(bf16[96,64,128]{2,1,0:T(8,128)(2,1)} %get-tuple-element.10), channel_id=1, source_target_pairs={{0,32},{1,33},{2,34},{3,35},{4,36},{5,37},{6,38},{7,39},{8,40},{9,... | collective-permute-start | bytes 4718600 | tf_op jit(solution)/shard_map/ppermute | solution.py:73
  5.8 26.6 %all-to-all-start = ((bf16[8,4,3,64,128]{4,3,2,1,0:T(8,128)(2,1)}), bf16[8,4,3,64,128]{4,3,2,1,0:T(8,128)(2,1)S(1)}, u32[]{:S(2)}, u32[]{:S(2)}) async-start(bf16[8,4,3,64,128]{4,3,2,1,0:T(8,128)(2,1)} %copy.22), calls=%async_computation | async-start | bytes 3145728 | tf_op jit(solution)/shard_map/all_to_all | solution.py:137
  32.4 65.5 %copy-start.1 = (bf16[8,4,3,64,128]{4,3,2,1,0:T(8,128)(2,1)}, bf16[8,4,3,64,128]{4,3,2,1,0:T(8,128)(2,1)S(1)}, u32[]{:S(2)}) copy-start(bf16[8,4,3,64,128]{4,3,2,1,0:T(8,128)(2,1)S(1)} %all-to-all-done) | copy-start | bytes 4718596
  32.4 71.0 %all-to-all-start.1 = ((bf16[32,6,64,128]{3,2,1,0:T(8,128)(2,1)}), bf16[32,6,64,128]{3,2,1,0:T(8,128)(2,1)}, u32[]{:S(2)}, u32[]{:S(2)}) async-start(bf16[32,6,64,128]{3,2,1,0:T(8,128)(2,1)} %pad_maximum_fusion), calls=%async_computation.1 | async-start | bytes 6291456 | tf_op jit(solution)/shard_map/all_to_all | solution.py:173
  40.2 4.2 %copy-start.8 = (bf16[2,64,2048]{2,1,0:T(8,128)(2,1)S(1)}, bf16[2,64,2048]{2,1,0:T(8,128)(2,1)}, u32[]{:S(2)}) copy-start(bf16[2,64,2048]{2,1,0:T(8,128)(2,1)} %param.10) | copy-start | bytes 1572868
  42.9 58.6 %collective-permute-start.13 = (bf16[96,64,128]{2,1,0:T(8,128)(2,1)S(1)}, bf16[96,64,128]{2,1,0:T(8,128)(2,1)S(1)}, u32[]{:S(2)}, u32[]{:S(2)}) collective-permute-start(bf16[96,64,128]{2,1,0:T(8,128)(2,1)S(1)} %get-tuple-element.8), channel_id=1, source_target_pairs={{0,32},{1,33},{2,34},{3,35},{4,36},{5,37},{6,38},{7,39},{8,40},{9,... | collective-permute-start | bytes 4718600 | tf_op jit(solution)/shard_map/ppermute | solution.py:73
  45.1 37.3 %collective-permute-start.5 = (bf16[1,64,2048]{2,1,0:T(8,128)(2,1)S(1)}, bf16[1,64,2048]{2,1,0:T(8,128)(2,1)S(1)}, u32[]{:S(2)}, u32[]{:S(2)}) collective-permute-start(bf16[1,64,2048]{2,1,0:T(8,128)(2,1)S(1)} %get-tuple-element.6), channel_id=1, source_target_pairs={{0,4},{1,5},{2,6},{3,7},{4,0},{5,1},{6,2},{7,3},{8,12},{9,13},{10,... | collective-permute-start | bytes 786440 | tf_op jit(solution)/shard_map/ppermute | solution.py:73
  82.5 9.6 %collective-permute-start.6 = (bf16[2,64,2048]{2,1,0:T(8,128)(2,1)S(1)}, bf16[2,64,2048]{2,1,0:T(8,128)(2,1)S(1)}, u32[]{:S(2)}, u32[]{:S(2)}) collective-permute-start(bf16[2,64,2048]{2,1,0:T(8,128)(2,1)S(1)} %pad_maximum_fusion.5), channel_id=1, source_target_pairs={{0,1},{1,2},{2,3},{3,0},{4,5},{5,6},{6,7},{7,4},{8,9},{9,10},{10,1... | collective-permute-start | bytes 1572872 | tf_op jit(solution)/shard_map/ppermute | solution.py:73
  82.6 10.3 %collective-permute-start.7 = (bf16[2,64,2048]{2,1,0:T(8,128)(2,1)S(1)}, bf16[2,64,2048]{2,1,0:T(8,128)(2,1)S(1)}, u32[]{:S(2)}, u32[]{:S(2)}) collective-permute-start(bf16[2,64,2048]{2,1,0:T(8,128)(2,1)S(1)} %pad_maximum_fusion.5), channel_id=1, source_target_pairs={{0,3},{1,0},{2,1},{3,2},{4,7},{5,4},{6,5},{7,6},{8,11},{9,8},{10,9... | collective-permute-start | bytes 1572872 | tf_op jit(solution)/shard_map/ppermute | solution.py:73
  92.8 14.8 %collective-permute-start.8 = (bf16[1,64,2048]{2,1,0:T(8,128)(2,1)}, bf16[1,64,2048]{2,1,0:T(8,128)(2,1)S(1)}, u32[]{:S(2)}, u32[]{:S(2)}) collective-permute-start(bf16[1,64,2048]{2,1,0:T(8,128)(2,1)} %slice.94), channel_id=1, source_target_pairs={{0,1},{1,2},{2,3},{3,0},{4,5},{5,6},{6,7},{7,4},{8,9},{9,10},{10,1... | collective-permute-start | bytes 786440 | tf_op jit(solution)/shard_map/ppermute | solution.py:73
  93.6 14.8 %collective-permute-start.9 = (bf16[1,64,2048]{2,1,0:T(8,128)(2,1)}, bf16[1,64,2048]{2,1,0:T(8,128)(2,1)}, u32[]{:S(2)}, u32[]{:S(2)}) collective-permute-start(bf16[1,64,2048]{2,1,0:T(8,128)(2,1)} %slice.95), channel_id=1, source_target_pairs={{0,3},{1,0},{2,1},{3,2},{4,7},{5,4},{6,5},{7,6},{8,11},{9,8},{10,9... | collective-permute-start | bytes 786440 | tf_op jit(solution)/shard_map/ppermute | solution.py:73
  99.2 149.1 %collective-permute-start.1 = (bf16[8,4,3,64,128]{4,3,0,2,1:T(8,128)(2,1)}, bf16[8,4,3,64,128]{4,3,0,2,1:T(8,128)(2,1)}, u32[]{:S(2)}, u32[]{:S(2)}) collective-permute-start(bf16[8,4,3,64,128]{4,3,0,2,1:T(8,128)(2,1)} %copy.23), channel_id=1, source_target_pairs={{0,96},{1,97},{2,98},{3,99},{4,100},{5,101},{6,102},{7,103},{8,104... | collective-permute-start | bytes 4718600 | tf_op jit(solution)/shard_map/ppermute | solution.py:73
  103.5 170.0 %all-to-all-start.2 = ((bf16[32,6,64,128]{3,2,1,0:T(8,128)(2,1)}), bf16[32,6,64,128]{3,2,1,0:T(8,128)(2,1)S(1)}, u32[]{:S(2)}, u32[]{:S(2)}) async-start(bf16[32,6,64,128]{3,2,1,0:T(8,128)(2,1)} %pad_maximum_fusion.1), calls=%async_computation.2 | async-start | bytes 6291456 | tf_op jit(solution)/shard_map/all_to_all | solution.py:173
  107.5 8.9 %copy-start.9 = (s32[2,2]{1,0:T(2,128)S(1)}, s32[2,2]{1,0:T(2,128)}, u32[]{:S(2)}) copy-start(s32[2,2]{1,0:T(2,128)} %param.11) | copy-start | bytes 52
  107.6 10.2 %copy-start.11 = (u32[128]{0:T(128)S(1)}, u32[128]{0:T(128)}, u32[]{:S(2)}) copy-start(u32[128]{0:T(128)} %constant.98) | copy-start | bytes 1540
  107.6 11.5 %copy-start.10 = (f32[64]{0:T(128)S(1)}, f32[64]{0:T(128)}, u32[]{:S(2)}) copy-start(f32[64]{0:T(128)} %param.7) | copy-start | bytes 772
  110.0 144.3 %collective-permute-start.14 = (bf16[8,64,2048]{2,1,0:T(8,128)(2,1)}, bf16[8,64,2048]{2,1,0:T(8,128)(2,1)}, u32[]{:S(2)}, u32[]{:S(2)}) collective-permute-start(bf16[8,64,2048]{2,1,0:T(8,128)(2,1)} %constant_dynamic-update-slice_fusion.rows_ref), channel_id=1, source_target_pairs={{0,8},{1,9},{2,10},{3,11},{4,12},{5,13},{6,14},{7,15},{8,16},{9,17... | collective-permute-start | bytes 6291464 | tf_op jit(solution)/shard_map/ppermute | solution.py:73
  111.1 145.9 %collective-permute-start.10 = (bf16[8,64,2048]{2,1,0:T(8,128)(2,1)}, bf16[8,64,2048]{2,1,0:T(8,128)(2,1)}, u32[]{:S(2)}, u32[]{:S(2)}) collective-permute-start(bf16[8,64,2048]{2,1,0:T(8,128)(2,1)} %constant_dynamic-update-slice_fusion.rows_ref), channel_id=1, source_target_pairs={{0,24},{1,25},{2,26},{3,27},{4,28},{5,29},{6,30},{7,31},{8,0},{9,1... | collective-permute-start | bytes 6291464 | tf_op jit(solution)/shard_map/ppermute | solution.py:73
  114.5 135.2 %collective-permute-start = (bf16[8,4,1,64,128]{4,3,0,2,1:T(8,128)(2,1)}, bf16[8,4,1,64,128]{4,3,0,2,1:T(8,128)(2,1)}, u32[]{:S(2)}, u32[]{:S(2)}) collective-permute-start(bf16[8,4,1,64,128]{4,3,0,2,1:T(8,128)(2,1)} %slice.84), channel_id=1, source_target_pairs={{0,97},{1,98},{2,99},{3,100},{4,101},{5,102},{6,103},{7,96},{8,105... | collective-permute-start | bytes 1572872 | tf_op jit(solution)/shard_map/ppermute | solution.py:73
  248.3 1.7 copy-start.2
  256.7 30.2 %collective-permute-start.15 = (bf16[4,64,2048]{2,1,0:T(8,128)(2,1)}, bf16[4,64,2048]{2,1,0:T(8,128)(2,1)}, u32[]{:S(2)}, u32[]{:S(2)}) collective-permute-start(bf16[4,64,2048]{2,1,0:T(8,128)(2,1)} %slice.97), channel_id=1, source_target_pairs={{0,8},{1,9},{2,10},{3,11},{4,12},{5,13},{6,14},{7,15},{8,16},{9,17... | collective-permute-start | bytes 3145736 | tf_op jit(solution)/shard_map/ppermute | solution.py:73
  259.3 30.1 %collective-permute-start.11 = (bf16[4,64,2048]{2,1,0:T(8,128)(2,1)}, bf16[4,64,2048]{2,1,0:T(8,128)(2,1)}, u32[]{:S(2)}, u32[]{:S(2)}) collective-permute-start(bf16[4,64,2048]{2,1,0:T(8,128)(2,1)} %slice.96), channel_id=1, source_target_pairs={{0,24},{1,25},{2,26},{3,27},{4,28},{5,29},{6,30},{7,31},{8,0},{9,1... | collective-permute-start | bytes 3145736 | tf_op jit(solution)/shard_map/ppermute | solution.py:73
  262.4 3.8 %copy-start.3 = (f32[4,1,2,3,64,64]{5,4,3,0,2,1:T(8,128)}, f32[4,1,2,3,64,64]{5,4,3,0,2,1:T(8,128)S(1)}, u32[]{:S(2)}) copy-start(f32[4,1,2,3,64,64]{5,4,3,0,2,1:T(8,128)S(1)} %get-tuple-element.14) | copy-start | bytes 1179652
  262.4 3.8 %copy-start.5 = (f32[4,1,2,3,64,64]{5,4,3,0,2,1:T(8,128)}, f32[4,1,2,3,64,64]{5,4,3,0,2,1:T(8,128)S(1)}, u32[]{:S(2)}) copy-start(f32[4,1,2,3,64,64]{5,4,3,0,2,1:T(8,128)S(1)} %get-tuple-element.15) | copy-start | bytes 1179652
  263.5 28.9 %collective-permute-start.2 = (f32[2,2,3,64,64]{4,3,2,1,0:T(8,128)}, f32[2,2,3,64,64]{4,3,2,1,0:T(8,128)S(1)}, u32[]{:S(2)}, u32[]{:S(2)}) collective-permute-start(f32[2,2,3,64,64]{4,3,2,1,0:T(8,128)} %get-tuple-element.11), channel_id=1, source_target_pairs={{0,8},{1,9},{2,10},{3,11},{4,12},{5,13},{6,14},{7,15},{8,16},{9,17... | collective-permute-start | bytes 589832 | tf_op jit(solution)/shard_map/ppermute | solution.py:73
  263.5 28.9 %collective-permute-start.3 = (f32[2,2,3,64,64]{4,3,2,1,0:T(8,128)}, f32[2,2,3,64,64]{4,3,2,1,0:T(8,128)}, u32[]{:S(2)}, u32[]{:S(2)}) collective-permute-start(f32[2,2,3,64,64]{4,3,2,1,0:T(8,128)} %get-tuple-element.12), channel_id=1, source_target_pairs={{0,16},{1,17},{2,18},{3,19},{4,20},{5,21},{6,22},{7,23},{8,24},{9,... | collective-permute-start | bytes 589832 | tf_op jit(solution)/shard_map/ppermute | solution.py:73
  263.6 28.9 %collective-permute-start.4 = (f32[2,2,3,64,64]{4,3,2,1,0:T(8,128)}, f32[2,2,3,64,64]{4,3,2,1,0:T(8,128)}, u32[]{:S(2)}, u32[]{:S(2)}) collective-permute-start(f32[2,2,3,64,64]{4,3,2,1,0:T(8,128)} %get-tuple-element.13), channel_id=1, source_target_pairs={{0,24},{1,25},{2,26},{3,27},{4,28},{5,29},{6,30},{7,31},{8,0},{9,1... | collective-permute-start | bytes 589832 | tf_op jit(solution)/shard_map/ppermute | solution.py:73
  273.5 1.9 copy-start
  291.9 1.1 copy-start.4
  291.9 1.4 copy-start.6
  292.1 2.6 collective-permute-start.16

commit v2 on v1

v2 whole, which is shorter than its diff:
```python
import functools

import jax
import jax.numpy as jnp
from jax import lax
from jax.experimental import pallas as pl
from jax.experimental.pallas import tpu as pltpu
from jax.sharding import PartitionSpec as P

NV = 8
NC = 8
NKY = 24
KX_DEV = 4
NOFF = 2
AXES = ("ka", "ga")
A_STEPS = (0, 0, -1, -1, 1, 1, 2, 2)
Z_STEPS = (0, 1, 0, 1, 0, 1, 0, 1)


def index_of(x, y, z_hi, z_lo, core):
    return (z_hi * 2 + core) * 32 + (y % 4) * 8 + (z_lo % 2) * 4 + x % 4


def route(move):
    pairs = []
    for source in range(128):
        ka, ga = divmod(source, 32)
        z_hi, core = divmod(ka, 2)
        y, rest = divmod(ga, 8)
        z_lo, x = divmod(rest, 4)
        pairs.append((source, move(x, y, z_hi, z_lo, core)))
    return pairs


def along_first(step):
    return route(
        lambda x, y, h, l, c: index_of(x + step, y, h, l, c) if c == 0 else index_of(x, y + step, h, l, c)
    )


def along_second(step):
    return route(
        lambda x, y, h, l, c: index_of(x, y + step, h, l, c) if c == 0 else index_of(x + step, y, h, l, c)
    )


def along_y(step):
    return route(lambda x, y, h, l, c: index_of(x, y + step, h, l, c))


def along_z():
    return route(lambda x, y, h, l, c: index_of(x, y, h, l + 1, c))


def other_core():
    return route(lambda x, y, h, l, c: index_of(x, y, h, l, 1 - c))


def ka_back():
    return [(i, (i - 32) % 128) for i in range(128)]


def ka_back_j_ahead():
    pairs = []
    for source in range(128):
        ka, ga = divmod(source, 32)
        y, j = divmod(ga, 8)
        pairs.append((source, ((ka - 1) % 4) * 32 + y * 8 + (j + 1) % 8))
    return pairs


def send(array, pairs):
    return lax.ppermute(array, AXES, pairs)


def ring_of_four(held, along):
    half = held.shape[0] // 2
    behind = send(held, along(1))
    ahead = send(held, along(-1))
    far_low = send(behind[:half], along(1))
    far_high = send(ahead[half:], along(-1))
    return behind, ahead, far_low, far_high


def image_kernel(rows_ref, valence_ref, out_ref):
    blocks, depth, width = rows_ref.shape
    rows = rows_ref[...].reshape(blocks * depth, width)
    out_ref[...] = jnp.dot(
        rows, valence_ref[...], preferred_element_type=jnp.float32
    ).astype(jnp.bfloat16)


def image_of(rows, valence):
    vmem = pl.BlockSpec(memory_space=pltpu.VMEM)
    count = rows.shape[0] * rows.shape[1]
    return pl.pallas_call(
        image_kernel,
        out_shape=jax.ShapeDtypeStruct((count, valence.shape[1]), jnp.bfloat16),
        in_specs=[vmem, vmem],
        out_specs=vmem,
        compiler_params=pltpu.CompilerParams(vmem_limit_bytes=40 * 1024 * 1024),
        cost_estimate=pl.CostEstimate(
            flops=2 * count * valence.shape[0] * valence.shape[1],
            bytes_accessed=2 * (count * 2048 + valence.size + count * valence.shape[1]),
            transcendentals=0,
        ),
    )(rows, valence)


def direct_kernel(from_k, pos_ref, own_ref, behind_ref, ahead_ref, low_ref, high_ref, conduction_ref, out_ref):
    x, y, z_lo, core = pos_ref[0], pos_ref[1], pos_ref[2], pos_ref[3]
    along_a = jnp.where(core == 0, x, y)
    along_b = jnp.where(core == 0, y, x)
    places = []
    for step, blocks in ((0, range(8)), (3, range(8)), (1, range(8)), (2, range(8))):
        b_now = lax.rem(along_b + step, 4)
        for block in blocks:
            a_now = lax.rem(along_a + (A_STEPS[block] + 4), 4)
            z_now = lax.rem(z_lo + Z_STEPS[block], 2)
            x_now = jnp.where(core == 0, a_now, b_now)
            y_now = jnp.where(core == 0, b_now, a_now)
            places.append(y_now * 8 + z_now * 4 + x_now)
    lane = lax.broadcasted_iota(jnp.int32, (64, 128), 1)
    for k in range(out_ref.shape[0]):
        columns = pl.ds((from_k + k) * 128, 128)
        full = jnp.zeros((128, 128), jnp.float32)
        first = 0
        for part in (own_ref, behind_ref, ahead_ref, low_ref, high_ref):
            blocks = part.shape[0] // 64
            right = jnp.concatenate(
                [conduction_ref[place, from_k + k] for place in places[first : first + blocks]], axis=0
            )
            first += blocks
            full += lax.dot_general(
                part[:, columns], right, (((0,), (0,)), ((), ())), preferred_element_type=jnp.float32
            )
        turned = pltpu.roll(full[64:], 64, 1)
        out_ref[k] = jnp.where(lane < 64, turned + full[:64], turned - full[:64])


def direct_of(from_k, pos, images, conduction):
    vmem = pl.BlockSpec(memory_space=pltpu.VMEM)
    return pl.pallas_call(
        functools.partial(direct_kernel, from_k),
        out_shape=jax.ShapeDtypeStruct((3, 64, 128), jnp.float32),
        in_specs=[pl.BlockSpec(memory_space=pltpu.SMEM)] + [vmem] * 6,
        out_specs=vmem,
        compiler_params=pltpu.CompilerParams(vmem_limit_bytes=40 * 1024 * 1024),
        cost_estimate=pl.CostEstimate(
            flops=2 * 3 * 2048 * 128 * 128, bytes_accessed=6 * 1024 * 1024, transcendentals=0
        ),
    )(pos, *images, conduction)


def final_kernel(pos_ref, exch_ref, mine_ref, theirs_ref, out_ref, turned_ref):
    core = pos_ref[3]
    lane = lax.broadcasted_iota(jnp.int32, (64, 128), 1)
    row = lax.broadcasted_iota(jnp.int32, (64, 128), 0)
    low_lane = lax.broadcasted_iota(jnp.int32, (32, 128), 1) < 64
    for k in range(3):
        for offset, block in ((core, mine_ref[k]), (1 - core, theirs_ref[k])):
            for step in (1, 2, 4):
                row_bit = (row & step) != 0
                lane_bit = (lane & (8 * step)) != 0
                up = pltpu.roll(pltpu.roll(block, 64 - step, 0), 8 * step, 1)
                down = pltpu.roll(pltpu.roll(block, step, 0), 128 - 8 * step, 1)
                swapped = jnp.where(row_bit, down, up)
                block = jnp.where(row_bit == lane_bit, block, swapped)
            turned_ref[...] = 2.0 * exch_ref[offset, k] - block
            even = turned_ref[pl.ds(0, 32, stride=2), :]
            odd = turned_ref[pl.ds(1, 32, stride=2), :]
            out_ref[offset, k, 0] = jnp.where(low_lane, even, pltpu.roll(odd, 64, 1))
            out_ref[offset, k, 1] = jnp.where(low_lane, pltpu.roll(even, 64, 1), odd)


def finish(pos, exch, mine, theirs):
    vmem = pl.BlockSpec(memory_space=pltpu.VMEM)
    return pl.pallas_call(
        final_kernel,
        out_shape=jax.ShapeDtypeStruct((NOFF, 3, 2, 32, 128), jnp.float32),
        in_specs=[pl.BlockSpec(memory_space=pltpu.SMEM)] + [vmem] * 3,
        out_specs=vmem,
        scratch_shapes=[pltpu.VMEM((64, 128), jnp.float32)],
    )(pos, exch, mine, theirs)


def three_pieces(values):
    high = lax.reduce_precision(values, 8, 7)
    rest = values - high
    middle = lax.reduce_precision(rest, 8, 7)
    low = rest - middle
    return jnp.stack([high, middle, low], axis=-1).astype(jnp.bfloat16)


def exchange_sums(pair_vc, coulomb, offsets, y, wait_for):
    groups = [[b * 8 + i for i in range(8)] for b in range(4)]
    sent = jnp.transpose(pair_vc.reshape(KX_DEV, 8, 3, 64, 128), (1, 0, 2, 3, 4)).reshape(8, 12, 64, 128)
    extra = jnp.pad(three_pieces(coulomb), ((0, 0), (0, 125)))
    sent = jnp.concatenate([sent, jnp.broadcast_to(extra, (8, 1, 64, 128))], axis=1)
    sent, _ = lax.optimization_barrier((sent, wait_for))
    here = lax.all_to_all(
        sent, "ga", split_axis=0, concat_axis=0, tiled=True, axis_index_groups=groups
    )
    near_coulomb = jnp.sum(here[:, 12, :, :3].astype(jnp.float32), axis=-1)
    here = here[:, :12].reshape(8, KX_DEV, 3, 64, 128)
    ahead = send(here, ka_back())
    before = send(here[:, :, 2:], ka_back_j_ahead())
    scaled = (near_coulomb.reshape(8, 1, 1, 64, 1) * here.astype(jnp.float32)).astype(jnp.bfloat16)
    special = jnp.where(offsets[0, 1] == NKY - 1, 0, 1)
    plain_x = offsets[1 - special, 0]
    shifted = jnp.concatenate([before, ahead[:, :, :2]], axis=2)
    joined = jnp.concatenate([here, ahead], axis=1)
    plain = lax.dynamic_slice_in_dim(joined, plain_x, KX_DEV, 1)

    def products(right):
        full = jnp.einsum("sabgp,sabgq->abpq", scaled, right, preferred_element_type=jnp.float32)
        half = full.shape[-1] // 2
        real_part = full[..., :half, :half] + full[..., half:, half:]
        imag_part = full[..., :half, half:] - full[..., half:, :half]
        return jnp.concatenate([real_part, imag_part], axis=-1)

    of_special = products(shifted)
    of_plain = products(plain)
    terms = jnp.stack(
        [jnp.where(special == 0, of_special, of_plain), jnp.where(special == 0, of_plain, of_special)],
        axis=1,
    )
    total = lax.dynamic_index_in_dim(terms, y, 0, keepdims=False)
    for step in (1, 2, 3):
        piece = lax.dynamic_index_in_dim(terms, lax.rem(y + step, 4), 0, keepdims=False)
        total = total + send(piece, along_y(step))
    return total


def swapped(dens, core):
    mine = lax.dynamic_index_in_dim(dens, core, 0, keepdims=False)
    theirs = lax.dynamic_index_in_dim(dens, 1 - core, 0, keepdims=False)
    got = send(theirs, other_core())
    return jnp.concatenate([mine.reshape(32, 3, 64, 128), got.reshape(32, 3, 64, 128)], axis=1)


def spread(packed):
    return lax.all_to_all(packed, "ga", split_axis=0, concat_axis=0, tiled=True)


def local(pair_vc, coulomb, dens_cc, dens_vv, screen, offsets):
    ka = lax.axis_index("ka")
    ga = lax.axis_index("ga")
    core = lax.rem(ka, 2)
    y, z_lo, x = ga // 8, lax.rem(ga // 4, 2), lax.rem(ga, 4)
    pos = jnp.stack([x, y, z_lo, core]).astype(jnp.int32)

    rows = lax.dynamic_index_in_dim(screen, core, 0, keepdims=True)
    rows = jnp.concatenate([rows, send(rows, along_z())], axis=0)
    exch = exchange_sums(pair_vc, coulomb, offsets, y, rows)
    rows = jnp.concatenate([rows, *ring_of_four(rows, along_first)], axis=0)
    valence = swapped(dens_vv, core)
    conduction = swapped(dens_cc, core)
    valence, rows = lax.optimization_barrier((valence, rows))
    behind, ahead, far_low, far_high = ring_of_four(rows, along_second)
    valence = spread(valence)
    conduction, _ = lax.optimization_barrier((conduction, valence))
    conduction = spread(conduction)

    valence = jnp.transpose(valence, (0, 2, 1, 3)).reshape(2048, 768)
    images = [image_of(part, valence) for part in (rows, behind, ahead, far_low, far_high)]
    theirs = send(direct_of(3, pos, images, conduction), other_core())
    mine = direct_of(0, pos, images, conduction)
    out = finish(pos, exch, mine, theirs)
    return jnp.transpose(out, (0, 2, 1, 3, 4)).reshape(NOFF, 2, 3, 4096)


def solution(mesh):
    placed = (
        P("ka", "ga", None),
        P("ga"),
        P(None, "ka", "ga", None),
        P(None, "ka", "ga", None),
        P(None, "ga", None),
        P(),
    )
    return jax.shard_map(
        local,
        mesh=mesh,
        in_specs=placed,
        out_specs=P(None, None, ("ka", "ga"), None),
        check_vma=False,
    )
```

time: 308 us -> 210 us (0.68)
  the two profiles are of different devices: /device:TPU:65 before, /device:TPU:35 now
where the time goes in v2:
time: 210 us; the launch traced here: 206 us
  waiting for transfers between devices  66.9 us (32%)
  starting transfers between devices  61.3 us (29%)
  local copies, waits for them, and re-layouts  40.3 us (19%)
  Pallas kernels  17.3 us (8%)
  other arithmetic  12.1 us (6%)
  matrix products  5.4 us (3%)
  between operations  3 us (1%)
    ppermute x17, waiting for transfers between devices, send(): return lax.ppermute(array, AXES, pairs)  48 us
    ppermute x17, starting transfers between devices, send(): return lax.ppermute(array, AXES, pairs)  39.1 us
    unnamed x49, local copies, waits for them, and re-layouts  17.4 us
    all_to_all x2, starting transfers between devices, spread(): return lax.all_to_all(packed, 'ga', split_axis=0, concat_axis=0, tiled=True)  17 us
    all_to_all x2, waiting for transfers between devices, spread(): return lax.all_to_all(packed, 'ga', split_axis=0, concat_axis=0, tiled=True)  13.1 us
    pallas_call x5, Pallas kernels, image_of(): pl.pallas_call(image_kernel, out_shape=jax.ShapeDtypeStruct((count, valen...  12.4 us
    dynamic_slice x2, local copies, waits for them, and re-layouts, swapped(): mine = lax.dynamic_index_in_dim(dens, core, 0, keepdims=False)  7.01 us
    all_to_all x1, waiting for transfers between devices, exchange_sums(): lax.all_to_all(sent, 'ga', split_axis=0, concat_axis=0, tiled=True, axis_...  5.76 us
  transfers between devices with their start and end apart: 20, of which 4 were waited for; matrix products, arithmetic and copies ran while one was open for 22% of the time, Pallas kernels for 7%

profile of v2, /device:TPU:35, one launch (start us, length us, event | category | flops | bytes accessed | tf_op | source)
XLA Modules:
  0.0 206.3 jit_solution(18026262682333704036)
XLA Ops:
  0.0 1.7 constant_dynamic-update-slice_fusion.5
  1.7 4.4 %constant_dynamic-slice_fusion.1 = (bf16[1,96,64,128]{3,2,1,0:T(8,128)(2,1)}, bf16[96,64,128]{2,1,0:T(8,128)(2,1)}) fusion(bf16[2,96,64,128]{3,2,1,0:T(8,128)(2,1)} %param.9, s32[]{:T(128)S(6)} %select_n.73, s32[]{:T(128)S(6)} %select_n.82), kind=kLoop, calls=%fused_computation.57 | loop fusion | bytes 6291464 | tf_op jit(solution)/shard_map/jit(dynamic_index_in_dim)/dynamic_slice | solution.py:236
  6.1 0.8 collective-permute-start.6
  6.9 1.9 collective-permute-done
  8.9 0.8 pad_maximum_fusion.3
  9.7 1.3 collective-permute-start.7
  11.0 1.4 collective-permute-start.8
  12.8 1.4 pad_maximum_fusion.2
  14.1 5.2 %all-to-all-start = ((bf16[8,13,64,128]{3,2,1,0:T(8,128)(2,1)}), bf16[8,13,64,128]{3,2,1,0:T(8,128)(2,1)S(1)}, u32[]{:S(2)}, u32[]{:S(2)}) async-start(bf16[8,13,64,128]{3,2,1,0:T(8,128)(2,1)} %pad_maximum_fusion.2), calls=%async_computation | async-start | bytes 3407872 | tf_op jit(solution)/shard_map/all_to_all | solution.py:201
  19.3 0.7 constant_dynamic-update-slice_fusion.4
  20.0 1.0 slice.80
  21.1 1.0 slice.81
  22.1 2.7 %collective-permute-start.10 = (bf16[1,64,2048]{2,1,0:T(8,128)(2,1)S(1)}, bf16[1,64,2048]{2,1,0:T(8,128)(2,1)S(1)}, u32[]{:S(2)}, u32[]{:S(2)}) collective-permute-start(bf16[1,64,2048]{2,1,0:T(8,128)(2,1)S(1)} %slice.81), channel_id=1, source_target_pairs={{0,3},{1,0},{2,1},{3,2},{4,7},{5,4},{6,5},{7,6},{8,11},{9,8},{10,9... | collective-permute-start | bytes 786440 | tf_op jit(solution)/shard_map/ppermute | solution.py:73
  24.8 1.9 constant_dynamic-update-slice_fusion.3
  26.7 1.9 constant_dynamic-update-slice_fusion.2
  28.6 0.7 constant_dynamic-update-slice_fusion.1
  29.3 0.7 constant_dynamic-update-slice_fusion.rows_ref
  30.1 3.4 %pad_maximum_fusion = bf16[32,6,64,128]{3,2,1,0:T(8,128)(2,1)} fusion(bf16[32,3,64,128]{3,2,1,0:T(8,128)(2,1)} %bitcast.29, bf16[32,3,64,128]{3,2,1,0:T(8,128)(2,1)S(1)} %bitcast.74), kind=kLoop, calls=%fused_computation.3 | loop fusion | flops 1572864 | bytes 6291456 | tf_op jit(solution)/shard_map/concatenate | solution.py:239
  33.4 5.8 %all-to-all-done = bf16[8,13,64,128]{3,2,1,0:T(8,128)(2,1)S(1)} async-done(((bf16[8,13,64,128]{3,2,1,0:T(8,128)(2,1)}), bf16[8,13,64,128]{3,2,1,0:T(8,128)(2,1)S(1)}, u32[]{:S(2)}, u32[]{:S(2)}) %all-to-all-start) | async-done | bytes 1703968 | tf_op jit(solution)/shard_map/all_to_all | solution.py:201
  39.2 1.2 copy-done.12
  40.4 7.5 %all-to-all-start.1 = ((bf16[32,6,64,128]{3,2,1,0:T(8,128)(2,1)}), bf16[32,6,64,128]{3,2,1,0:T(8,128)(2,1)S(1)}, u32[]{:S(2)}, u32[]{:S(2)}) async-start(bf16[32,6,64,128]{3,2,1,0:T(8,128)(2,1)} %pad_maximum_fusion), calls=%async_computation.1 | async-start | bytes 6291456 | tf_op jit(solution)/shard_map/all_to_all | solution.py:243
  47.9 2.6 %constant_dynamic-slice_fusion = (bf16[1,96,64,128]{3,2,1,0:T(8,128)(2,1)S(1)}, bf16[96,64,128]{2,1,0:T(8,128)(2,1)S(1)}) fusion(bf16[2,96,64,128]{3,2,1,0:T(8,128)(2,1)} %param.8, s32[]{:T(128)S(6)} %select_n.73, s32[]{:T(128)S(6)} %select_n.82), kind=kLoop, calls=%fused_computation.56 | loop fusion | bytes 6291464 | tf_op jit(solution)/shard_map/jit(dynamic_index_in_dim)/dynamic_slice | solution.py:236
  50.5 9.2 %collective-permute-start.15 = (bf16[96,64,128]{2,1,0:T(8,128)(2,1)S(1)}, bf16[96,64,128]{2,1,0:T(8,128)(2,1)S(1)}, u32[]{:S(2)}, u32[]{:S(2)}) collective-permute-start(bf16[96,64,128]{2,1,0:T(8,128)(2,1)S(1)} %get-tuple-element.16), channel_id=1, source_target_pairs={{0,32},{1,33},{2,34},{3,35},{4,36},{5,37},{6,38},{7,39},{8,40},{9,... | collective-permute-start | bytes 4718600 | tf_op jit(solution)/shard_map/ppermute | solution.py:73
  59.7 1.3 copy.14
  61.0 1.3 collective-permute-start.2
  62.3 1.2 collective-permute-start.11
  63.8 1.9 pad_maximum_fusion.1
  65.7 13.1 %all-to-all-done.1 = bf16[32,6,64,128]{3,2,1,0:T(8,128)(2,1)S(1)} async-done(((bf16[32,6,64,128]{3,2,1,0:T(8,128)(2,1)}), bf16[32,6,64,128]{3,2,1,0:T(8,128)(2,1)S(1)}, u32[]{:S(2)}, u32[]{:S(2)}) %all-to-all-start.1) | async-done | bytes 3145760 | tf_op jit(solution)/shard_map/all_to_all | solution.py:243
  78.8 1.7 copy-done.10
  80.5 9.5 %all-to-all-start.2 = ((bf16[32,6,64,128]{3,2,1,0:T(8,128)(2,1)}), bf16[32,6,64,128]{3,2,1,0:T(8,128)(2,1)S(1)}, u32[]{:S(2)}, u32[]{:S(2)}) async-start(bf16[32,6,64,128]{3,2,1,0:T(8,128)(2,1)} %pad_maximum_fusion.1), calls=%async_computation.2 | async-start | bytes 6291456 | tf_op jit(solution)/shard_map/all_to_all | solution.py:243
  90.0 1.9 slice.70
  91.9 15.9 %collective-permute-start.1 = (bf16[8,4,1,64,128]{4,3,0,2,1:T(8,128)(2,1)}, bf16[8,4,1,64,128]{4,3,0,2,1:T(8,128)(2,1)}, u32[]{:S(2)}, u32[]{:S(2)}) collective-permute-start(bf16[8,4,1,64,128]{4,3,0,2,1:T(8,128)(2,1)} %slice.70), channel_id=1, source_target_pairs={{0,97},{1,98},{2,99},{3,100},{4,101},{5,102},{6,103},{7,96},{8,105... | collective-permute-start | bytes 1572872 | tf_op jit(solution)/shard_map/ppermute | solution.py:73
  107.8 0.6 slice.51
  109.0 0.6 constant_dynamic-slice_fusion.2
  111.7 1.0 convert_reduce_fusion
  112.7 1.3 slice.71
  114.0 46.0 %collective-permute-done.1 = bf16[8,4,1,64,128]{4,3,0,2,1:T(8,128)(2,1)} collective-permute-done((bf16[8,4,1,64,128]{4,3,0,2,1:T(8,128)(2,1)}, bf16[8,4,1,64,128]{4,3,0,2,1:T(8,128)(2,1)}, u32[]{:S(2)}, u32[]{:S(2)}) %collective-permute-start.1) | collective-permute-done | bytes 524320 | tf_op jit(solution)/shard_map/ppermute | solution.py:73
  160.1 2.3 %fusion.7 = f32[4,3,128,128]{3,2,1,0:T(8,128)S(1)} fusion(bf16[8,4,2,64,128]{4,3,0,2,1:T(8,128)(2,1)S(1)} %slice.71, bf16[8,4,1,64,128]{4,3,0,2,1:T(8,128)(2,1)} %collective-permute-done.1, bf16[8,4,3,64,128]{4,3,0,2,1:T(8,128)(2,1)} %bitcast.11, f32[8,64]{1,0:T(8,128)S(1)} %convert_reduce_fusion), kind=kOutput, calls=%fused_computation.15 | convolution fusion | flops 204472320 | bytes 3934208 | tf_op jit(solution)/shard_map/sabgp,sabgq->abpq/dot_general | solution.py:216
  162.4 3.1 %fusion.10 = f32[4,3,128,128]{3,2,1,0:T(8,128)S(1)} fusion(s32[]{:T(128)S(6)} %select_n.75, bf16[8,4,3,64,128]{4,3,0,2,1:T(8,128)(2,1)} %bitcast.11, bf16[8,4,3,64,128]{4,3,0,2,1:T(8,128)(2,1)} %collective-permute-done.2, f32[8,64]{1,0:T(8,128)S(1)} %convert_reduce_fusion), kind=kOutput, calls=%fused_computation.16 | convolution fusion | flops 204472320 | bytes 5507076 | tf_op jit(solution)/shard_map/sabgp,sabgq->abpq/dot_general | solution.py:216
  165.5 1.3 slice.82
  166.9 1.3 slice.83
  168.2 1.7 collective-permute-start.14
  170.8 0.8 fusion.25
  171.6 1.8 collective-permute-start.5
  174.0 0.7 collective-permute-start.3
  174.8 2.9 %copy.15 = bf16[32,64,6,128]{3,2,1,0:T(8,128)(2,1)S(1)} copy(bf16[32,64,6,128]{3,1,2,0:T(8,128)(2,1)S(1)} %bitcast.72) | data formatting | bytes 6291456 | tf_op jit(solution)/shard_map/transpose | solution.py:265
  177.7 0.8 copy.21
  178.5 3.4 %shard_map.64.own_ref = bf16[512,768]{1,0:T(8,128)(2,1)S(1)} custom-call(bf16[8,64,2048]{2,1,0:T(8,128)(2,1)} %constant_dynamic-update-slice_fusion.rows_ref, bf16[2048,768]{1,0:T(8,128)(2,1)S(1)} %bitcast.66), custom_call_target="tpu_custom_call" | custom-call | flops 1610612736 | bytes 6029312 | tf_op jit(solution)/shard_map/pallas_call | solution.py:96
  181.9 3.7 %shard_map.65.behind_ref = bf16[512,768]{1,0:T(8,128)(2,1)S(1)} custom-call(bf16[8,64,2048]{2,1,0:T(8,128)(2,1)} %collective-permute-done.11.rows_ref, bf16[2048,768]{1,0:T(8,128)(2,1)S(1)} %bitcast.67), custom_call_target="tpu_custom_call" | custom-call | flops 1610612736 | bytes 6029312 | tf_op jit(solution)/shard_map/pallas_call | solution.py:96
  185.6 0.9 copy-done.2
  186.5 3.4 %shard_map.66.ahead_ref = bf16[512,768]{1,0:T(8,128)(2,1)S(1)} custom-call(bf16[8,64,2048]{2,1,0:T(8,128)(2,1)} %collective-permute-done.12.rows_ref, bf16[2048,768]{1,0:T(8,128)(2,1)S(1)} %bitcast.68), custom_call_target="tpu_custom_call" | custom-call | flops 1610612736 | bytes 6029312 | tf_op jit(solution)/shard_map/pallas_call | solution.py:96
  189.9 1.0 shard_map.67.low_ref
  190.9 1.0 shard_map.68.high_ref
  191.9 0.7 copy-done.6
  192.6 1.1 copy-done.1
  193.8 1.1 copy-done.3
  194.9 1.1 copy-done.5
  196.0 1.0 copy-done.7
  197.0 1.2 shard_map.70
  198.4 1.8 fusion.23.exch_ref
  200.3 1.2 shard_map.69.mine_ref
  201.5 0.6 copy-done.8
  202.1 2.5 %shard_map.71 = f32[2,3,2,32,128]{4,3,2,1,0:T(8,128)} custom-call(s32[4]{0:T(128)} %copy-done.9, f32[2,3,64,128]{3,2,1,0:T(8,128)} %fusion.23.exch_ref, f32[3,64,128]{2,1,0:T(8,128)} %copy-done.8, f32[3,64,128]{2,1,0:T(8,128)} %collective-permute-done.16.theirs_ref), custom_call_target="tpu_custom_call" | custom-call | tf_op jit(solution)/shard_map/pallas_call | solution.py:178
  204.6 1.7 reshape.161
  (67 shorter events, 2.4 us)
Async XLA Ops:
  1.7 7.2 %collective-permute-start = (bf16[1,64,2048]{2,1,0:T(8,128)(2,1)S(1)}, bf16[1,64,2048]{2,1,0:T(8,128)(2,1)S(1)}, u32[]{:S(2)}, u32[]{:S(2)}) collective-permute-start(bf16[1,64,2048]{2,1,0:T(8,128)(2,1)S(1)} %get-tuple-element.14), channel_id=1, source_target_pairs={{0,4},{1,5},{2,6},{3,7},{4,0},{5,1},{6,2},{7,3},{8,12},{9,13},{10,... | collective-permute-start | bytes 786440 | tf_op jit(solution)/shard_map/ppermute | solution.py:73
  1.7 5.2 %copy-start.19 = (f32[64]{0:T(128)S(1)}, f32[64]{0:T(128)}, u32[]{:S(2)}) copy-start(f32[64]{0:T(128)} %param.7) | copy-start | bytes 772
  1.7 10.9 %copy-start.18 = (bf16[96,64,128]{2,1,0:T(8,128)(2,1)S(1)}, bf16[96,64,128]{2,1,0:T(8,128)(2,1)}, u32[]{:S(2)}) copy-start(bf16[96,64,128]{2,1,0:T(8,128)(2,1)} %param.6) | copy-start | bytes 4718596
  6.1 23.9 %collective-permute-start.6 = (bf16[96,64,128]{2,1,0:T(8,128)(2,1)}, bf16[96,64,128]{2,1,0:T(8,128)(2,1)}, u32[]{:S(2)}, u32[]{:S(2)}) collective-permute-start(bf16[96,64,128]{2,1,0:T(8,128)(2,1)} %get-tuple-element.18), channel_id=1, source_target_pairs={{0,32},{1,33},{2,34},{3,35},{4,36},{5,37},{6,38},{7,39},{8,40},{9,... | collective-permute-start | bytes 4718600 | tf_op jit(solution)/shard_map/ppermute | solution.py:73
  9.7 10.3 %collective-permute-start.7 = (bf16[2,64,2048]{2,1,0:T(8,128)(2,1)}, bf16[2,64,2048]{2,1,0:T(8,128)(2,1)}, u32[]{:S(2)}, u32[]{:S(2)}) collective-permute-start(bf16[2,64,2048]{2,1,0:T(8,128)(2,1)} %pad_maximum_fusion.3), channel_id=1, source_target_pairs={{0,1},{1,2},{2,3},{3,0},{4,5},{5,6},{6,7},{7,4},{8,9},{9,10},{10,1... | collective-permute-start | bytes 1572872 | tf_op jit(solution)/shard_map/ppermute | solution.py:73
  11.0 10.1 %collective-permute-start.8 = (bf16[2,64,2048]{2,1,0:T(8,128)(2,1)}, bf16[2,64,2048]{2,1,0:T(8,128)(2,1)}, u32[]{:S(2)}, u32[]{:S(2)}) collective-permute-start(bf16[2,64,2048]{2,1,0:T(8,128)(2,1)} %pad_maximum_fusion.3), channel_id=1, source_target_pairs={{0,3},{1,0},{2,1},{3,2},{4,7},{5,4},{6,5},{7,6},{8,11},{9,8},{10,9... | collective-permute-start | bytes 1572872 | tf_op jit(solution)/shard_map/ppermute | solution.py:73
  14.1 25.1 %all-to-all-start = ((bf16[8,13,64,128]{3,2,1,0:T(8,128)(2,1)}), bf16[8,13,64,128]{3,2,1,0:T(8,128)(2,1)S(1)}, u32[]{:S(2)}, u32[]{:S(2)}) async-start(bf16[8,13,64,128]{3,2,1,0:T(8,128)(2,1)} %pad_maximum_fusion.2), calls=%async_computation | async-start | bytes 3407872 | tf_op jit(solution)/shard_map/all_to_all | solution.py:201
  21.0 7.6 %collective-permute-start.9 = (bf16[1,64,2048]{2,1,0:T(8,128)(2,1)S(1)}, bf16[1,64,2048]{2,1,0:T(8,128)(2,1)S(1)}, u32[]{:S(2)}, u32[]{:S(2)}) collective-permute-start(bf16[1,64,2048]{2,1,0:T(8,128)(2,1)S(1)} %slice.80), channel_id=1, source_target_pairs={{0,1},{1,2},{2,3},{3,0},{4,5},{5,6},{6,7},{7,4},{8,9},{9,10},{10,1... | collective-permute-start | bytes 786440 | tf_op jit(solution)/shard_map/ppermute | solution.py:73
  22.1 8.0 %copy-start.13 = (bf16[1,96,64,128]{3,2,1,0:T(8,128)(2,1)S(1)}, bf16[1,96,64,128]{3,2,1,0:T(8,128)(2,1)}, u32[]{:S(2)}) copy-start(bf16[1,96,64,128]{3,2,1,0:T(8,128)(2,1)} %get-tuple-element.17) | copy-start | bytes 4718596
  22.1 7.2 %collective-permute-start.10 = (bf16[1,64,2048]{2,1,0:T(8,128)(2,1)S(1)}, bf16[1,64,2048]{2,1,0:T(8,128)(2,1)S(1)}, u32[]{:S(2)}, u32[]{:S(2)}) collective-permute-start(bf16[1,64,2048]{2,1,0:T(8,128)(2,1)S(1)} %slice.81), channel_id=1, source_target_pairs={{0,3},{1,0},{2,1},{3,2},{4,7},{5,4},{6,5},{7,6},{8,11},{9,8},{10,9... | collective-permute-start | bytes 786440 | tf_op jit(solution)/shard_map/ppermute | solution.py:73
  39.2 1.2 copy-start.12
  40.4 38.4 %all-to-all-start.1 = ((bf16[32,6,64,128]{3,2,1,0:T(8,128)(2,1)}), bf16[32,6,64,128]{3,2,1,0:T(8,128)(2,1)S(1)}, u32[]{:S(2)}, u32[]{:S(2)}) async-start(bf16[32,6,64,128]{3,2,1,0:T(8,128)(2,1)} %pad_maximum_fusion), calls=%async_computation.1 | async-start | bytes 6291456 | tf_op jit(solution)/shard_map/all_to_all | solution.py:243
  50.5 9.2 %slice-start = ((bf16[8,13,64,128]{3,2,1,0:T(8,128)(2,1)}), bf16[8,12,64,128]{3,2,1,0:T(8,128)(2,1)S(1)}, s32[]{:S(2)}) async-start(bf16[8,13,64,128]{3,2,1,0:T(8,128)(2,1)} %copy-done.12), calls=%async_computation.3 | async-start | bytes 3145728 | tf_op jit(solution)/shard_map/slice | solution.py:205
  50.5 13.3 %collective-permute-start.15 = (bf16[96,64,128]{2,1,0:T(8,128)(2,1)S(1)}, bf16[96,64,128]{2,1,0:T(8,128)(2,1)S(1)}, u32[]{:S(2)}, u32[]{:S(2)}) collective-permute-start(bf16[96,64,128]{2,1,0:T(8,128)(2,1)S(1)} %get-tuple-element.16), channel_id=1, source_target_pairs={{0,32},{1,33},{2,34},{3,35},{4,36},{5,37},{6,38},{7,39},{8,40},{9,... | collective-permute-start | bytes 4718600 | tf_op jit(solution)/shard_map/ppermute | solution.py:73
  61.0 51.7 %collective-permute-start.2 = (bf16[8,4,3,64,128]{4,3,0,2,1:T(8,128)(2,1)}, bf16[8,4,3,64,128]{4,3,0,2,1:T(8,128)(2,1)}, u32[]{:S(2)}, u32[]{:S(2)}) collective-permute-start(bf16[8,4,3,64,128]{4,3,0,2,1:T(8,128)(2,1)} %bitcast.11), channel_id=1, source_target_pairs={{0,96},{1,97},{2,98},{3,99},{4,100},{5,101},{6,102},{7,103},{8,104... | collective-permute-start | bytes 4718600 | tf_op jit(solution)/shard_map/ppermute | solution.py:73
  62.3 103.2 %collective-permute-start.11 = (bf16[8,64,2048]{2,1,0:T(8,128)(2,1)}, bf16[8,64,2048]{2,1,0:T(8,128)(2,1)}, u32[]{:S(2)}, u32[]{:S(2)}) collective-permute-start(bf16[8,64,2048]{2,1,0:T(8,128)(2,1)} %constant_dynamic-update-slice_fusion.rows_ref), channel_id=1, source_target_pairs={{0,8},{1,9},{2,10},{3,11},{4,12},{5,13},{6,14},{7,15},{8,16},{9,17... | collective-permute-start | bytes 6291464 | tf_op jit(solution)/shard_map/ppermute | solution.py:73
  63.5 103.4 %collective-permute-start.12 = (bf16[8,64,2048]{2,1,0:T(8,128)(2,1)}, bf16[8,64,2048]{2,1,0:T(8,128)(2,1)}, u32[]{:S(2)}, u32[]{:S(2)}) collective-permute-start(bf16[8,64,2048]{2,1,0:T(8,128)(2,1)} %constant_dynamic-update-slice_fusion.rows_ref), channel_id=1, source_target_pairs={{0,24},{1,25},{2,26},{3,27},{4,28},{5,29},{6,30},{7,31},{8,0},{9,1... | collective-permute-start | bytes 6291464 | tf_op jit(solution)/shard_map/ppermute | solution.py:73
  65.7 42.1 %copy-start.20 = (s32[2,2]{1,0:T(2,128)S(1)}, s32[2,2]{1,0:T(2,128)}, u32[]{:S(2)}) copy-start(s32[2,2]{1,0:T(2,128)} %param.11) | copy-start | bytes 52
  78.8 1.7 copy-start.10
  80.5 112.1 %all-to-all-start.2 = ((bf16[32,6,64,128]{3,2,1,0:T(8,128)(2,1)}), bf16[32,6,64,128]{3,2,1,0:T(8,128)(2,1)S(1)}, u32[]{:S(2)}, u32[]{:S(2)}) async-start(bf16[32,6,64,128]{3,2,1,0:T(8,128)(2,1)} %pad_maximum_fusion.1), calls=%async_computation.2 | async-start | bytes 6291456 | tf_op jit(solution)/shard_map/all_to_all | solution.py:243
  91.9 68.2 %collective-permute-start.1 = (bf16[8,4,1,64,128]{4,3,0,2,1:T(8,128)(2,1)}, bf16[8,4,1,64,128]{4,3,0,2,1:T(8,128)(2,1)}, u32[]{:S(2)}, u32[]{:S(2)}) collective-permute-start(bf16[8,4,1,64,128]{4,3,0,2,1:T(8,128)(2,1)} %slice.70), channel_id=1, source_target_pairs={{0,97},{1,98},{2,99},{3,100},{4,101},{5,102},{6,103},{7,96},{8,105... | collective-permute-start | bytes 1572872 | tf_op jit(solution)/shard_map/ppermute | solution.py:73
  111.7 88.6 %copy-start.9 = (s32[4]{0:T(128)}, s32[4]{0:T(128)S(1)}, u32[]{:S(2)}) copy-start(s32[4]{0:T(128)S(1)} %pad_add_fusion.pos_ref) | copy-start | bytes 52
  166.8 23.1 %collective-permute-start.13 = (bf16[4,64,2048]{2,1,0:T(8,128)(2,1)S(1)}, bf16[4,64,2048]{2,1,0:T(8,128)(2,1)S(1)}, u32[]{:S(2)}, u32[]{:S(2)}) collective-permute-start(bf16[4,64,2048]{2,1,0:T(8,128)(2,1)S(1)} %slice.82), channel_id=1, source_target_pairs={{0,8},{1,9},{2,10},{3,11},{4,12},{5,13},{6,14},{7,15},{8,16},{9,17... | collective-permute-start | bytes 3145736 | tf_op jit(solution)/shard_map/ppermute | solution.py:73
  168.2 22.7 %collective-permute-start.14 = (bf16[4,64,2048]{2,1,0:T(8,128)(2,1)S(1)}, bf16[4,64,2048]{2,1,0:T(8,128)(2,1)S(1)}, u32[]{:S(2)}, u32[]{:S(2)}) collective-permute-start(bf16[4,64,2048]{2,1,0:T(8,128)(2,1)S(1)} %slice.83), channel_id=1, source_target_pairs={{0,24},{1,25},{2,26},{3,27},{4,28},{5,29},{6,30},{7,31},{8,0},{9,1... | collective-permute-start | bytes 3145736 | tf_op jit(solution)/shard_map/ppermute | solution.py:73
  170.5 4.3 %copy-start.11 = (bf16[32,6,64,128]{3,2,1,0:T(8,128)(2,1)S(1)}, bf16[32,6,64,128]{3,2,1,0:T(8,128)(2,1)}, u32[]{:S(2)}) copy-start(bf16[32,6,64,128]{3,2,1,0:T(8,128)(2,1)} %copy-done.10) | copy-start | bytes 9437188
  170.8 4.0 %copy-start.14 = (f32[4,1,3,64,128]{4,3,2,0,1:T(8,128)}, f32[4,1,3,64,128]{4,3,2,0,1:T(8,128)S(1)}, u32[]{:S(2)}) copy-start(f32[4,1,3,64,128]{4,3,2,0,1:T(8,128)S(1)} %get-tuple-element.19) | copy-start | bytes 1179652
  170.8 4.0 %copy-start.16 = (f32[4,1,3,64,128]{4,3,2,0,1:T(8,128)}, f32[4,1,3,64,128]{4,3,2,0,1:T(8,128)S(1)}, u32[]{:S(2)}) copy-start(f32[4,1,3,64,128]{4,3,2,0,1:T(8,128)S(1)} %get-tuple-element.20) | copy-start | bytes 1179652
  171.6 26.7 %collective-permute-start.5 = (f32[2,3,64,128]{3,2,1,0:T(8,128)}, f32[2,3,64,128]{3,2,1,0:T(8,128)}, u32[]{:S(2)}, u32[]{:S(2)}) collective-permute-start(f32[2,3,64,128]{3,2,1,0:T(8,128)} %get-tuple-element.23), channel_id=1, source_target_pairs={{0,24},{1,25},{2,26},{3,27},{4,28},{5,29},{6,30},{7,31},{8,0},{9,1... | collective-permute-start | bytes 589832 | tf_op jit(solution)/shard_map/ppermute | solution.py:73
  173.4 24.9 %collective-permute-start.4 = (f32[2,3,64,128]{3,2,1,0:T(8,128)}, f32[2,3,64,128]{3,2,1,0:T(8,128)}, u32[]{:S(2)}, u32[]{:S(2)}) collective-permute-start(f32[2,3,64,128]{3,2,1,0:T(8,128)} %get-tuple-element.22), channel_id=1, source_target_pairs={{0,16},{1,17},{2,18},{3,19},{4,20},{5,21},{6,22},{7,23},{8,24},{9,... | collective-permute-start | bytes 589832 | tf_op jit(solution)/shard_map/ppermute | solution.py:73
  174.0 24.4 %collective-permute-start.3 = (f32[2,3,64,128]{3,2,1,0:T(8,128)}, f32[2,3,64,128]{3,2,1,0:T(8,128)}, u32[]{:S(2)}, u32[]{:S(2)}) collective-permute-start(f32[2,3,64,128]{3,2,1,0:T(8,128)} %get-tuple-element.21), channel_id=1, source_target_pairs={{0,8},{1,9},{2,10},{3,11},{4,12},{5,13},{6,14},{7,15},{8,16},{9,17... | collective-permute-start | bytes 589832 | tf_op jit(solution)/shard_map/ppermute | solution.py:73
  181.9 3.7 %copy-start = (bf16[512,768]{1,0:T(8,128)(2,1)}, bf16[512,768]{1,0:T(8,128)(2,1)S(1)}, u32[]{:S(2)}) copy-start(bf16[512,768]{1,0:T(8,128)(2,1)S(1)} %shard_map.64.own_ref) | copy-start | bytes 2359300
  185.6 0.9 copy-start.2
  189.9 1.0 copy-start.4
  191.9 0.7 copy-start.6
  192.6 1.1 copy-start.1
  193.8 1.1 copy-start.3
  194.9 1.1 copy-start.5
  196.0 1.0 copy-start.7
  197.0 1.4 copy-start.15
  197.0 1.4 copy-start.17
  198.3 3.9 %collective-permute-start.16 = (f32[3,64,128]{2,1,0:T(8,128)S(1)}, f32[3,64,128]{2,1,0:T(8,128)}, u32[]{:S(2)}, u32[]{:S(2)}) collective-permute-start(f32[3,64,128]{2,1,0:T(8,128)S(1)} %shard_map.70), channel_id=1, source_target_pairs={{0,32},{1,33},{2,34},{3,35},{4,36},{5,37},{6,38},{7,39},{8,40},{9,... | collective-permute-start | bytes 294920 | tf_op jit(solution)/shard_map/ppermute | solution.py:73
  201.5 0.6 copy-start.8

commit v3 on v2

v3 whole, which is shorter than its diff:
```python
import functools

import jax
import jax.numpy as jnp
from jax import lax
from jax.experimental import pallas as pl
from jax.experimental.pallas import tpu as pltpu
from jax.sharding import PartitionSpec as P

NV = 8
NC = 8
NKY = 24
KX_DEV = 4
NOFF = 2
AXES = ("ka", "ga")
A_STEPS = (0, 0, -1, -1, 1, 1, 2, 2)
Z_STEPS = (0, 1, 0, 1, 0, 1, 0, 1)
B_STEPS = (0, -1, 1, 2)


def index_of(x, y, z_hi, z_lo, core):
    return (z_hi * 2 + core) * 32 + (y % 4) * 8 + (z_lo % 2) * 4 + x % 4


def route(move):
    pairs = []
    for source in range(128):
        ka, ga = divmod(source, 32)
        z_hi, core = divmod(ka, 2)
        y, rest = divmod(ga, 8)
        z_lo, x = divmod(rest, 4)
        pairs.append((source, move(x, y, z_hi, z_lo, core)))
    return pairs


def along_first(step):
    return route(
        lambda x, y, h, l, c: index_of(x + step, y, h, l, c) if c == 0 else index_of(x, y + step, h, l, c)
    )


def along_second(step):
    return route(
        lambda x, y, h, l, c: index_of(x, y + step, h, l, c) if c == 0 else index_of(x + step, y, h, l, c)
    )


def along_y(step):
    return route(lambda x, y, h, l, c: index_of(x, y + step, h, l, c))


def along_z():
    return route(lambda x, y, h, l, c: index_of(x, y, h, l + 1, c))


def other_core():
    return route(lambda x, y, h, l, c: index_of(x, y, h, l, 1 - c))


def ka_back():
    return [(i, (i - 32) % 128) for i in range(128)]


def ka_back_j_ahead():
    pairs = []
    for source in range(128):
        ka, ga = divmod(source, 32)
        y, j = divmod(ga, 8)
        pairs.append((source, ((ka - 1) % 4) * 32 + y * 8 + (j + 1) % 8))
    return pairs


def send(array, pairs):
    return lax.ppermute(array, AXES, pairs)


def image_kernel(*refs):
    valence_ref, out_ref = refs[-2], refs[-1]
    first = 0
    for rows_ref in refs[:-2]:
        blocks, depth, width = rows_ref.shape
        for block in range(0, blocks, 4):
            rows = rows_ref[block : block + 4].reshape(4 * depth, width)
            out_ref[first : first + 4 * depth] = jnp.dot(
                rows, valence_ref[...], preferred_element_type=jnp.float32
            ).astype(jnp.bfloat16)
            first += 4 * depth


def image_of(parts, valence):
    vmem = pl.BlockSpec(memory_space=pltpu.VMEM)
    count = sum(part.shape[0] * part.shape[1] for part in parts)
    return pl.pallas_call(
        image_kernel,
        out_shape=jax.ShapeDtypeStruct((count, valence.shape[1]), jnp.bfloat16),
        in_specs=[vmem] * (len(parts) + 1),
        out_specs=vmem,
        compiler_params=pltpu.CompilerParams(vmem_limit_bytes=28 * 1024 * 1024),
        cost_estimate=pl.CostEstimate(
            flops=2 * count * valence.shape[0] * valence.shape[1],
            bytes_accessed=2 * (count * 2048 + valence.size + count * valence.shape[1]),
            transcendentals=0,
        ),
    )(*parts, valence)


def direct_kernel(from_k, pos_ref, *refs):
    parts, conduction_ref, out_ref = refs[:-2], refs[-2], refs[-1]
    x, y, z_lo, core = pos_ref[0], pos_ref[1], pos_ref[2], pos_ref[3]
    along_a = jnp.where(core == 0, x, y)
    along_b = jnp.where(core == 0, y, x)
    places = []
    for step in B_STEPS:
        b_now = lax.rem(along_b + (step + 4), 4)
        for block in range(8):
            a_now = lax.rem(along_a + (A_STEPS[block] + 4), 4)
            z_now = lax.rem(z_lo + Z_STEPS[block], 2)
            x_now = jnp.where(core == 0, a_now, b_now)
            y_now = jnp.where(core == 0, b_now, a_now)
            places.append(y_now * 8 + z_now * 4 + x_now)
    lane = lax.broadcasted_iota(jnp.int32, (64, 128), 1)
    for k in range(out_ref.shape[0]):
        columns = pl.ds((from_k + k) * 128, 128)
        full = jnp.zeros((128, 128), jnp.float32)
        first = 0
        for part in parts:
            blocks = part.shape[0] // 64
            right = jnp.concatenate(
                [conduction_ref[place, from_k + k] for place in places[first : first + blocks]], axis=0
            )
            first += blocks
            full += lax.dot_general(
                part[:, columns], right, (((0,), (0,)), ((), ())), preferred_element_type=jnp.float32
            )
        turned = pltpu.roll(full[64:], 64, 1)
        out_ref[k] = jnp.where(lane < 64, turned + full[:64], turned - full[:64])


def direct_of(from_k, pos, images, conduction):
    vmem = pl.BlockSpec(memory_space=pltpu.VMEM)
    return pl.pallas_call(
        functools.partial(direct_kernel, from_k),
        out_shape=jax.ShapeDtypeStruct((3, 64, 128), jnp.float32),
        in_specs=[pl.BlockSpec(memory_space=pltpu.SMEM)] + [vmem] * (len(images) + 1),
        out_specs=vmem,
        compiler_params=pltpu.CompilerParams(vmem_limit_bytes=20 * 1024 * 1024),
        cost_estimate=pl.CostEstimate(
            flops=2 * 3 * 2048 * 128 * 128, bytes_accessed=6 * 1024 * 1024, transcendentals=0
        ),
    )(pos, *images, conduction)


def final_kernel(pos_ref, exch_0, exch_1, exch_2, exch_3, mine_ref, theirs_ref, out_ref):
    core = pos_ref[3]
    lane = lax.broadcasted_iota(jnp.int32, (64, 128), 1)
    row = lax.broadcasted_iota(jnp.int32, (64, 128), 0)

    def exchanged(block, row_step, lane_step):
        row_bit = (row & row_step) != 0
        lane_bit = (lane & lane_step) != 0
        up = pltpu.roll(pltpu.roll(block, 64 - row_step, 0), lane_step, 1)
        down = pltpu.roll(pltpu.roll(block, row_step, 0), 128 - lane_step, 1)
        return jnp.where(row_bit == lane_bit, block, jnp.where(row_bit, down, up))

    for k in range(3):
        for offset, block in ((core, mine_ref[k]), (1 - core, theirs_ref[k])):
            for step in (1, 2, 4):
                block = exchanged(block, step, 8 * step)
            exch = (exch_0[offset, k] + exch_1[offset, k]) + (exch_2[offset, k] + exch_3[offset, k])
            out_ref[offset, k] = exchanged(2.0 * exch - block, 1, 64)


def finish(pos, exch, mine, theirs):
    vmem = pl.BlockSpec(memory_space=pltpu.VMEM)
    return pl.pallas_call(
        final_kernel,
        out_shape=jax.ShapeDtypeStruct((NOFF, 3, 64, 128), jnp.float32),
        in_specs=[pl.BlockSpec(memory_space=pltpu.SMEM)] + [vmem] * 6,
        out_specs=vmem,
    )(pos, *exch, mine, theirs)


def three_pieces(values):
    high = lax.reduce_precision(values, 8, 7)
    rest = values - high
    middle = lax.reduce_precision(rest, 8, 7)
    low = rest - middle
    return jnp.stack([high, middle, low], axis=-1).astype(jnp.bfloat16)


def exchange_spread(pair_vc, coulomb):
    main = pair_vc.reshape(KX_DEV, 8, 3, 64, 128)
    last = main[:, :, 2:]
    before = jnp.concatenate([last[:, 7:], last[:, :7]], axis=1)
    sent = jnp.concatenate([before, main], axis=2)
    sent = jnp.transpose(sent, (1, 0, 2, 3, 4)).reshape(8, 16, 64, 128)
    extra = jnp.pad(three_pieces(coulomb), ((0, 0), (0, 125)))
    return jnp.concatenate([sent, jnp.broadcast_to(extra, (8, 1, 64, 128))], axis=1)


def exchange_sums(here, ahead, near_coulomb, offsets, y):
    left = here[:, :, 1:].astype(jnp.float32)
    scaled = (near_coulomb.reshape(8, 1, 1, 64, 1) * left).astype(jnp.bfloat16)
    special = jnp.where(offsets[0, 1] == NKY - 1, 0, 1)
    plain_x = offsets[1 - special, 0]
    shifted = ahead[:, :, :3]
    joined = jnp.concatenate([here[:, :, 1:], ahead[:, :, 1:]], axis=1)
    plain = lax.dynamic_slice_in_dim(joined, plain_x, KX_DEV, 1)

    def products(right):
        full = jnp.einsum("sabgp,sabgq->abpq", scaled, right, preferred_element_type=jnp.float32)
        half = full.shape[-1] // 2
        real_part = full[..., :half, :half] + full[..., half:, half:]
        imag_part = full[..., :half, half:] - full[..., half:, :half]
        return jnp.concatenate([real_part, imag_part], axis=-1)

    of_special = products(shifted)
    of_plain = products(plain)
    terms = jnp.stack(
        [jnp.where(special == 0, of_special, of_plain), jnp.where(special == 0, of_plain, of_special)],
        axis=1,
    )
    pieces = [lax.dynamic_index_in_dim(terms, y, 0, keepdims=False)]
    for step in (1, 2, 3):
        piece = lax.dynamic_index_in_dim(terms, lax.rem(y + step, 4), 0, keepdims=False)
        pieces.append(send(piece, along_y(step)))
    return pieces


def both_cores(dens, core):
    mine = lax.dynamic_index_in_dim(dens, core, 0, keepdims=False)
    theirs = lax.dynamic_index_in_dim(dens, 1 - core, 0, keepdims=False)
    got = send(theirs, other_core())
    return jnp.concatenate([mine.reshape(32, 3, 64, 128), got.reshape(32, 3, 64, 128)], axis=1)


def spread(packed, groups=None):
    return lax.all_to_all(
        packed, "ga", split_axis=0, concat_axis=0, tiled=True, axis_index_groups=groups
    )


def local(pair_vc, coulomb, dens_cc, dens_vv, screen, offsets):
    ka = lax.axis_index("ka")
    ga = lax.axis_index("ga")
    core = lax.rem(ka, 2)
    y, z_lo, x = ga // 8, lax.rem(ga // 4, 2), lax.rem(ga, 4)
    pos = jnp.stack([x, y, z_lo, core]).astype(jnp.int32)
    after = lax.optimization_barrier

    rows = lax.dynamic_index_in_dim(screen, core, 0, keepdims=True)
    rows = jnp.concatenate([rows, send(rows, along_z())], axis=0)
    sent = exchange_spread(pair_vc, coulomb)
    sent, rows = after((sent, rows))
    near = [send(rows, along_first(step)) for step in (1, -1)]
    across = send(rows, along_first(2))
    here = spread(sent, [[b * 8 + i for i in range(8)] for b in range(4)])
    valence = both_cores(dens_vv, core)
    valence, near, across = after((valence, near, across))
    rows = jnp.concatenate([rows, *near, across], axis=0)
    behind = send(rows, along_second(1))
    ahead = send(rows, along_second(-1))
    valence = spread(valence)

    near_coulomb = jnp.sum(here[:, 16, :, :3].astype(jnp.float32), axis=-1)
    here = here[:, :16].reshape(8, KX_DEV, 4, 64, 128)
    next_rows = send(here, ka_back())

    conduction = both_cores(dens_cc, core)
    conduction, valence, next_rows, behind, ahead = after((conduction, valence, next_rows, behind, ahead))
    far_low, far_high = send(behind[:4], along_second(1)), send(ahead[4:], along_second(-1))
    conduction = spread(conduction)

    valence = jnp.transpose(valence, (0, 2, 1, 3)).reshape(2048, 768)
    images = [image_of((rows, behind, ahead), valence), image_of((far_low, far_high), valence)]
    exch = exchange_sums(here, next_rows, near_coulomb, offsets, y)

    theirs = send(direct_of(3, pos, images, conduction), other_core())
    mine = direct_of(0, pos, images, conduction)
    out = finish(pos, exch, mine, theirs).reshape(NOFF, 3, 32, 2, 128)
    return jnp.transpose(out, (0, 3, 1, 2, 4)).reshape(NOFF, 2, 3, 4096)


def solution(mesh):
    placed = (
        P("ka", "ga", None),
        P("ga"),
        P(None, "ka", "ga", None),
        P(None, "ka", "ga", None),
        P(None, "ga", None),
        P(),
    )
    return jax.shard_map(
        local,
        mesh=mesh,
        in_specs=placed,
        out_specs=P(None, None, ("ka", "ga"), None),
        check_vma=False,
    )
```

time: 210 us -> 194 us (0.924)
  the two profiles are of different devices: /device:TPU:35 before, /device:TPU:5 now
where the time goes in v3:
time: 194 us; the launch traced here: 193 us
  waiting for transfers between devices  69.6 us (36%)
  starting transfers between devices  59.9 us (31%)
  local copies, waits for them, and re-layouts  33.9 us (17%)
  Pallas kernels  14.7 us (8%)
  other arithmetic  8.2 us (4%)
  matrix products  3.57 us (2%)
  between operations  2.9 us (1%)
    ppermute x15, waiting for transfers between devices, send(): return lax.ppermute(array, AXES, pairs)  64.5 us
    ppermute x15, starting transfers between devices, send(): return lax.ppermute(array, AXES, pairs)  38.2 us
    all_to_all x3, starting transfers between devices, spread(): lax.all_to_all(packed, 'ga', split_axis=0, concat_axis=0, tiled=True, axi...  21.7 us
    unnamed x61, local copies, waits for them, and re-layouts  17.7 us
    pallas_call x2, Pallas kernels, image_of(): pl.pallas_call(image_kernel, out_shape=jax.ShapeDtypeStruct((count, valen...  9.32 us
    all_to_all x3, waiting for transfers between devices, spread(): lax.all_to_all(packed, 'ga', split_axis=0, concat_axis=0, tiled=True, axi...  5.1 us
  transfers between devices with their start and end apart: 18, of which 9 were waited for; matrix products, arithmetic and copies ran while one was open for 16% of the time, Pallas kernels for 6%

profile of v3, /device:TPU:5, one launch (start us, length us, event | category | flops | bytes accessed | tf_op | source)
XLA Modules:
  0.0 192.7 jit_solution(1533982961810627415)
XLA Ops:
  0.0 1.0 copy-done
  1.1 1.7 collective-permute-start
  2.8 0.8 slice.76
  3.6 1.1 slice.77
  4.7 0.7 fusion.24
  5.8 1.6 pad_maximum_fusion.2
  7.4 1.3 collective-permute-done
  8.8 5.2 %all-to-all-start = ((bf16[8,17,64,128]{3,2,1,0:T(8,128)(2,1)}), bf16[8,17,64,128]{3,2,1,0:T(8,128)(2,1)S(1)}, u32[]{:S(2)}, u32[]{:S(2)}) async-start(bf16[8,17,64,128]{3,2,1,0:T(8,128)(2,1)} %pad_maximum_fusion.2), calls=%async_computation | async-start | bytes 4456448 | tf_op jit(solution)/shard_map/all_to_all | solution.py:238
  14.0 2.6 %constant_dynamic-slice_fusion.1 = (bf16[1,96,64,128]{3,2,1,0:T(8,128)(2,1)S(1)}, bf16[96,64,128]{2,1,0:T(8,128)(2,1)S(1)}) fusion(bf16[2,96,64,128]{3,2,1,0:T(8,128)(2,1)} %param.9, s32[]{:T(128)S(6)} %select_n.73, s32[]{:T(128)S(6)} %select_n.74), kind=kLoop, calls=%fused_computation.52 | loop fusion | bytes 6291464 | tf_op jit(solution)/shard_map/jit(dynamic_index_in_dim)/dynamic_slice | solution.py:231
  16.6 2.2 %collective-permute-start.2 = (bf16[96,64,128]{2,1,0:T(8,128)(2,1)S(1)}, bf16[96,64,128]{2,1,0:T(8,128)(2,1)S(1)}, u32[]{:S(2)}, u32[]{:S(2)}) collective-permute-start(bf16[96,64,128]{2,1,0:T(8,128)(2,1)S(1)} %get-tuple-element.28), channel_id=1, source_target_pairs={{0,32},{1,33},{2,34},{3,35},{4,36},{5,37},{6,38},{7,39},{8,40},{9,... | collective-permute-start | bytes 4718600 | tf_op jit(solution)/shard_map/ppermute | solution.py:74
  18.8 2.9 %collective-permute-start.5 = (bf16[2,64,2048]{2,1,0:T(8,128)(2,1)S(1)}, bf16[2,64,2048]{2,1,0:T(8,128)(2,1)S(1)}, u32[]{:S(2)}, u32[]{:S(2)}) collective-permute-start(bf16[2,64,2048]{2,1,0:T(8,128)(2,1)S(1)} %pad_maximum_fusion.4), channel_id=1, source_target_pairs={{0,2},{1,3},{2,0},{3,1},{4,6},{5,7},{6,4},{7,5},{8,10},{9,11},{10,... | collective-permute-start | bytes 1572872 | tf_op jit(solution)/shard_map/ppermute | solution.py:74
  21.7 0.8 collective-permute-start.4
  22.4 0.7 collective-permute-start.3
  23.1 1.9 %pad_maximum_fusion.1 = bf16[32,6,64,128]{3,2,1,0:T(8,128)(2,1)} fusion(bf16[32,3,64,128]{3,2,1,0:T(8,128)(2,1)S(1)} %bitcast.73, bf16[32,3,64,128]{3,2,1,0:T(8,128)(2,1)S(1)} %bitcast.68), kind=kLoop, calls=%fused_computation.2 | loop fusion | flops 1572864 | bytes 6291456 | tf_op jit(solution)/shard_map/concatenate | solution.py:234
  25.1 3.3 %collective-permute-done.5 = bf16[2,64,2048]{2,1,0:T(8,128)(2,1)S(1)} collective-permute-done((bf16[2,64,2048]{2,1,0:T(8,128)(2,1)S(1)}, bf16[2,64,2048]{2,1,0:T(8,128)(2,1)S(1)}, u32[]{:S(2)}, u32[]{:S(2)}) %collective-permute-start.5) | collective-permute-done | bytes 524320 | tf_op jit(solution)/shard_map/ppermute | solution.py:74
  28.4 6.2 %collective-permute-done.4 = bf16[2,64,2048]{2,1,0:T(8,128)(2,1)S(1)} collective-permute-done((bf16[2,64,2048]{2,1,0:T(8,128)(2,1)S(1)}, bf16[2,64,2048]{2,1,0:T(8,128)(2,1)S(1)}, u32[]{:S(2)}, u32[]{:S(2)}) %collective-permute-start.4) | collective-permute-done | bytes 524320 | tf_op jit(solution)/shard_map/ppermute | solution.py:74
  34.6 0.8 copy-done.23
  35.4 5.1 %all-to-all-done = bf16[8,17,64,128]{3,2,1,0:T(8,128)(2,1)S(1)} async-done(((bf16[8,17,64,128]{3,2,1,0:T(8,128)(2,1)}), bf16[8,17,64,128]{3,2,1,0:T(8,128)(2,1)S(1)}, u32[]{:S(2)}, u32[]{:S(2)}) %all-to-all-start) | async-done | bytes 2228256 | tf_op jit(solution)/shard_map/all_to_all | solution.py:238
  40.5 1.4 copy-done.14
  41.9 7.3 %all-to-all-start.1 = ((bf16[32,6,64,128]{3,2,1,0:T(8,128)(2,1)}), bf16[32,6,64,128]{3,2,1,0:T(8,128)(2,1)S(1)}, u32[]{:S(2)}, u32[]{:S(2)}) async-start(bf16[32,6,64,128]{3,2,1,0:T(8,128)(2,1)} %pad_maximum_fusion.1), calls=%async_computation.1 | async-start | bytes 6291456 | tf_op jit(solution)/shard_map/all_to_all | solution.py:238
  49.3 1.2 constant_dynamic-update-slice_fusion.3
  50.4 1.1 constant_dynamic-update-slice_fusion.2
  52.0 1.2 collective-permute-start.7
  53.2 0.8 slice-done
  54.2 14.1 %collective-permute-start.6 = (bf16[8,4,4,64,128]{4,3,0,2,1:T(8,128)(2,1)S(1)}, bf16[8,4,4,64,128]{4,3,0,2,1:T(8,128)(2,1)}, u32[]{:S(2)}, u32[]{:S(2)}) collective-permute-start(bf16[8,4,4,64,128]{4,3,0,2,1:T(8,128)(2,1)S(1)} %bitcast.65), channel_id=1, source_target_pairs={{0,96},{1,97},{2,98},{3,99},{4,100},{5,101},{6,102},{7,103},{8,104... | collective-permute-start | bytes 6291464 | tf_op jit(solution)/shard_map/ppermute | solution.py:74
  68.3 0.7 constant_dynamic-slice_fusion.2
  69.0 2.4 %collective-permute-start.1 = (bf16[96,64,128]{2,1,0:T(8,128)(2,1)S(1)}, bf16[96,64,128]{2,1,0:T(8,128)(2,1)S(1)}, u32[]{:S(2)}, u32[]{:S(2)}) collective-permute-start(bf16[96,64,128]{2,1,0:T(8,128)(2,1)S(1)} %get-tuple-element.30), channel_id=1, source_target_pairs={{0,32},{1,33},{2,34},{3,35},{4,36},{5,37},{6,38},{7,39},{8,40},{9,... | collective-permute-start | bytes 4718600 | tf_op jit(solution)/shard_map/ppermute | solution.py:74
  71.4 3.0 %collective-permute-done.1 = bf16[96,64,128]{2,1,0:T(8,128)(2,1)S(1)} collective-permute-done((bf16[96,64,128]{2,1,0:T(8,128)(2,1)S(1)}, bf16[96,64,128]{2,1,0:T(8,128)(2,1)S(1)}, u32[]{:S(2)}, u32[]{:S(2)}) %collective-permute-start.1) | collective-permute-done | bytes 1572896 | tf_op jit(solution)/shard_map/ppermute | solution.py:74
  74.5 1.9 pad_maximum_fusion
  76.4 33.7 %collective-permute-done.8.refs_2_ = bf16[8,64,2048]{2,1,0:T(8,128)(2,1)} collective-permute-done((bf16[8,64,2048]{2,1,0:T(8,128)(2,1)S(1)}, bf16[8,64,2048]{2,1,0:T(8,128)(2,1)}, u32[]{:S(2)}, u32[]{:S(2)}) %collective-permute-start.8) | collective-permute-done | bytes 2097184 | tf_op jit(solution)/shard_map/ppermute | solution.py:74
  110.4 1.7 copy-done.12
  112.1 9.2 %all-to-all-start.2 = ((bf16[32,6,64,128]{3,2,1,0:T(8,128)(2,1)}), bf16[32,6,64,128]{3,2,1,0:T(8,128)(2,1)S(1)}, u32[]{:S(2)}, u32[]{:S(2)}) async-start(bf16[32,6,64,128]{3,2,1,0:T(8,128)(2,1)} %pad_maximum_fusion), calls=%async_computation.2 | async-start | bytes 6291456 | tf_op jit(solution)/shard_map/all_to_all | solution.py:238
  121.3 0.7 slice.58
  122.7 0.5 constant_dynamic-slice_fusion
  125.0 1.7 slice.80
  127.2 1.3 slice.75
  128.5 1.3 slice.74
  129.8 1.0 collective-permute-start.12
  130.8 0.6 collective-permute-start.13
  131.3 1.5 slice.69
  132.9 2.3 %fusion.5 = f32[4,3,128,128]{3,2,1,0:T(8,128)S(1)} fusion(bf16[8,4,4,64,128]{4,3,0,2,1:T(8,128)(2,1)} %collective-permute-done.6, f32[8,64]{1,0:T(8,128)S(1)} %convert_reduce_fusion, bf16[8,4,4,64,128]{4,3,0,2,1:T(8,128)(2,1)S(1)} %bitcast.67), kind=kOutput, calls=%fused_computation.14 | convolution fusion | flops 203685888 | bytes 3936256 | tf_op jit(solution)/shard_map/sabgp,sabgq->abpq/dot_general | solution.py:211
  135.2 1.3 fusion.8
  136.5 0.6 copy-done.13
  137.0 2.9 %copy.19 = bf16[32,64,6,128]{3,2,1,0:T(8,128)(2,1)S(1)} copy(bf16[32,64,6,128]{3,1,2,0:T(8,128)(2,1)S(1)} %bitcast.63) | data formatting | bytes 6291456 | tf_op jit(solution)/shard_map/transpose | solution.py:274
  140.0 0.8 copy.28
  140.8 0.5 fusion.12
  141.5 0.8 fusion.16
  142.4 2.5 %collective-permute-start.11 = (f32[2,3,64,128]{3,2,1,0:T(8,128)}, f32[2,3,64,128]{3,2,1,0:T(8,128)}, u32[]{:S(2)}, u32[]{:S(2)}) collective-permute-start(f32[2,3,64,128]{3,2,1,0:T(8,128)} %get-tuple-element.33), channel_id=1, source_target_pairs={{0,24},{1,25},{2,26},{3,27},{4,28},{5,29},{6,30},{7,31},{8,0},{9,1... | collective-permute-start | bytes 589832 | tf_op jit(solution)/shard_map/ppermute | solution.py:74
  144.8 1.7 collective-permute-start.10
  146.5 7.5 %shard_map.64.refs_0_ = bf16[1536,768]{1,0:T(8,128)(2,1)S(1)} custom-call(bf16[8,64,2048]{2,1,0:T(8,128)(2,1)S(1)} %copy-done.10, bf16[8,64,2048]{2,1,0:T(8,128)(2,1)} %collective-permute-done.7.refs_1_, bf16[8,64,2048]{2,1,0:T(8,128)(2,1)} %collective-permute-done.8.refs_2_, bf16[2048,768]{1,0:T(8,128)(2,1)S(1)} %bitcast.60), custom_call_target="tpu_custom_call" | custom-call | flops 4831838208 | bytes 11796480 | tf_op jit(solution)/shard_map/pallas_call | solution.py:93
  154.0 1.4 copy-done.4
  155.4 14.2 %collective-permute-done.12.refs_0_ = bf16[4,64,2048]{2,1,0:T(8,128)(2,1)S(1)} collective-permute-done((bf16[4,64,2048]{2,1,0:T(8,128)(2,1)S(1)}, bf16[4,64,2048]{2,1,0:T(8,128)(2,1)S(1)}, u32[]{:S(2)}, u32[]{:S(2)}) %collective-permute-start.12) | collective-permute-done | bytes 1048608 | tf_op jit(solution)/shard_map/ppermute | solution.py:74
  169.7 2.4 %collective-permute-done.13.refs_1_ = bf16[4,64,2048]{2,1,0:T(8,128)(2,1)S(1)} collective-permute-done((bf16[4,64,2048]{2,1,0:T(8,128)(2,1)S(1)}, bf16[4,64,2048]{2,1,0:T(8,128)(2,1)S(1)}, u32[]{:S(2)}, u32[]{:S(2)}) %collective-permute-start.13) | collective-permute-done | bytes 1048608 | tf_op jit(solution)/shard_map/ppermute | solution.py:74
  172.0 1.8 shard_map.65.refs_1_
  173.9 0.9 copy-done.6
  174.7 1.7 copy-done.5
  176.4 1.1 copy-done.7
  177.5 1.2 shard_map.67
  179.2 6.2 %collective-permute-start.14 = (f32[3,64,128]{2,1,0:T(8,128)S(1)}, f32[3,64,128]{2,1,0:T(8,128)S(1)}, u32[]{:S(2)}, u32[]{:S(2)}) collective-permute-start(f32[3,64,128]{2,1,0:T(8,128)S(1)} %shard_map.67), channel_id=1, source_target_pairs={{0,32},{1,33},{2,34},{3,35},{4,36},{5,37},{6,38},{7,39},{8,40},{9,... | collective-permute-start | bytes 294920 | tf_op jit(solution)/shard_map/ppermute | solution.py:74
  185.4 1.9 copy-done.3
  187.3 1.2 shard_map.66.mine_ref
  188.5 0.6 copy-done.8
  189.2 0.6 copy-done.25
  189.8 2.9 %shard_map.68 = f32[2,3,64,128]{3,2,1,0:T(8,128)} custom-call(s32[4]{0:T(128)} %copy-done.11, f32[2,3,64,128]{3,2,1,0:T(8,128)} %get-tuple-element.34.exch_0, f32[2,3,64,128]{3,2,1,0:T(8,128)} %collective-permute-done.9.exch_1, f32[2,3,64,128]{3,2,1,0:T(8,128)} %collective-permute-done.10.exch_2, f32[2,3,64,128]{3,2,1,0:T(8,128)} %collective-permute-done.11.exch_3, ...), custom_call_target="tpu_custom_call" | custom-call | tf_op jit(solution)/shard_map/pallas_call | solution.py:175
  (70 shorter events, 2.8 us)
Async XLA Ops:
  0.0 1.0 copy-start
  1.0 4.4 %copy-start.19 = (bf16[96,64,128]{2,1,0:T(8,128)(2,1)S(1)}, bf16[96,64,128]{2,1,0:T(8,128)(2,1)}, u32[]{:S(2)}) copy-start(bf16[96,64,128]{2,1,0:T(8,128)(2,1)} %param.6) | copy-start | bytes 4718596
  1.1 7.6 %collective-permute-start = (bf16[1,64,2048]{2,1,0:T(8,128)(2,1)S(1)}, bf16[1,64,2048]{2,1,0:T(8,128)(2,1)S(1)}, u32[]{:S(2)}, u32[]{:S(2)}) collective-permute-start(bf16[1,64,2048]{2,1,0:T(8,128)(2,1)S(1)} %constant_dynamic-slice_fusion.3), channel_id=1, source_target_pairs={{0,4},{1,5},{2,6},{3,7},{4,0},{5,1},{6,2},{7,3},{8,12},{9,13},{10,... | collective-permute-start | bytes 786440 | tf_op jit(solution)/shard_map/ppermute | solution.py:74
  8.7 13.7 %copy-start.20 = (bf16[2,64,2048]{2,1,0:T(8,128)(2,1)}, bf16[2,64,2048]{2,1,0:T(8,128)(2,1)S(1)}, u32[]{:S(2)}) copy-start(bf16[2,64,2048]{2,1,0:T(8,128)(2,1)S(1)} %pad_maximum_fusion.4) | copy-start | bytes 1572868
  8.8 31.8 %all-to-all-start = ((bf16[8,17,64,128]{3,2,1,0:T(8,128)(2,1)}), bf16[8,17,64,128]{3,2,1,0:T(8,128)(2,1)S(1)}, u32[]{:S(2)}, u32[]{:S(2)}) async-start(bf16[8,17,64,128]{3,2,1,0:T(8,128)(2,1)} %pad_maximum_fusion.2), calls=%async_computation | async-start | bytes 4456448 | tf_op jit(solution)/shard_map/all_to_all | solution.py:238
  16.6 6.6 %collective-permute-start.2 = (bf16[96,64,128]{2,1,0:T(8,128)(2,1)S(1)}, bf16[96,64,128]{2,1,0:T(8,128)(2,1)S(1)}, u32[]{:S(2)}, u32[]{:S(2)}) collective-permute-start(bf16[96,64,128]{2,1,0:T(8,128)(2,1)S(1)} %get-tuple-element.28), channel_id=1, source_target_pairs={{0,32},{1,33},{2,34},{3,35},{4,36},{5,37},{6,38},{7,39},{8,40},{9,... | collective-permute-start | bytes 4718600 | tf_op jit(solution)/shard_map/ppermute | solution.py:74
  18.8 9.6 %collective-permute-start.5 = (bf16[2,64,2048]{2,1,0:T(8,128)(2,1)S(1)}, bf16[2,64,2048]{2,1,0:T(8,128)(2,1)S(1)}, u32[]{:S(2)}, u32[]{:S(2)}) collective-permute-start(bf16[2,64,2048]{2,1,0:T(8,128)(2,1)S(1)} %pad_maximum_fusion.4), channel_id=1, source_target_pairs={{0,2},{1,3},{2,0},{3,1},{4,6},{5,7},{6,4},{7,5},{8,10},{9,11},{10,... | collective-permute-start | bytes 1572872 | tf_op jit(solution)/shard_map/ppermute | solution.py:74
  21.7 12.9 %collective-permute-start.4 = (bf16[2,64,2048]{2,1,0:T(8,128)(2,1)S(1)}, bf16[2,64,2048]{2,1,0:T(8,128)(2,1)S(1)}, u32[]{:S(2)}, u32[]{:S(2)}) collective-permute-start(bf16[2,64,2048]{2,1,0:T(8,128)(2,1)S(1)} %pad_maximum_fusion.4), channel_id=1, source_target_pairs={{0,3},{1,0},{2,1},{3,2},{4,7},{5,4},{6,5},{7,6},{8,11},{9,8},{10,9... | collective-permute-start | bytes 1572872 | tf_op jit(solution)/shard_map/ppermute | solution.py:74
  22.4 13.0 %collective-permute-start.3 = (bf16[2,64,2048]{2,1,0:T(8,128)(2,1)S(1)}, bf16[2,64,2048]{2,1,0:T(8,128)(2,1)}, u32[]{:S(2)}, u32[]{:S(2)}) collective-permute-start(bf16[2,64,2048]{2,1,0:T(8,128)(2,1)S(1)} %pad_maximum_fusion.4), channel_id=1, source_target_pairs={{0,1},{1,2},{2,3},{3,0},{4,5},{5,6},{6,7},{7,4},{8,9},{9,10},{10,1... | collective-permute-start | bytes 1572872 | tf_op jit(solution)/shard_map/ppermute | solution.py:74
  28.4 6.2 %copy-start.21 = (bf16[2,64,2048]{2,1,0:T(8,128)(2,1)}, bf16[2,64,2048]{2,1,0:T(8,128)(2,1)S(1)}, u32[]{:S(2)}) copy-start(bf16[2,64,2048]{2,1,0:T(8,128)(2,1)S(1)} %collective-permute-done.5) | copy-start | bytes 1572868
  34.6 0.8 copy-start.23
  40.5 1.4 copy-start.14
  41.9 68.5 %all-to-all-start.1 = ((bf16[32,6,64,128]{3,2,1,0:T(8,128)(2,1)}), bf16[32,6,64,128]{3,2,1,0:T(8,128)(2,1)S(1)}, u32[]{:S(2)}, u32[]{:S(2)}) async-start(bf16[32,6,64,128]{3,2,1,0:T(8,128)(2,1)} %pad_maximum_fusion.1), calls=%async_computation.1 | async-start | bytes 6291456 | tf_op jit(solution)/shard_map/all_to_all | solution.py:238
  49.2 2.3 %copy-start.24 = (bf16[2,64,2048]{2,1,0:T(8,128)(2,1)S(1)}, bf16[2,64,2048]{2,1,0:T(8,128)(2,1)}, u32[]{:S(2)}) copy-start(bf16[2,64,2048]{2,1,0:T(8,128)(2,1)} %copy-done.23) | copy-start | bytes 1572868
  49.2 2.3 %copy-start.22 = (bf16[2,64,2048]{2,1,0:T(8,128)(2,1)S(1)}, bf16[2,64,2048]{2,1,0:T(8,128)(2,1)}, u32[]{:S(2)}) copy-start(bf16[2,64,2048]{2,1,0:T(8,128)(2,1)} %copy-done.21) | copy-start | bytes 1572868
  51.6 1.6 copy-start.9
  51.6 2.3 %slice-start = ((bf16[8,17,64,128]{3,2,1,0:T(8,128)(2,1)}), bf16[8,16,64,128]{3,2,1,0:T(8,128)(2,1)S(1)}, s32[]{:S(2)}) async-start(bf16[8,17,64,128]{3,2,1,0:T(8,128)(2,1)} %copy-done.14), calls=%async_computation.3 | async-start | bytes 4194304 | tf_op jit(solution)/shard_map/slice | solution.py:266
  51.6 58.5 %collective-permute-start.8 = (bf16[8,64,2048]{2,1,0:T(8,128)(2,1)S(1)}, bf16[8,64,2048]{2,1,0:T(8,128)(2,1)}, u32[]{:S(2)}, u32[]{:S(2)}) collective-permute-start(bf16[8,64,2048]{2,1,0:T(8,128)(2,1)S(1)} %constant_dynamic-update-slice_fusion.refs_0_), channel_id=1, source_target_pairs={{0,24},{1,25},{2,26},{3,27},{4,28},{5,29},{6,30},{7,31},{8,0},{9,1... | collective-permute-start | bytes 6291464 | tf_op jit(solution)/shard_map/ppermute | solution.py:74
  52.0 58.1 %collective-permute-start.7 = (bf16[8,64,2048]{2,1,0:T(8,128)(2,1)S(1)}, bf16[8,64,2048]{2,1,0:T(8,128)(2,1)}, u32[]{:S(2)}, u32[]{:S(2)}) collective-permute-start(bf16[8,64,2048]{2,1,0:T(8,128)(2,1)S(1)} %constant_dynamic-update-slice_fusion.refs_0_), channel_id=1, source_target_pairs={{0,8},{1,9},{2,10},{3,11},{4,12},{5,13},{6,14},{7,15},{8,16},{9,17... | collective-permute-start | bytes 6291464 | tf_op jit(solution)/shard_map/ppermute | solution.py:74
  54.0 14.3 %copy-start.18 = (bf16[2,96,64,128]{3,2,1,0:T(8,128)(2,1)S(1)}, bf16[2,96,64,128]{3,2,1,0:T(8,128)(2,1)}, u32[]{:S(2)}) copy-start(bf16[2,96,64,128]{3,2,1,0:T(8,128)(2,1)} %param.8) | copy-start | bytes 9437188
  54.2 14.8 %copy-start.16 = (bf16[8,16,64,128]{3,2,0,1:T(8,128)(2,1)}, bf16[8,16,64,128]{3,2,0,1:T(8,128)(2,1)S(1)}, u32[]{:S(2)}) copy-start(bf16[8,16,64,128]{3,2,0,1:T(8,128)(2,1)S(1)} %copy.18) | copy-start | bytes 6291460
  54.2 56.2 %collective-permute-start.6 = (bf16[8,4,4,64,128]{4,3,0,2,1:T(8,128)(2,1)S(1)}, bf16[8,4,4,64,128]{4,3,0,2,1:T(8,128)(2,1)}, u32[]{:S(2)}, u32[]{:S(2)}) collective-permute-start(bf16[8,4,4,64,128]{4,3,0,2,1:T(8,128)(2,1)S(1)} %bitcast.65), channel_id=1, source_target_pairs={{0,96},{1,97},{2,98},{3,99},{4,100},{5,101},{6,102},{7,103},{8,104... | collective-permute-start | bytes 6291464 | tf_op jit(solution)/shard_map/ppermute | solution.py:74
  69.0 5.4 %collective-permute-start.1 = (bf16[96,64,128]{2,1,0:T(8,128)(2,1)S(1)}, bf16[96,64,128]{2,1,0:T(8,128)(2,1)S(1)}, u32[]{:S(2)}, u32[]{:S(2)}) collective-permute-start(bf16[96,64,128]{2,1,0:T(8,128)(2,1)S(1)} %get-tuple-element.30), channel_id=1, source_target_pairs={{0,32},{1,33},{2,34},{3,35},{4,36},{5,37},{6,38},{7,39},{8,40},{9,... | collective-permute-start | bytes 4718600 | tf_op jit(solution)/shard_map/ppermute | solution.py:74
  76.4 45.0 %copy-start.26 = (s32[2,2]{1,0:T(2,128)S(1)}, s32[2,2]{1,0:T(2,128)}, u32[]{:S(2)}) copy-start(s32[2,2]{1,0:T(2,128)} %param.11) | copy-start | bytes 52
  110.4 1.7 copy-start.12
  112.1 62.7 %all-to-all-start.2 = ((bf16[32,6,64,128]{3,2,1,0:T(8,128)(2,1)}), bf16[32,6,64,128]{3,2,1,0:T(8,128)(2,1)S(1)}, u32[]{:S(2)}, u32[]{:S(2)}) async-start(bf16[32,6,64,128]{3,2,1,0:T(8,128)(2,1)} %pad_maximum_fusion), calls=%async_computation.2 | async-start | bytes 6291456 | tf_op jit(solution)/shard_map/all_to_all | solution.py:238
  125.0 2.1 %copy-start.15 = (bf16[8,17,64,128]{3,2,1,0:T(8,128)(2,1)S(1)}, bf16[8,17,64,128]{3,2,1,0:T(8,128)(2,1)}, u32[]{:S(2)}) copy-start(bf16[8,17,64,128]{3,2,1,0:T(8,128)(2,1)} %copy-done.14) | copy-start | bytes 6684676
  125.0 60.3 %copy-start.11 = (s32[4]{0:T(128)}, s32[4]{0:T(128)S(1)}, u32[]{:S(2)}) copy-start(s32[4]{0:T(128)S(1)} %pad_add_fusion.pos_ref) | copy-start | bytes 52
  129.8 3.1 %copy-start.17 = (bf16[8,16,64,128]{3,2,0,1:T(8,128)(2,1)S(1)}, bf16[8,16,64,128]{3,2,0,1:T(8,128)(2,1)}, u32[]{:S(2)}) copy-start(bf16[8,16,64,128]{3,2,0,1:T(8,128)(2,1)} %copy-done.16) | copy-start | bytes 6291460
  129.8 39.9 %collective-permute-start.12 = (bf16[4,64,2048]{2,1,0:T(8,128)(2,1)S(1)}, bf16[4,64,2048]{2,1,0:T(8,128)(2,1)S(1)}, u32[]{:S(2)}, u32[]{:S(2)}) collective-permute-start(bf16[4,64,2048]{2,1,0:T(8,128)(2,1)S(1)} %slice.74), channel_id=1, source_target_pairs={{0,8},{1,9},{2,10},{3,11},{4,12},{5,13},{6,14},{7,15},{8,16},{9,17... | collective-permute-start | bytes 3145736 | tf_op jit(solution)/shard_map/ppermute | solution.py:74
  130.8 41.3 %collective-permute-start.13 = (bf16[4,64,2048]{2,1,0:T(8,128)(2,1)S(1)}, bf16[4,64,2048]{2,1,0:T(8,128)(2,1)S(1)}, u32[]{:S(2)}, u32[]{:S(2)}) collective-permute-start(bf16[4,64,2048]{2,1,0:T(8,128)(2,1)S(1)} %slice.75), channel_id=1, source_target_pairs={{0,24},{1,25},{2,26},{3,27},{4,28},{5,29},{6,30},{7,31},{8,0},{9,1... | collective-permute-start | bytes 3145736 | tf_op jit(solution)/shard_map/ppermute | solution.py:74
  135.2 1.9 copy-start.13
  141.2 5.3 %copy-start.10 = (bf16[8,64,2048]{2,1,0:T(8,128)(2,1)S(1)}, bf16[8,64,2048]{2,1,0:T(8,128)(2,1)}, u32[]{:S(2)}) copy-start(bf16[8,64,2048]{2,1,0:T(8,128)(2,1)} %copy-done.9) | copy-start | bytes 6291460
  142.4 46.8 %collective-permute-start.11 = (f32[2,3,64,128]{3,2,1,0:T(8,128)}, f32[2,3,64,128]{3,2,1,0:T(8,128)}, u32[]{:S(2)}, u32[]{:S(2)}) collective-permute-start(f32[2,3,64,128]{3,2,1,0:T(8,128)} %get-tuple-element.33), channel_id=1, source_target_pairs={{0,24},{1,25},{2,26},{3,27},{4,28},{5,29},{6,30},{7,31},{8,0},{9,1... | collective-permute-start | bytes 589832 | tf_op jit(solution)/shard_map/ppermute | solution.py:74
  144.8 44.3 %collective-permute-start.9 = (f32[2,3,64,128]{3,2,1,0:T(8,128)S(1)}, f32[2,3,64,128]{3,2,1,0:T(8,128)}, u32[]{:S(2)}, u32[]{:S(2)}) collective-permute-start(f32[2,3,64,128]{3,2,1,0:T(8,128)S(1)} %get-tuple-element.35), channel_id=1, source_target_pairs={{0,8},{1,9},{2,10},{3,11},{4,12},{5,13},{6,14},{7,15},{8,16},{9,17... | collective-permute-start | bytes 589832 | tf_op jit(solution)/shard_map/ppermute | solution.py:74
  144.8 44.3 %collective-permute-start.10 = (f32[2,3,64,128]{3,2,1,0:T(8,128)S(1)}, f32[2,3,64,128]{3,2,1,0:T(8,128)}, u32[]{:S(2)}, u32[]{:S(2)}) collective-permute-start(f32[2,3,64,128]{3,2,1,0:T(8,128)S(1)} %get-tuple-element.36), channel_id=1, source_target_pairs={{0,16},{1,17},{2,18},{3,19},{4,20},{5,21},{6,22},{7,23},{8,24},{9,... | collective-permute-start | bytes 589832 | tf_op jit(solution)/shard_map/ppermute | solution.py:74
  154.0 1.4 copy-start.4
  173.9 0.9 copy-start.6
  174.7 1.7 copy-start.5
  176.4 1.1 copy-start.7
  177.5 1.6 copy-start.2
  179.2 10.0 %collective-permute-start.14 = (f32[3,64,128]{2,1,0:T(8,128)S(1)}, f32[3,64,128]{2,1,0:T(8,128)S(1)}, u32[]{:S(2)}, u32[]{:S(2)}) collective-permute-start(f32[3,64,128]{2,1,0:T(8,128)S(1)} %shard_map.67), channel_id=1, source_target_pairs={{0,32},{1,33},{2,34},{3,35},{4,36},{5,37},{6,38},{7,39},{8,40},{9,... | collective-permute-start | bytes 294920 | tf_op jit(solution)/shard_map/ppermute | solution.py:74
  185.4 1.9 copy-start.3
  187.3 5.4 %copy-start.1 = (bf16[2,64,2048]{2,1,0:T(8,128)(2,1)S(1)}, bf16[2,64,2048]{2,1,0:T(8,128)(2,1)}, u32[]{:S(2)}) copy-start(bf16[2,64,2048]{2,1,0:T(8,128)(2,1)} %param.10) | copy-start | bytes 1572868
  188.5 0.6 copy-start.8
  189.1 0.6 copy-start.25

commit v4 on v3

--- a/solution.py
+++ b/solution.py
@@ -81,9 +81,9 @@
         blocks, depth, width = rows_ref.shape
         for block in range(0, blocks, 4):
             rows = rows_ref[block : block + 4].reshape(4 * depth, width)
-            out_ref[first : first + 4 * depth] = jnp.dot(
-                rows, valence_ref[...], preferred_element_type=jnp.float32
-            ).astype(jnp.bfloat16)
+            image = jnp.dot(rows, valence_ref[...], preferred_element_type=jnp.float32).astype(jnp.bfloat16)
+            for k in range(6):
+                out_ref[k, first : first + 4 * depth] = image[:, k * 128 : (k + 1) * 128]
             first += 4 * depth
 
 
@@ -92,10 +92,10 @@
     count = sum(part.shape[0] * part.shape[1] for part in parts)
     return pl.pallas_call(
         image_kernel,
-        out_shape=jax.ShapeDtypeStruct((count, valence.shape[1]), jnp.bfloat16),
+        out_shape=jax.ShapeDtypeStruct((6, count, 128), jnp.bfloat16),
         in_specs=[vmem] * (len(parts) + 1),
         out_specs=vmem,
-        compiler_params=pltpu.CompilerParams(vmem_limit_bytes=28 * 1024 * 1024),
+        compiler_params=pltpu.CompilerParams(vmem_limit_bytes=18 * 1024 * 1024),
         cost_estimate=pl.CostEstimate(
             flops=2 * count * valence.shape[0] * valence.shape[1],
             bytes_accessed=2 * (count * 2048 + valence.size + count * valence.shape[1]),
@@ -104,11 +104,31 @@
     )(*parts, valence)
 
 
-def direct_kernel(from_k, pos_ref, *refs):
-    parts, conduction_ref, out_ref = refs[:-2], refs[-2], refs[-1]
+def traded(block, row_step, lane_step):
+    row_bit = (lax.broadcasted_iota(jnp.int32, (64, 128), 0) & row_step) != 0
+    lane_bit = (lax.broadcasted_iota(jnp.int32, (64, 128), 1) & lane_step) != 0
+    up = pltpu.roll(pltpu.roll(block, 64 - row_step, 0), lane_step, 1)
+    down = pltpu.roll(pltpu.roll(block, row_step, 0), 128 - lane_step, 1)
+    return jnp.where(row_bit == lane_bit, block, jnp.where(row_bit, down, up))
+
+
+def direct_kernel(pos_ref, near_ref, far_ref, conduction_ref, theirs_ref, mine_ref, image, right, sems):
     x, y, z_lo, core = pos_ref[0], pos_ref[1], pos_ref[2], pos_ref[3]
     along_a = jnp.where(core == 0, x, y)
     along_b = jnp.where(core == 0, y, x)
+    split = near_ref.shape[1]
+    order = (3, 4, 5, 0, 1, 2)
+
+    def copies(k):
+        return (
+            pltpu.make_async_copy(near_ref.at[k], image.at[k, pl.ds(0, split)], sems.at[k, 0]),
+            pltpu.make_async_copy(far_ref.at[k], image.at[k, pl.ds(split, 2048 - split)], sems.at[k, 1]),
+            pltpu.make_async_copy(conduction_ref.at[:, k], right.at[k], sems.at[k, 2]),
+        )
+
+    for k in order:
+        for copy in copies(k):
+            copy.start()
     places = []
     for step in B_STEPS:
         b_now = lax.rem(along_b + (step + 4), 4)
@@ -119,65 +139,60 @@
             y_now = jnp.where(core == 0, b_now, a_now)
             places.append(y_now * 8 + z_now * 4 + x_now)
     lane = lax.broadcasted_iota(jnp.int32, (64, 128), 1)
-    for k in range(out_ref.shape[0]):
-        columns = pl.ds((from_k + k) * 128, 128)
-        full = jnp.zeros((128, 128), jnp.float32)
-        first = 0
-        for part in parts:
-            blocks = part.shape[0] // 64
-            right = jnp.concatenate(
-                [conduction_ref[place, from_k + k] for place in places[first : first + blocks]], axis=0
+    for k in order:
+        for copy in copies(k):
+            copy.wait()
+        gathered = jnp.concatenate([right[k, place] for place in places], axis=0)
+        full = lax.dot_general(
+            image[k], gathered, (((0,), (0,)), ((), ())), preferred_element_type=jnp.float32
+        )
+        turned = pltpu.roll(full[64:], 64, 1)
+        block = jnp.where(lane < 64, turned + full[:64], turned - full[:64])
+        for row_step, lane_step in ((1, 8), (2, 16), (4, 32), (1, 64)):
+            block = traded(block, row_step, lane_step)
+        if k < 3:
+            mine_ref[k] = block
+        else:
+            theirs_ref[k - 3] = block
+
+
+def direct_of(pos, images, conduction):
+    vmem = pl.BlockSpec(memory_space=pltpu.VMEM)
+    shape = jax.ShapeDtypeStruct((3, 64, 128), jnp.float32)
+    return pl.pallas_call(
+        direct_kernel,
+        out_shape=(shape, shape),
+        in_specs=[pl.BlockSpec(memory_space=pltpu.SMEM)] + [pl.BlockSpec(memory_space=pl.ANY)] * 3,
+        out_specs=(vmem, vmem),
+        scratch_shapes=[
+            pltpu.VMEM((6, 2048, 128), jnp.bfloat16),
+            pltpu.VMEM((6, 32, 64, 128), jnp.bfloat16),
+            pltpu.SemaphoreType.DMA((6, 3)),
+        ],
+        compiler_params=pltpu.CompilerParams(vmem_limit_bytes=60 * 1024 * 1024),
+        cost_estimate=pl.CostEstimate(
+            flops=2 * 6 * 2048 * 128 * 128, bytes_accessed=7 * 1024 * 1024, transcendentals=0
+        ),
+    )(pos, *images, conduction)
+
+
+def exchange_kernel(first_ref, second_ref, third_ref, fourth_ref, out_ref):
+    for offset in range(NOFF):
+        for k in range(3):
+            total = (first_ref[offset, k] + second_ref[offset, k]) + (
+                third_ref[offset, k] + fourth_ref[offset, k]
             )
-            first += blocks
-            full += lax.dot_general(
-                part[:, columns], right, (((0,), (0,)), ((), ())), preferred_element_type=jnp.float32
-            )
-        turned = pltpu.roll(full[64:], 64, 1)
-        out_ref[k] = jnp.where(lane < 64, turned + full[:64], turned - full[:64])
-
-
-def direct_of(from_k, pos, images, conduction):
+            out_ref[offset, k] = traded(2.0 * total, 1, 64)
+
+
+def exchange_of(pieces):
     vmem = pl.BlockSpec(memory_space=pltpu.VMEM)
     return pl.pallas_call(
-        functools.partial(direct_kernel, from_k),
-        out_shape=jax.ShapeDtypeStruct((3, 64, 128), jnp.float32),
-        in_specs=[pl.BlockSpec(memory_space=pltpu.SMEM)] + [vmem] * (len(images) + 1),
+        exchange_kernel,
+        out_shape=jax.ShapeDtypeStruct((NOFF, 3, 64, 128), jnp.float32),
+        in_specs=[vmem] * 4,
         out_specs=vmem,
-        compiler_params=pltpu.CompilerParams(vmem_limit_bytes=20 * 1024 * 1024),
-        cost_estimate=pl.CostEstimate(
-            flops=2 * 3 * 2048 * 128 * 128, bytes_accessed=6 * 1024 * 1024, transcendentals=0
-        ),
-    )(pos, *images, conduction)
-
-
-def final_kernel(pos_ref, exch_0, exch_1, exch_2, exch_3, mine_ref, theirs_ref, out_ref):
-    core = pos_ref[3]
-    lane = lax.broadcasted_iota(jnp.int32, (64, 128), 1)
-    row = lax.broadcasted_iota(jnp.int32, (64, 128), 0)
-
-    def exchanged(block, row_step, lane_step):
-        row_bit = (row & row_step) != 0
-        lane_bit = (lane & lane_step) != 0
-        up = pltpu.roll(pltpu.roll(block, 64 - row_step, 0), lane_step, 1)
-        down = pltpu.roll(pltpu.roll(block, row_step, 0), 128 - lane_step, 1)
-        return jnp.where(row_bit == lane_bit, block, jnp.where(row_bit, down, up))
-
-    for k in range(3):
-        for offset, block in ((core, mine_ref[k]), (1 - core, theirs_ref[k])):
-            for step in (1, 2, 4):
-                block = exchanged(block, step, 8 * step)
-            exch = (exch_0[offset, k] + exch_1[offset, k]) + (exch_2[offset, k] + exch_3[offset, k])
-            out_ref[offset, k] = exchanged(2.0 * exch - block, 1, 64)
-
-
-def finish(pos, exch, mine, theirs):
-    vmem = pl.BlockSpec(memory_space=pltpu.VMEM)
-    return pl.pallas_call(
-        final_kernel,
-        out_shape=jax.ShapeDtypeStruct((NOFF, 3, 64, 128), jnp.float32),
-        in_specs=[pl.BlockSpec(memory_space=pltpu.SMEM)] + [vmem] * 6,
-        out_specs=vmem,
-    )(pos, *exch, mine, theirs)
+    )(*pieces)
 
 
 def three_pieces(values):
@@ -275,9 +290,10 @@
     images = [image_of((rows, behind, ahead), valence), image_of((far_low, far_high), valence)]
     exch = exchange_sums(here, next_rows, near_coulomb, offsets, y)
 
-    theirs = send(direct_of(3, pos, images, conduction), other_core())
-    mine = direct_of(0, pos, images, conduction)
-    out = finish(pos, exch, mine, theirs).reshape(NOFF, 3, 32, 2, 128)
+    theirs, mine = direct_of(pos, images, conduction)
+    theirs = send(theirs, other_core())
+    direct = jnp.where((jnp.arange(NOFF) == core)[:, None, None, None], mine[None], theirs[None])
+    out = (exchange_of(exch) - direct).reshape(NOFF, 3, 32, 2, 128)
     return jnp.transpose(out, (0, 3, 1, 2, 4)).reshape(NOFF, 2, 3, 4096)
 
 

time: 194 us -> 192 us (0.990)
  local copies, waits for them, and re-layouts: 33.9 us -> 23.8 us
  starting transfers between devices: 59.9 us -> 64 us
  Pallas kernels: 14.7 us -> 17.9 us
  other arithmetic: 8.2 us -> 11.3 us
  waiting for transfers between devices: 69.6 us -> 67.4 us
    unnamed x61 -> x35, local copies, waits for them, and re-layouts: 17.7 us -> 6.24 us
    ppermute x15, starting transfers between devices: 38.2 us -> 42.1 us  [send(): return lax.ppermute(array, AXES, pairs)]
    pallas_call x5 -> x4, Pallas kernels: 14.7 us -> 17.9 us  [the longest x2 8.67 us: image_of(): pl.pallas_call(image_kernel, out_shape=jax.ShapeDtypeStruct((6, count, 12...]
    ppermute x15, waiting for transfers between devices: 64.5 us -> 61.6 us  [send(): return lax.ppermute(array, AXES, pairs)]
  transfers between devices with their start and end apart: 18 -> 18, of which waited for: 9 -> 9; matrix products, arithmetic and copies ran while one was open for 16% -> 17% of each run, Pallas kernels for 6% -> 9%
where the time goes in v4:
time: 192 us; the launch traced here: 191 us
  waiting for transfers between devices  67.4 us (35%)
  starting transfers between devices  64 us (33%)
  local copies, waits for them, and re-layouts  23.8 us (12%)
  Pallas kernels  17.9 us (9%)
  other arithmetic  11.3 us (6%)
  matrix products  3.57 us (2%)
  between operations  2.99 us (2%)
    ppermute x15, waiting for transfers between devices, send(): return lax.ppermute(array, AXES, pairs)  61.6 us
    ppermute x15, starting transfers between devices, send(): return lax.ppermute(array, AXES, pairs)  42.1 us
    all_to_all x3, starting transfers between devices, spread(): lax.all_to_all(packed, 'ga', split_axis=0, concat_axis=0, tiled=True, axi...  21.9 us
    pallas_call x2, Pallas kernels, image_of(): pl.pallas_call(image_kernel, out_shape=jax.ShapeDtypeStruct((6, count, 12...  8.67 us
    pallas_call x1, Pallas kernels, direct_of(): pl.pallas_call(direct_kernel, out_shape=(shape, shape), in_specs=[pl.Bloc...  7.15 us
    unnamed x35, local copies, waits for them, and re-layouts  6.24 us
    all_to_all x3, waiting for transfers between devices, spread(): lax.all_to_all(packed, 'ga', split_axis=0, concat_axis=0, tiled=True, axi...  5.82 us
    transpose x1, local copies, waits for them, and re-layouts, local(): valence = jnp.transpose(valence, (0, 2, 1, 3)).reshape(2048, 768)  4.81 us
  transfers between devices with their start and end apart: 18, of which 9 were waited for; matrix products, arithmetic and copies ran while one was open for 17% of the time, Pallas kernels for 9%

profile of v4, /device:TPU:5, one launch (start us, length us, event | category | flops | bytes accessed | tf_op | source)
XLA Modules:
  0.0 191.0 jit_solution(11951971384379269255)
XLA Ops:
  0.0 1.0 copy-done
  1.1 1.7 collective-permute-start
  2.8 0.8 slice.76
  3.6 1.1 slice.77
  4.7 0.7 fusion.24
  5.4 0.2 pad_maximum_fusion.3
  5.6 0.1 copy.23
  5.8 1.6 pad_maximum_fusion.2
  7.4 1.3 collective-permute-done
  8.7 5.2 %all-to-all-start = ((bf16[8,17,64,128]{3,2,1,0:T(8,128)(2,1)}), bf16[8,17,64,128]{3,2,1,0:T(8,128)(2,1)}, u32[]{:S(2)}, u32[]{:S(2)}) async-start(bf16[8,17,64,128]{3,2,1,0:T(8,128)(2,1)} %pad_maximum_fusion.2), calls=%async_computation | async-start | bytes 4456448 | tf_op jit(solution)/shard_map/all_to_all | solution.py:253
  14.0 2.6 %constant_dynamic-slice_fusion.1 = (bf16[1,96,64,128]{3,2,1,0:T(8,128)(2,1)S(1)}, bf16[96,64,128]{2,1,0:T(8,128)(2,1)S(1)}) fusion(bf16[2,96,64,128]{3,2,1,0:T(8,128)(2,1)} %param.9, s32[]{:T(128)S(6)} %select_n.75, s32[]{:T(128)S(6)} %select_n.76), kind=kLoop, calls=%fused_computation.53 | loop fusion | bytes 6291464 | tf_op jit(solution)/shard_map/jit(dynamic_index_in_dim)/dynamic_slice | solution.py:246
  16.6 2.2 %collective-permute-start.2 = (bf16[96,64,128]{2,1,0:T(8,128)(2,1)S(1)}, bf16[96,64,128]{2,1,0:T(8,128)(2,1)S(1)}, u32[]{:S(2)}, u32[]{:S(2)}) collective-permute-start(bf16[96,64,128]{2,1,0:T(8,128)(2,1)S(1)} %get-tuple-element.32), channel_id=1, source_target_pairs={{0,32},{1,33},{2,34},{3,35},{4,36},{5,37},{6,38},{7,39},{8,40},{9,... | collective-permute-start | bytes 4718600 | tf_op jit(solution)/shard_map/ppermute | solution.py:74
  18.7 2.9 %collective-permute-start.5 = (bf16[2,64,2048]{2,1,0:T(8,128)(2,1)S(1)}, bf16[2,64,2048]{2,1,0:T(8,128)(2,1)S(1)}, u32[]{:S(2)}, u32[]{:S(2)}) collective-permute-start(bf16[2,64,2048]{2,1,0:T(8,128)(2,1)S(1)} %pad_maximum_fusion.4), channel_id=1, source_target_pairs={{0,2},{1,3},{2,0},{3,1},{4,6},{5,7},{6,4},{7,5},{8,10},{9,11},{10,... | collective-permute-start | bytes 1572872 | tf_op jit(solution)/shard_map/ppermute | solution.py:74
  21.7 0.8 collective-permute-start.4
  22.4 0.7 collective-permute-start.3
  23.1 1.9 pad_maximum_fusion.1
  25.0 3.4 %collective-permute-done.5 = bf16[2,64,2048]{2,1,0:T(8,128)(2,1)S(1)} collective-permute-done((bf16[2,64,2048]{2,1,0:T(8,128)(2,1)S(1)}, bf16[2,64,2048]{2,1,0:T(8,128)(2,1)S(1)}, u32[]{:S(2)}, u32[]{:S(2)}) %collective-permute-start.5) | collective-permute-done | bytes 524320 | tf_op jit(solution)/shard_map/ppermute | solution.py:74
  28.4 6.3 %collective-permute-done.4 = bf16[2,64,2048]{2,1,0:T(8,128)(2,1)S(1)} collective-permute-done((bf16[2,64,2048]{2,1,0:T(8,128)(2,1)S(1)}, bf16[2,64,2048]{2,1,0:T(8,128)(2,1)S(1)}, u32[]{:S(2)}, u32[]{:S(2)}) %collective-permute-start.4) | collective-permute-done | bytes 524320 | tf_op jit(solution)/shard_map/ppermute | solution.py:74
  34.7 5.8 %all-to-all-done = bf16[8,17,64,128]{3,2,1,0:T(8,128)(2,1)} async-done(((bf16[8,17,64,128]{3,2,1,0:T(8,128)(2,1)}), bf16[8,17,64,128]{3,2,1,0:T(8,128)(2,1)}, u32[]{:S(2)}, u32[]{:S(2)}) %all-to-all-start) | async-done | bytes 2228256 | tf_op jit(solution)/shard_map/all_to_all | solution.py:253
  40.5 7.5 %all-to-all-start.1 = ((bf16[32,6,64,128]{3,2,1,0:T(8,128)(2,1)}), bf16[32,6,64,128]{3,2,1,0:T(8,128)(2,1)}, u32[]{:S(2)}, u32[]{:S(2)}) async-start(bf16[32,6,64,128]{3,2,1,0:T(8,128)(2,1)} %pad_maximum_fusion.1), calls=%async_computation.1 | async-start | bytes 6291456 | tf_op jit(solution)/shard_map/all_to_all | solution.py:253
  48.0 1.1 constant_dynamic-update-slice_fusion.2
  49.2 0.4 collective-permute-start.8
  49.5 1.2 collective-permute-start.7
  50.7 1.8 slice.79
  52.5 0.2 copy.18
  52.7 16.6 %collective-permute-start.6 = (bf16[8,4,4,64,128]{4,3,0,2,1:T(8,128)(2,1)S(1)}, bf16[8,4,4,64,128]{4,3,0,2,1:T(8,128)(2,1)}, u32[]{:S(2)}, u32[]{:S(2)}) collective-permute-start(bf16[8,4,4,64,128]{4,3,0,2,1:T(8,128)(2,1)S(1)} %bitcast.64), channel_id=1, source_target_pairs={{0,96},{1,97},{2,98},{3,99},{4,100},{5,101},{6,102},{7,103},{8,104... | collective-permute-start | bytes 6291464 | tf_op jit(solution)/shard_map/ppermute | solution.py:74
  69.3 0.7 constant_dynamic-slice_fusion.2
  70.0 2.4 %collective-permute-start.1 = (bf16[96,64,128]{2,1,0:T(8,128)(2,1)S(1)}, bf16[96,64,128]{2,1,0:T(8,128)(2,1)S(1)}, u32[]{:S(2)}, u32[]{:S(2)}) collective-permute-start(bf16[96,64,128]{2,1,0:T(8,128)(2,1)S(1)} %get-tuple-element.34), channel_id=1, source_target_pairs={{0,32},{1,33},{2,34},{3,35},{4,36},{5,37},{6,38},{7,39},{8,40},{9,... | collective-permute-start | bytes 4718600 | tf_op jit(solution)/shard_map/ppermute | solution.py:74
  72.4 3.0 %collective-permute-done.1 = bf16[96,64,128]{2,1,0:T(8,128)(2,1)S(1)} collective-permute-done((bf16[96,64,128]{2,1,0:T(8,128)(2,1)S(1)}, bf16[96,64,128]{2,1,0:T(8,128)(2,1)S(1)}, u32[]{:S(2)}, u32[]{:S(2)}) %collective-permute-start.1) | collective-permute-done | bytes 1572896 | tf_op jit(solution)/shard_map/ppermute | solution.py:74
  75.5 2.0 %pad_maximum_fusion = bf16[32,6,64,128]{3,2,1,0:T(8,128)(2,1)} fusion(bf16[32,3,64,128]{3,2,1,0:T(8,128)(2,1)S(1)} %bitcast.73, bf16[32,3,64,128]{3,2,1,0:T(8,128)(2,1)S(1)} %bitcast.68), kind=kLoop, calls=%fused_computation.1 | loop fusion | flops 1572864 | bytes 6291456 | tf_op jit(solution)/shard_map/concatenate | solution.py:249
  77.5 31.5 %collective-permute-done.8.refs_2_ = bf16[8,64,2048]{2,1,0:T(8,128)(2,1)S(1)} collective-permute-done((bf16[8,64,2048]{2,1,0:T(8,128)(2,1)S(1)}, bf16[8,64,2048]{2,1,0:T(8,128)(2,1)S(1)}, u32[]{:S(2)}, u32[]{:S(2)}) %collective-permute-start.8) | collective-permute-done | bytes 2097184 | tf_op jit(solution)/shard_map/ppermute | solution.py:74
  108.9 1.8 collective-permute-done.6
  110.7 9.2 %all-to-all-start.2 = ((bf16[32,6,64,128]{3,2,1,0:T(8,128)(2,1)}), bf16[32,6,64,128]{3,2,1,0:T(8,128)(2,1)}, u32[]{:S(2)}, u32[]{:S(2)}) async-start(bf16[32,6,64,128]{3,2,1,0:T(8,128)(2,1)} %pad_maximum_fusion), calls=%async_computation.2 | async-start | bytes 6291456 | tf_op jit(solution)/shard_map/all_to_all | solution.py:253
  120.0 0.6 slice.58
  121.3 0.5 constant_dynamic-slice_fusion
  123.8 0.6 pad_add_fusion.pos_ref
  124.4 1.5 slice.80
  125.9 1.1 convert_reduce_fusion
  127.0 0.1 slice.75
  127.0 1.3 slice.74
  128.3 1.0 collective-permute-start.12
  129.3 0.6 collective-permute-start.13
  129.9 1.5 slice.69
  131.4 2.3 %fusion.5 = f32[4,3,128,128]{3,2,1,0:T(8,128)S(1)} fusion(bf16[8,4,4,64,128]{4,3,0,2,1:T(8,128)(2,1)} %collective-permute-done.6, f32[8,64]{1,0:T(8,128)S(1)} %convert_reduce_fusion, bf16[8,4,4,64,128]{4,3,0,2,1:T(8,128)(2,1)S(1)} %bitcast.66), kind=kOutput, calls=%fused_computation.14 | convolution fusion | flops 203685888 | bytes 3936256 | tf_op jit(solution)/shard_map/sabgp,sabgq->abpq/dot_general | solution.py:226
  133.7 1.3 fusion.8
  135.0 4.8 %copy.19 = bf16[32,64,6,128]{3,2,1,0:T(8,128)(2,1)S(1)} copy(bf16[32,64,6,128]{3,1,2,0:T(8,128)(2,1)} %bitcast.33) | data formatting | bytes 6291456 | tf_op jit(solution)/shard_map/transpose | solution.py:289
  139.8 0.8 copy.28
  140.6 0.5 fusion.12
  141.1 0.3 broadcast_select_fusion
  141.4 0.8 fusion.16
  142.1 2.5 %collective-permute-start.11 = (f32[2,3,64,128]{3,2,1,0:T(8,128)S(1)}, f32[2,3,64,128]{3,2,1,0:T(8,128)S(1)}, u32[]{:S(2)}, u32[]{:S(2)}) collective-permute-start(f32[2,3,64,128]{3,2,1,0:T(8,128)S(1)} %get-tuple-element.37), channel_id=1, source_target_pairs={{0,24},{1,25},{2,26},{3,27},{4,28},{5,29},{6,30},{7,31},{8,0},{9,1... | collective-permute-start | bytes 589832 | tf_op jit(solution)/shard_map/ppermute | solution.py:74
  144.6 1.7 collective-permute-start.10
  146.3 6.9 %shard_map.65.near_ref = bf16[6,1536,128]{2,1,0:T(8,128)(2,1)S(1)} custom-call(bf16[8,64,2048]{2,1,0:T(8,128)(2,1)S(1)} %copy-done.5, bf16[8,64,2048]{2,1,0:T(8,128)(2,1)} %collective-permute-done.7.refs_1_, bf16[8,64,2048]{2,1,0:T(8,128)(2,1)S(1)} %collective-permute-done.8.refs_2_, bf16[2048,768]{1,0:T(8,128)(2,1)S(1)} %bitcast.60), custom_call_target="tpu_custom_call" | custom-call | flops 4831838208 | bytes 11796480 | tf_op jit(solution)/shard_map/pallas_call | solution.py:93
  153.2 1.4 copy-done.3
  154.6 11.9 %collective-permute-done.12.refs_0_ = bf16[4,64,2048]{2,1,0:T(8,128)(2,1)S(1)} collective-permute-done((bf16[4,64,2048]{2,1,0:T(8,128)(2,1)S(1)}, bf16[4,64,2048]{2,1,0:T(8,128)(2,1)S(1)}, u32[]{:S(2)}, u32[]{:S(2)}) %collective-permute-start.12) | collective-permute-done | bytes 1048608 | tf_op jit(solution)/shard_map/ppermute | solution.py:74
  166.5 2.4 %collective-permute-done.13.refs_1_ = bf16[4,64,2048]{2,1,0:T(8,128)(2,1)S(1)} collective-permute-done((bf16[4,64,2048]{2,1,0:T(8,128)(2,1)S(1)}, bf16[4,64,2048]{2,1,0:T(8,128)(2,1)S(1)}, u32[]{:S(2)}, u32[]{:S(2)}) %collective-permute-start.13) | collective-permute-done | bytes 1048608 | tf_op jit(solution)/shard_map/ppermute | solution.py:74
  168.8 1.8 shard_map.66.far_ref
  170.7 0.9 copy-done.2
  171.6 7.2 %shard_map.67 = (f32[3,64,128]{2,1,0:T(8,128)}, f32[3,64,128]{2,1,0:T(8,128)}) custom-call(s32[4]{0:T(128)} %pad_add_fusion.pos_ref, bf16[6,1536,128]{2,1,0:T(8,128)(2,1)} %copy-done.3, bf16[6,512,128]{2,1,0:T(8,128)(2,1)} %copy-done.2, bf16[32,6,64,128]{3,2,1,0:T(8,128)(2,1)} %all-to-all-done.2.conduction_ref), custom_call_target="tpu_custom_call" | custom-call | flops 402653184 | bytes 7340032 | tf_op jit(solution)/shard_map/pallas_call | solution.py:162
  178.7 7.6 %collective-permute-start.14 = (f32[3,64,128]{2,1,0:T(8,128)}, f32[3,64,128]{2,1,0:T(8,128)S(1)}, u32[]{:S(2)}, u32[]{:S(2)}) collective-permute-start(f32[3,64,128]{2,1,0:T(8,128)} %get-tuple-element.30), channel_id=1, source_target_pairs={{0,32},{1,33},{2,34},{3,35},{4,36},{5,37},{6,38},{7,39},{8,40},{9,... | collective-permute-start | bytes 294920 | tf_op jit(solution)/shard_map/ppermute | solution.py:74
  186.4 0.6 copy-done.10
  187.0 0.1 copy-done.11
  187.2 2.1 %shard_map.64 = f32[2,3,64,128]{3,2,1,0:T(8,128)} custom-call(f32[2,3,64,128]{3,2,1,0:T(8,128)} %get-tuple-element.38.first_ref, f32[2,3,64,128]{3,2,1,0:T(8,128)} %copy-done.11, f32[2,3,64,128]{3,2,1,0:T(8,128)} %copy-done.12, f32[2,3,64,128]{3,2,1,0:T(8,128)} %copy-done.10), custom_call_target="tpu_custom_call" | custom-call | tf_op jit(solution)/shard_map/pallas_call | solution.py:190
  189.2 1.8 select_subtract_fusion
  (44 shorter events, 0.4 us)
Async XLA Ops:
  0.0 1.0 copy-start
  1.0 4.4 %copy-start.9 = (bf16[96,64,128]{2,1,0:T(8,128)(2,1)S(1)}, bf16[96,64,128]{2,1,0:T(8,128)(2,1)}, u32[]{:S(2)}) copy-start(bf16[96,64,128]{2,1,0:T(8,128)(2,1)} %param.6) | copy-start | bytes 4718596
  1.1 7.6 %collective-permute-start = (bf16[1,64,2048]{2,1,0:T(8,128)(2,1)S(1)}, bf16[1,64,2048]{2,1,0:T(8,128)(2,1)S(1)}, u32[]{:S(2)}, u32[]{:S(2)}) collective-permute-start(bf16[1,64,2048]{2,1,0:T(8,128)(2,1)S(1)} %constant_dynamic-slice_fusion.3), channel_id=1, source_target_pairs={{0,4},{1,5},{2,6},{3,7},{4,0},{5,1},{6,2},{7,3},{8,12},{9,13},{10,... | collective-permute-start | bytes 786440 | tf_op jit(solution)/shard_map/ppermute | solution.py:74
  8.7 31.8 %all-to-all-start = ((bf16[8,17,64,128]{3,2,1,0:T(8,128)(2,1)}), bf16[8,17,64,128]{3,2,1,0:T(8,128)(2,1)}, u32[]{:S(2)}, u32[]{:S(2)}) async-start(bf16[8,17,64,128]{3,2,1,0:T(8,128)(2,1)} %pad_maximum_fusion.2), calls=%async_computation | async-start | bytes 4456448 | tf_op jit(solution)/shard_map/all_to_all | solution.py:253
  16.6 6.6 %collective-permute-start.2 = (bf16[96,64,128]{2,1,0:T(8,128)(2,1)S(1)}, bf16[96,64,128]{2,1,0:T(8,128)(2,1)S(1)}, u32[]{:S(2)}, u32[]{:S(2)}) collective-permute-start(bf16[96,64,128]{2,1,0:T(8,128)(2,1)S(1)} %get-tuple-element.32), channel_id=1, source_target_pairs={{0,32},{1,33},{2,34},{3,35},{4,36},{5,37},{6,38},{7,39},{8,40},{9,... | collective-permute-start | bytes 4718600 | tf_op jit(solution)/shard_map/ppermute | solution.py:74
  18.7 9.6 %collective-permute-start.5 = (bf16[2,64,2048]{2,1,0:T(8,128)(2,1)S(1)}, bf16[2,64,2048]{2,1,0:T(8,128)(2,1)S(1)}, u32[]{:S(2)}, u32[]{:S(2)}) collective-permute-start(bf16[2,64,2048]{2,1,0:T(8,128)(2,1)S(1)} %pad_maximum_fusion.4), channel_id=1, source_target_pairs={{0,2},{1,3},{2,0},{3,1},{4,6},{5,7},{6,4},{7,5},{8,10},{9,11},{10,... | collective-permute-start | bytes 1572872 | tf_op jit(solution)/shard_map/ppermute | solution.py:74
  21.7 13.0 %collective-permute-start.4 = (bf16[2,64,2048]{2,1,0:T(8,128)(2,1)S(1)}, bf16[2,64,2048]{2,1,0:T(8,128)(2,1)S(1)}, u32[]{:S(2)}, u32[]{:S(2)}) collective-permute-start(bf16[2,64,2048]{2,1,0:T(8,128)(2,1)S(1)} %pad_maximum_fusion.4), channel_id=1, source_target_pairs={{0,3},{1,0},{2,1},{3,2},{4,7},{5,4},{6,5},{7,6},{8,11},{9,8},{10,9... | collective-permute-start | bytes 1572872 | tf_op jit(solution)/shard_map/ppermute | solution.py:74
  22.4 12.3 %collective-permute-start.3 = (bf16[2,64,2048]{2,1,0:T(8,128)(2,1)S(1)}, bf16[2,64,2048]{2,1,0:T(8,128)(2,1)}, u32[]{:S(2)}, u32[]{:S(2)}) collective-permute-start(bf16[2,64,2048]{2,1,0:T(8,128)(2,1)S(1)} %pad_maximum_fusion.4), channel_id=1, source_target_pairs={{0,1},{1,2},{2,3},{3,0},{4,5},{5,6},{6,7},{7,4},{8,9},{9,10},{10,1... | collective-permute-start | bytes 1572872 | tf_op jit(solution)/shard_map/ppermute | solution.py:74
  40.5 70.2 %all-to-all-start.1 = ((bf16[32,6,64,128]{3,2,1,0:T(8,128)(2,1)}), bf16[32,6,64,128]{3,2,1,0:T(8,128)(2,1)}, u32[]{:S(2)}, u32[]{:S(2)}) async-start(bf16[32,6,64,128]{3,2,1,0:T(8,128)(2,1)} %pad_maximum_fusion.1), calls=%async_computation.1 | async-start | bytes 6291456 | tf_op jit(solution)/shard_map/all_to_all | solution.py:253
  49.2 3.3 %copy-start.4 = (bf16[8,64,2048]{2,1,0:T(8,128)(2,1)}, bf16[8,64,2048]{2,1,0:T(8,128)(2,1)S(1)}, u32[]{:S(2)}) copy-start(bf16[8,64,2048]{2,1,0:T(8,128)(2,1)S(1)} %constant_dynamic-update-slice_fusion.refs_0_) | copy-start | bytes 6291460
  49.2 59.7 %collective-permute-start.8 = (bf16[8,64,2048]{2,1,0:T(8,128)(2,1)S(1)}, bf16[8,64,2048]{2,1,0:T(8,128)(2,1)S(1)}, u32[]{:S(2)}, u32[]{:S(2)}) collective-permute-start(bf16[8,64,2048]{2,1,0:T(8,128)(2,1)S(1)} %constant_dynamic-update-slice_fusion.refs_0_), channel_id=1, source_target_pairs={{0,24},{1,25},{2,26},{3,27},{4,28},{5,29},{6,30},{7,31},{8,0},{9,1... | collective-permute-start | bytes 6291464 | tf_op jit(solution)/shard_map/ppermute | solution.py:74
  49.5 59.4 %collective-permute-start.7 = (bf16[8,64,2048]{2,1,0:T(8,128)(2,1)S(1)}, bf16[8,64,2048]{2,1,0:T(8,128)(2,1)}, u32[]{:S(2)}, u32[]{:S(2)}) collective-permute-start(bf16[8,64,2048]{2,1,0:T(8,128)(2,1)S(1)} %constant_dynamic-update-slice_fusion.refs_0_), channel_id=1, source_target_pairs={{0,8},{1,9},{2,10},{3,11},{4,12},{5,13},{6,14},{7,15},{8,16},{9,17... | collective-permute-start | bytes 6291464 | tf_op jit(solution)/shard_map/ppermute | solution.py:74
  52.5 16.8 %copy-start.8 = (bf16[2,96,64,128]{3,2,1,0:T(8,128)(2,1)S(1)}, bf16[2,96,64,128]{3,2,1,0:T(8,128)(2,1)}, u32[]{:S(2)}) copy-start(bf16[2,96,64,128]{3,2,1,0:T(8,128)(2,1)} %param.8) | copy-start | bytes 9437188
  52.7 17.3 %copy-start.6 = (bf16[8,16,64,128]{3,2,0,1:T(8,128)(2,1)}, bf16[8,16,64,128]{3,2,0,1:T(8,128)(2,1)S(1)}, u32[]{:S(2)}) copy-start(bf16[8,16,64,128]{3,2,0,1:T(8,128)(2,1)S(1)} %copy.18) | copy-start | bytes 6291460
  52.7 58.0 %collective-permute-start.6 = (bf16[8,4,4,64,128]{4,3,0,2,1:T(8,128)(2,1)S(1)}, bf16[8,4,4,64,128]{4,3,0,2,1:T(8,128)(2,1)}, u32[]{:S(2)}, u32[]{:S(2)}) collective-permute-start(bf16[8,4,4,64,128]{4,3,0,2,1:T(8,128)(2,1)S(1)} %bitcast.64), channel_id=1, source_target_pairs={{0,96},{1,97},{2,98},{3,99},{4,100},{5,101},{6,102},{7,103},{8,104... | collective-permute-start | bytes 6291464 | tf_op jit(solution)/shard_map/ppermute | solution.py:74
  70.0 5.4 %collective-permute-start.1 = (bf16[96,64,128]{2,1,0:T(8,128)(2,1)S(1)}, bf16[96,64,128]{2,1,0:T(8,128)(2,1)S(1)}, u32[]{:S(2)}, u32[]{:S(2)}) collective-permute-start(bf16[96,64,128]{2,1,0:T(8,128)(2,1)S(1)} %get-tuple-element.34), channel_id=1, source_target_pairs={{0,32},{1,33},{2,34},{3,35},{4,36},{5,37},{6,38},{7,39},{8,40},{9,... | collective-permute-start | bytes 4718600 | tf_op jit(solution)/shard_map/ppermute | solution.py:74
  77.5 42.6 %copy-start.13 = (s32[2,2]{1,0:T(2,128)S(1)}, s32[2,2]{1,0:T(2,128)}, u32[]{:S(2)}) copy-start(s32[2,2]{1,0:T(2,128)} %param.11) | copy-start | bytes 52
  110.7 60.8 %all-to-all-start.2 = ((bf16[32,6,64,128]{3,2,1,0:T(8,128)(2,1)}), bf16[32,6,64,128]{3,2,1,0:T(8,128)(2,1)}, u32[]{:S(2)}, u32[]{:S(2)}) async-start(bf16[32,6,64,128]{3,2,1,0:T(8,128)(2,1)} %pad_maximum_fusion), calls=%async_computation.2 | async-start | bytes 6291456 | tf_op jit(solution)/shard_map/all_to_all | solution.py:253
  128.3 3.1 %copy-start.7 = (bf16[8,16,64,128]{3,2,0,1:T(8,128)(2,1)S(1)}, bf16[8,16,64,128]{3,2,0,1:T(8,128)(2,1)}, u32[]{:S(2)}) copy-start(bf16[8,16,64,128]{3,2,0,1:T(8,128)(2,1)} %copy-done.6) | copy-start | bytes 6291460
  128.3 38.1 %collective-permute-start.12 = (bf16[4,64,2048]{2,1,0:T(8,128)(2,1)S(1)}, bf16[4,64,2048]{2,1,0:T(8,128)(2,1)S(1)}, u32[]{:S(2)}, u32[]{:S(2)}) collective-permute-start(bf16[4,64,2048]{2,1,0:T(8,128)(2,1)S(1)} %slice.74), channel_id=1, source_target_pairs={{0,8},{1,9},{2,10},{3,11},{4,12},{5,13},{6,14},{7,15},{8,16},{9,17... | collective-permute-start | bytes 3145736 | tf_op jit(solution)/shard_map/ppermute | solution.py:74
  129.3 39.5 %collective-permute-start.13 = (bf16[4,64,2048]{2,1,0:T(8,128)(2,1)S(1)}, bf16[4,64,2048]{2,1,0:T(8,128)(2,1)S(1)}, u32[]{:S(2)}, u32[]{:S(2)}) collective-permute-start(bf16[4,64,2048]{2,1,0:T(8,128)(2,1)S(1)} %slice.75), channel_id=1, source_target_pairs={{0,24},{1,25},{2,26},{3,27},{4,28},{5,29},{6,30},{7,31},{8,0},{9,1... | collective-permute-start | bytes 3145736 | tf_op jit(solution)/shard_map/ppermute | solution.py:74
  141.1 5.2 %copy-start.5 = (bf16[8,64,2048]{2,1,0:T(8,128)(2,1)S(1)}, bf16[8,64,2048]{2,1,0:T(8,128)(2,1)}, u32[]{:S(2)}) copy-start(bf16[8,64,2048]{2,1,0:T(8,128)(2,1)} %copy-done.4) | copy-start | bytes 6291460
  142.1 44.2 %collective-permute-start.11 = (f32[2,3,64,128]{3,2,1,0:T(8,128)S(1)}, f32[2,3,64,128]{3,2,1,0:T(8,128)S(1)}, u32[]{:S(2)}, u32[]{:S(2)}) collective-permute-start(f32[2,3,64,128]{3,2,1,0:T(8,128)S(1)} %get-tuple-element.37), channel_id=1, source_target_pairs={{0,24},{1,25},{2,26},{3,27},{4,28},{5,29},{6,30},{7,31},{8,0},{9,1... | collective-permute-start | bytes 589832 | tf_op jit(solution)/shard_map/ppermute | solution.py:74
  144.6 41.8 %collective-permute-start.9 = (f32[2,3,64,128]{3,2,1,0:T(8,128)S(1)}, f32[2,3,64,128]{3,2,1,0:T(8,128)S(1)}, u32[]{:S(2)}, u32[]{:S(2)}) collective-permute-start(f32[2,3,64,128]{3,2,1,0:T(8,128)S(1)} %get-tuple-element.39), channel_id=1, source_target_pairs={{0,8},{1,9},{2,10},{3,11},{4,12},{5,13},{6,14},{7,15},{8,16},{9,17... | collective-permute-start | bytes 589832 | tf_op jit(solution)/shard_map/ppermute | solution.py:74
  144.6 41.8 %collective-permute-start.10 = (f32[2,3,64,128]{3,2,1,0:T(8,128)S(1)}, f32[2,3,64,128]{3,2,1,0:T(8,128)S(1)}, u32[]{:S(2)}, u32[]{:S(2)}) collective-permute-start(f32[2,3,64,128]{3,2,1,0:T(8,128)S(1)} %get-tuple-element.40), channel_id=1, source_target_pairs={{0,16},{1,17},{2,18},{3,19},{4,20},{5,21},{6,22},{7,23},{8,24},{9,... | collective-permute-start | bytes 589832 | tf_op jit(solution)/shard_map/ppermute | solution.py:74
  153.2 1.4 copy-start.3
  170.7 0.9 copy-start.2
  171.6 19.4 %copy-start.1 = (bf16[2,64,2048]{2,1,0:T(8,128)(2,1)S(1)}, bf16[2,64,2048]{2,1,0:T(8,128)(2,1)}, u32[]{:S(2)}) copy-start(bf16[2,64,2048]{2,1,0:T(8,128)(2,1)} %param.10) | copy-start | bytes 1572868
  178.7 10.5 %collective-permute-start.14 = (f32[3,64,128]{2,1,0:T(8,128)}, f32[3,64,128]{2,1,0:T(8,128)S(1)}, u32[]{:S(2)}, u32[]{:S(2)}) collective-permute-start(f32[3,64,128]{2,1,0:T(8,128)} %get-tuple-element.30), channel_id=1, source_target_pairs={{0,32},{1,33},{2,34},{3,35},{4,36},{5,37},{6,38},{7,39},{8,40},{9,... | collective-permute-start | bytes 294920 | tf_op jit(solution)/shard_map/ppermute | solution.py:74
  186.4 0.7 copy-start.10
  186.4 0.8 copy-start.11
  186.4 0.8 copy-start.12

commit v5 on v4

--- a/solution.py
+++ b/solution.py
@@ -282,7 +282,8 @@
     next_rows = send(here, ka_back())
 
     conduction = both_cores(dens_cc, core)
-    conduction, valence, next_rows, behind, ahead = after((conduction, valence, next_rows, behind, ahead))
+    conduction, valence = after((conduction, valence))
+    next_rows, behind, ahead = after((next_rows, behind, ahead))
     far_low, far_high = send(behind[:4], along_second(1)), send(ahead[4:], along_second(-1))
     conduction = spread(conduction)
 

time: 192 us -> 183 us (0.953)
  the two profiles are of different devices: /device:TPU:5 before, /device:TPU:35 now
where the time goes in v5:
time: 183 us; the launch traced here: 182 us
  starting transfers between devices  63.5 us (35%)
  waiting for transfers between devices  52.1 us (28%)
  local copies, waits for them, and re-layouts  30.2 us (17%)
  Pallas kernels  18.5 us (10%)
  other arithmetic  11.4 us (6%)
  matrix products  4 us (2%)
  between operations  2.62 us (1%)
    ppermute x15, waiting for transfers between devices, send(): return lax.ppermute(array, AXES, pairs)  48.1 us
    ppermute x15, starting transfers between devices, send(): return lax.ppermute(array, AXES, pairs)  42.7 us
    all_to_all x3, starting transfers between devices, spread(): lax.all_to_all(packed, 'ga', split_axis=0, concat_axis=0, tiled=True, axi...  20.9 us
    pallas_call x2, Pallas kernels, image_of(): pl.pallas_call(image_kernel, out_shape=jax.ShapeDtypeStruct((6, count, 12...  9.31 us
    unnamed x25, local copies, waits for them, and re-layouts  7.57 us
    pallas_call x1, Pallas kernels, direct_of(): pl.pallas_call(direct_kernel, out_shape=(shape, shape), in_specs=[pl.Bloc...  7.16 us
    dynamic_slice x2, local copies, waits for them, and re-layouts, both_cores(): mine = lax.dynamic_index_in_dim(dens, core, 0, keepdims=False)  5.15 us
    transpose x1, local copies, waits for them, and re-layouts, local(): valence = jnp.transpose(valence, (0, 2, 1, 3)).reshape(2048, 768)  4.8 us
  transfers between devices with their start and end apart: 18, of which 7 were waited for; matrix products, arithmetic and copies ran while one was open for 22% of the time, Pallas kernels for 10%

profile of v5, /device:TPU:35, one launch (start us, length us, event | category | flops | bytes accessed | tf_op | source)
XLA Modules:
  0.0 182.4 jit_solution(4060546890023105323)
XLA Ops:
  0.0 1.0 copy-done
  1.1 0.1 collective-permute-start
  1.2 1.2 slice.77
  2.3 0.9 slice.76
  3.2 0.7 fusion.24
  3.9 0.2 pad_maximum_fusion.3
  4.1 0.1 copy.23
  4.3 1.6 pad_maximum_fusion.2
  5.9 2.4 %collective-permute-done = bf16[1,64,2048]{2,1,0:T(8,128)(2,1)S(1)} collective-permute-done((bf16[1,64,2048]{2,1,0:T(8,128)(2,1)S(1)}, bf16[1,64,2048]{2,1,0:T(8,128)(2,1)S(1)}, u32[]{:S(2)}, u32[]{:S(2)}) %collective-permute-start) | collective-permute-done | bytes 262176 | tf_op jit(solution)/shard_map/ppermute | solution.py:74
  8.4 5.2 %all-to-all-start = ((bf16[8,17,64,128]{3,2,1,0:T(8,128)(2,1)}), bf16[8,17,64,128]{3,2,1,0:T(8,128)(2,1)}, u32[]{:S(2)}, u32[]{:S(2)}) async-start(bf16[8,17,64,128]{3,2,1,0:T(8,128)(2,1)} %pad_maximum_fusion.2), calls=%async_computation | async-start | bytes 4456448 | tf_op jit(solution)/shard_map/all_to_all | solution.py:253
  13.6 2.6 %constant_dynamic-slice_fusion.2 = (bf16[1,96,64,128]{3,2,1,0:T(8,128)(2,1)S(1)}, bf16[96,64,128]{2,1,0:T(8,128)(2,1)S(1)}) fusion(bf16[2,96,64,128]{3,2,1,0:T(8,128)(2,1)} %param.9, s32[]{:T(128)S(6)} %select_n.75, s32[]{:T(128)S(6)} %select_n.76), kind=kLoop, calls=%fused_computation.54 | loop fusion | bytes 6291464 | tf_op jit(solution)/shard_map/jit(dynamic_index_in_dim)/dynamic_slice | solution.py:246
  16.1 2.2 %collective-permute-start.2 = (bf16[96,64,128]{2,1,0:T(8,128)(2,1)S(1)}, bf16[96,64,128]{2,1,0:T(8,128)(2,1)S(1)}, u32[]{:S(2)}, u32[]{:S(2)}) collective-permute-start(bf16[96,64,128]{2,1,0:T(8,128)(2,1)S(1)} %get-tuple-element.34), channel_id=1, source_target_pairs={{0,32},{1,33},{2,34},{3,35},{4,36},{5,37},{6,38},{7,39},{8,40},{9,... | collective-permute-start | bytes 4718600 | tf_op jit(solution)/shard_map/ppermute | solution.py:74
  18.3 1.3 collective-permute-start.3
  19.6 1.4 collective-permute-start.4
  21.1 1.6 collective-permute-start.5
  22.7 2.0 %pad_maximum_fusion = bf16[32,6,64,128]{3,2,1,0:T(8,128)(2,1)} fusion(bf16[32,3,64,128]{3,2,1,0:T(8,128)(2,1)S(1)} %bitcast.70, bf16[32,3,64,128]{3,2,1,0:T(8,128)(2,1)S(1)} %bitcast.65), kind=kLoop, calls=%fused_computation.1 | loop fusion | flops 1572864 | bytes 6291456 | tf_op jit(solution)/shard_map/concatenate | solution.py:249
  24.7 3.2 %collective-permute-done.3 = bf16[2,64,2048]{2,1,0:T(8,128)(2,1)S(1)} collective-permute-done((bf16[2,64,2048]{2,1,0:T(8,128)(2,1)S(1)}, bf16[2,64,2048]{2,1,0:T(8,128)(2,1)S(1)}, u32[]{:S(2)}, u32[]{:S(2)}) %collective-permute-start.3) | collective-permute-done | bytes 524320 | tf_op jit(solution)/shard_map/ppermute | solution.py:74
  27.9 0.2 collective-permute-done.4
  28.0 6.5 %collective-permute-done.5 = bf16[2,64,2048]{2,1,0:T(8,128)(2,1)} collective-permute-done((bf16[2,64,2048]{2,1,0:T(8,128)(2,1)S(1)}, bf16[2,64,2048]{2,1,0:T(8,128)(2,1)}, u32[]{:S(2)}, u32[]{:S(2)}) %collective-permute-start.5) | collective-permute-done | bytes 524320 | tf_op jit(solution)/shard_map/ppermute | solution.py:74
  34.5 4.0 %all-to-all-done = bf16[8,17,64,128]{3,2,1,0:T(8,128)(2,1)} async-done(((bf16[8,17,64,128]{3,2,1,0:T(8,128)(2,1)}), bf16[8,17,64,128]{3,2,1,0:T(8,128)(2,1)}, u32[]{:S(2)}, u32[]{:S(2)}) %all-to-all-start) | async-done | bytes 2228256 | tf_op jit(solution)/shard_map/all_to_all | solution.py:253
  38.5 9.0 %all-to-all-start.1 = ((bf16[32,6,64,128]{3,2,1,0:T(8,128)(2,1)}), bf16[32,6,64,128]{3,2,1,0:T(8,128)(2,1)}, u32[]{:S(2)}, u32[]{:S(2)}) async-start(bf16[32,6,64,128]{3,2,1,0:T(8,128)(2,1)} %pad_maximum_fusion), calls=%async_computation.1 | async-start | bytes 6291456 | tf_op jit(solution)/shard_map/all_to_all | solution.py:253
  47.5 2.6 %constant_dynamic-slice_fusion = (bf16[1,96,64,128]{3,2,1,0:T(8,128)(2,1)S(1)}, bf16[96,64,128]{2,1,0:T(8,128)(2,1)S(1)}) fusion(bf16[2,96,64,128]{3,2,1,0:T(8,128)(2,1)} %param.8, s32[]{:T(128)S(6)} %select_n.75, s32[]{:T(128)S(6)} %select_n.76), kind=kLoop, calls=%fused_computation.51 | loop fusion | bytes 6291464 | tf_op jit(solution)/shard_map/jit(dynamic_index_in_dim)/dynamic_slice | solution.py:246
  50.1 15.2 %collective-permute-start.11 = (bf16[96,64,128]{2,1,0:T(8,128)(2,1)S(1)}, bf16[96,64,128]{2,1,0:T(8,128)(2,1)S(1)}, u32[]{:S(2)}, u32[]{:S(2)}) collective-permute-start(bf16[96,64,128]{2,1,0:T(8,128)(2,1)S(1)} %get-tuple-element.32), channel_id=1, source_target_pairs={{0,32},{1,33},{2,34},{3,35},{4,36},{5,37},{6,38},{7,39},{8,40},{9,... | collective-permute-start | bytes 4718600 | tf_op jit(solution)/shard_map/ppermute | solution.py:74
  65.4 0.8 constant_dynamic-update-slice_fusion.3
  66.2 0.8 constant_dynamic-update-slice_fusion.2
  67.0 0.8 constant_dynamic-update-slice_fusion.1
  67.9 1.9 %constant_dynamic-update-slice_fusion.refs_0_ = bf16[8,64,2048]{2,1,0:T(8,128)(2,1)} fusion(bf16[8,64,2048]{2,1,0:T(8,128)(2,1)} %constant_dynamic-update-slice_fusion.1, bf16[2,64,2048]{2,1,0:T(8,128)(2,1)} %collective-permute-done.5), kind=kLoop, calls=%fused_computation.47 | loop fusion | bytes 1048576 | tf_op jit(solution)/shard_map/concatenate | solution.py:275
  69.8 1.2 collective-permute-start.6
  70.9 0.3 collective-permute-start.7
  71.2 1.8 slice.79
  73.0 1.5 copy.18
  74.5 1.8 collective-permute-start.1
  76.3 2.0 %pad_maximum_fusion.1 = bf16[32,6,64,128]{3,2,1,0:T(8,128)(2,1)} fusion(bf16[32,3,64,128]{3,2,1,0:T(8,128)(2,1)S(1)} %bitcast.69, bf16[32,3,64,128]{3,2,1,0:T(8,128)(2,1)S(1)} %bitcast.64), kind=kLoop, calls=%fused_computation.4 | loop fusion | flops 1572864 | bytes 6291456 | tf_op jit(solution)/shard_map/concatenate | solution.py:249
  78.3 6.7 %all-to-all-start.2 = ((bf16[32,6,64,128]{3,2,1,0:T(8,128)(2,1)}), bf16[32,6,64,128]{3,2,1,0:T(8,128)(2,1)}, u32[]{:S(2)}, u32[]{:S(2)}) async-start(bf16[32,6,64,128]{3,2,1,0:T(8,128)(2,1)} %pad_maximum_fusion.1), calls=%async_computation.2 | async-start | bytes 6291456 | tf_op jit(solution)/shard_map/all_to_all | solution.py:253
  85.0 0.6 slice.58
  86.2 0.5 constant_dynamic-slice_fusion.1
  88.5 0.6 pad_add_fusion.pos_ref
  89.0 1.5 slice.80
  90.6 1.1 convert_reduce_fusion
  91.6 19.5 %collective-permute-done.6.refs_1_ = bf16[8,64,2048]{2,1,0:T(8,128)(2,1)S(1)} collective-permute-done((bf16[8,64,2048]{2,1,0:T(8,128)(2,1)}, bf16[8,64,2048]{2,1,0:T(8,128)(2,1)S(1)}, u32[]{:S(2)}, u32[]{:S(2)}) %collective-permute-start.6) | collective-permute-done | bytes 2097184 | tf_op jit(solution)/shard_map/ppermute | solution.py:74
  111.1 16.3 %collective-permute-done.1 = bf16[8,4,4,64,128]{4,3,0,2,1:T(8,128)(2,1)} collective-permute-done((bf16[8,4,4,64,128]{4,3,0,2,1:T(8,128)(2,1)}, bf16[8,4,4,64,128]{4,3,0,2,1:T(8,128)(2,1)}, u32[]{:S(2)}, u32[]{:S(2)}) %collective-permute-start.1) | collective-permute-done | bytes 2097184 | tf_op jit(solution)/shard_map/ppermute | solution.py:74
  127.4 1.5 slice.69
  129.0 9.9 %collective-permute-start.12 = (bf16[4,64,2048]{2,1,0:T(8,128)(2,1)S(1)}, bf16[4,64,2048]{2,1,0:T(8,128)(2,1)S(1)}, u32[]{:S(2)}, u32[]{:S(2)}) collective-permute-start(bf16[4,64,2048]{2,1,0:T(8,128)(2,1)S(1)} %slice.74), channel_id=1, source_target_pairs={{0,8},{1,9},{2,10},{3,11},{4,12},{5,13},{6,14},{7,15},{8,16},{9,17... | collective-permute-start | bytes 3145736 | tf_op jit(solution)/shard_map/ppermute | solution.py:74
  138.9 1.3 slice.75
  140.3 2.7 %fusion.5 = f32[4,3,128,128]{3,2,1,0:T(8,128)S(1)} fusion(bf16[8,4,4,64,128]{4,3,0,2,1:T(8,128)(2,1)} %collective-permute-done.1, f32[8,64]{1,0:T(8,128)S(1)} %convert_reduce_fusion, bf16[8,4,4,64,128]{4,3,0,2,1:T(8,128)(2,1)} %bitcast.7), kind=kOutput, calls=%fused_computation.14 | convolution fusion | flops 203685888 | bytes 3934208 | tf_op jit(solution)/shard_map/sabgp,sabgq->abpq/dot_general | solution.py:226
  143.0 1.3 fusion.8
  144.3 0.5 fusion.12
  144.8 0.3 broadcast_select_fusion
  145.1 0.8 fusion.16
  145.8 3.1 %collective-permute-start.8 = (f32[2,3,64,128]{3,2,1,0:T(8,128)S(1)}, f32[2,3,64,128]{3,2,1,0:T(8,128)S(1)}, u32[]{:S(2)}, u32[]{:S(2)}) collective-permute-start(f32[2,3,64,128]{3,2,1,0:T(8,128)S(1)} %get-tuple-element.39), channel_id=1, source_target_pairs={{0,8},{1,9},{2,10},{3,11},{4,12},{5,13},{6,14},{7,15},{8,16},{9,17... | collective-permute-start | bytes 589832 | tf_op jit(solution)/shard_map/ppermute | solution.py:74
  148.9 1.9 %collective-permute-start.9 = (f32[2,3,64,128]{3,2,1,0:T(8,128)S(1)}, f32[2,3,64,128]{3,2,1,0:T(8,128)S(1)}, u32[]{:S(2)}, u32[]{:S(2)}) collective-permute-start(f32[2,3,64,128]{3,2,1,0:T(8,128)S(1)} %get-tuple-element.40), channel_id=1, source_target_pairs={{0,16},{1,17},{2,18},{3,19},{4,20},{5,21},{6,22},{7,23},{8,24},{9,... | collective-permute-start | bytes 589832 | tf_op jit(solution)/shard_map/ppermute | solution.py:74
  150.8 0.5 collective-permute-start.10
  151.3 4.8 %copy.19 = bf16[32,64,6,128]{3,2,1,0:T(8,128)(2,1)S(1)} copy(bf16[32,64,6,128]{3,1,2,0:T(8,128)(2,1)} %bitcast.33) | data formatting | bytes 6291456 | tf_op jit(solution)/shard_map/transpose | solution.py:290
  156.1 0.8 copy.28
  156.9 7.5 %shard_map.65.near_ref = bf16[6,1536,128]{2,1,0:T(8,128)(2,1)S(1)} custom-call(bf16[8,64,2048]{2,1,0:T(8,128)(2,1)} %constant_dynamic-update-slice_fusion.refs_0_, bf16[8,64,2048]{2,1,0:T(8,128)(2,1)S(1)} %collective-permute-done.6.refs_1_, bf16[8,64,2048]{2,1,0:T(8,128)(2,1)} %collective-permute-done.7.refs_2_, bf16[2048,768]{1,0:T(8,128)(2,1)S(1)} %bitcast.60), custom_call_target="tpu_custom_call" | custom-call | flops 4831838208 | bytes 11796480 | tf_op jit(solution)/shard_map/pallas_call | solution.py:93
  164.4 1.4 copy-done.3
  165.8 1.8 shard_map.66.far_ref
  167.6 0.9 copy-done.2
  168.5 7.2 %shard_map.67 = (f32[3,64,128]{2,1,0:T(8,128)}, f32[3,64,128]{2,1,0:T(8,128)}) custom-call(s32[4]{0:T(128)} %pad_add_fusion.pos_ref, bf16[6,1536,128]{2,1,0:T(8,128)(2,1)} %copy-done.3, bf16[6,512,128]{2,1,0:T(8,128)(2,1)} %copy-done.2, bf16[32,6,64,128]{3,2,1,0:T(8,128)(2,1)} %all-to-all-done.2.conduction_ref), custom_call_target="tpu_custom_call" | custom-call | flops 402653184 | bytes 7340032 | tf_op jit(solution)/shard_map/pallas_call | solution.py:162
  175.7 2.1 %collective-permute-start.14 = (f32[3,64,128]{2,1,0:T(8,128)}, f32[3,64,128]{2,1,0:T(8,128)S(1)}, u32[]{:S(2)}, u32[]{:S(2)}) collective-permute-start(f32[3,64,128]{2,1,0:T(8,128)} %get-tuple-element.30), channel_id=1, source_target_pairs={{0,32},{1,33},{2,34},{3,35},{4,36},{5,37},{6,38},{7,39},{8,40},{9,... | collective-permute-start | bytes 294920 | tf_op jit(solution)/shard_map/ppermute | solution.py:74
  177.8 0.6 copy-done.5
  178.4 0.1 copy-done.6
  178.6 2.1 %shard_map.64 = f32[2,3,64,128]{3,2,1,0:T(8,128)} custom-call(f32[2,3,64,128]{3,2,1,0:T(8,128)} %get-tuple-element.38.first_ref, f32[2,3,64,128]{3,2,1,0:T(8,128)} %copy-done.5, f32[2,3,64,128]{3,2,1,0:T(8,128)} %copy-done.6, f32[2,3,64,128]{3,2,1,0:T(8,128)} %copy-done.7), custom_call_target="tpu_custom_call" | custom-call | tf_op jit(solution)/shard_map/pallas_call | solution.py:190
  180.7 1.8 select_subtract_fusion
  (34 shorter events, 0.4 us)
Async XLA Ops:
  0.0 1.0 copy-start
  1.0 2.8 %copy-start.4 = (bf16[96,64,128]{2,1,0:T(8,128)(2,1)S(1)}, bf16[96,64,128]{2,1,0:T(8,128)(2,1)}, u32[]{:S(2)}) copy-start(bf16[96,64,128]{2,1,0:T(8,128)(2,1)} %param.6) | copy-start | bytes 4718596
  1.1 7.3 %collective-permute-start = (bf16[1,64,2048]{2,1,0:T(8,128)(2,1)S(1)}, bf16[1,64,2048]{2,1,0:T(8,128)(2,1)S(1)}, u32[]{:S(2)}, u32[]{:S(2)}) collective-permute-start(bf16[1,64,2048]{2,1,0:T(8,128)(2,1)S(1)} %constant_dynamic-slice_fusion.3), channel_id=1, source_target_pairs={{0,4},{1,5},{2,6},{3,7},{4,0},{5,1},{6,2},{7,3},{8,12},{9,13},{10,... | collective-permute-start | bytes 786440 | tf_op jit(solution)/shard_map/ppermute | solution.py:74
  8.4 30.2 %all-to-all-start = ((bf16[8,17,64,128]{3,2,1,0:T(8,128)(2,1)}), bf16[8,17,64,128]{3,2,1,0:T(8,128)(2,1)}, u32[]{:S(2)}, u32[]{:S(2)}) async-start(bf16[8,17,64,128]{3,2,1,0:T(8,128)(2,1)} %pad_maximum_fusion.2), calls=%async_computation | async-start | bytes 4456448 | tf_op jit(solution)/shard_map/all_to_all | solution.py:253
  16.1 6.6 %collective-permute-start.2 = (bf16[96,64,128]{2,1,0:T(8,128)(2,1)S(1)}, bf16[96,64,128]{2,1,0:T(8,128)(2,1)S(1)}, u32[]{:S(2)}, u32[]{:S(2)}) collective-permute-start(bf16[96,64,128]{2,1,0:T(8,128)(2,1)S(1)} %get-tuple-element.34), channel_id=1, source_target_pairs={{0,32},{1,33},{2,34},{3,35},{4,36},{5,37},{6,38},{7,39},{8,40},{9,... | collective-permute-start | bytes 4718600 | tf_op jit(solution)/shard_map/ppermute | solution.py:74
  18.3 9.5 %collective-permute-start.3 = (bf16[2,64,2048]{2,1,0:T(8,128)(2,1)S(1)}, bf16[2,64,2048]{2,1,0:T(8,128)(2,1)S(1)}, u32[]{:S(2)}, u32[]{:S(2)}) collective-permute-start(bf16[2,64,2048]{2,1,0:T(8,128)(2,1)S(1)} %pad_maximum_fusion.4), channel_id=1, source_target_pairs={{0,1},{1,2},{2,3},{3,0},{4,5},{5,6},{6,7},{7,4},{8,9},{9,10},{10,1... | collective-permute-start | bytes 1572872 | tf_op jit(solution)/shard_map/ppermute | solution.py:74
  19.6 8.4 %collective-permute-start.4 = (bf16[2,64,2048]{2,1,0:T(8,128)(2,1)S(1)}, bf16[2,64,2048]{2,1,0:T(8,128)(2,1)S(1)}, u32[]{:S(2)}, u32[]{:S(2)}) collective-permute-start(bf16[2,64,2048]{2,1,0:T(8,128)(2,1)S(1)} %pad_maximum_fusion.4), channel_id=1, source_target_pairs={{0,3},{1,0},{2,1},{3,2},{4,7},{5,4},{6,5},{7,6},{8,11},{9,8},{10,9... | collective-permute-start | bytes 1572872 | tf_op jit(solution)/shard_map/ppermute | solution.py:74
  21.1 13.5 %collective-permute-start.5 = (bf16[2,64,2048]{2,1,0:T(8,128)(2,1)S(1)}, bf16[2,64,2048]{2,1,0:T(8,128)(2,1)}, u32[]{:S(2)}, u32[]{:S(2)}) collective-permute-start(bf16[2,64,2048]{2,1,0:T(8,128)(2,1)S(1)} %pad_maximum_fusion.4), channel_id=1, source_target_pairs={{0,2},{1,3},{2,0},{3,1},{4,6},{5,7},{6,4},{7,5},{8,10},{9,11},{10,... | collective-permute-start | bytes 1572872 | tf_op jit(solution)/shard_map/ppermute | solution.py:74
  38.5 39.8 %all-to-all-start.1 = ((bf16[32,6,64,128]{3,2,1,0:T(8,128)(2,1)}), bf16[32,6,64,128]{3,2,1,0:T(8,128)(2,1)}, u32[]{:S(2)}, u32[]{:S(2)}) async-start(bf16[32,6,64,128]{3,2,1,0:T(8,128)(2,1)} %pad_maximum_fusion), calls=%async_computation.1 | async-start | bytes 6291456 | tf_op jit(solution)/shard_map/all_to_all | solution.py:253
  50.1 26.2 %collective-permute-start.11 = (bf16[96,64,128]{2,1,0:T(8,128)(2,1)S(1)}, bf16[96,64,128]{2,1,0:T(8,128)(2,1)S(1)}, u32[]{:S(2)}, u32[]{:S(2)}) collective-permute-start(bf16[96,64,128]{2,1,0:T(8,128)(2,1)S(1)} %get-tuple-element.32), channel_id=1, source_target_pairs={{0,32},{1,33},{2,34},{3,35},{4,36},{5,37},{6,38},{7,39},{8,40},{9,... | collective-permute-start | bytes 4718600 | tf_op jit(solution)/shard_map/ppermute | solution.py:74
  69.8 41.3 %collective-permute-start.6 = (bf16[8,64,2048]{2,1,0:T(8,128)(2,1)}, bf16[8,64,2048]{2,1,0:T(8,128)(2,1)S(1)}, u32[]{:S(2)}, u32[]{:S(2)}) collective-permute-start(bf16[8,64,2048]{2,1,0:T(8,128)(2,1)} %constant_dynamic-update-slice_fusion.refs_0_), channel_id=1, source_target_pairs={{0,8},{1,9},{2,10},{3,11},{4,12},{5,13},{6,14},{7,15},{8,16},{9,17... | collective-permute-start | bytes 6291464 | tf_op jit(solution)/shard_map/ppermute | solution.py:74
  70.9 40.1 %collective-permute-start.7 = (bf16[8,64,2048]{2,1,0:T(8,128)(2,1)}, bf16[8,64,2048]{2,1,0:T(8,128)(2,1)}, u32[]{:S(2)}, u32[]{:S(2)}) collective-permute-start(bf16[8,64,2048]{2,1,0:T(8,128)(2,1)} %constant_dynamic-update-slice_fusion.refs_0_), channel_id=1, source_target_pairs={{0,24},{1,25},{2,26},{3,27},{4,28},{5,29},{6,30},{7,31},{8,0},{9,1... | collective-permute-start | bytes 6291464 | tf_op jit(solution)/shard_map/ppermute | solution.py:74
  74.5 52.9 %collective-permute-start.1 = (bf16[8,4,4,64,128]{4,3,0,2,1:T(8,128)(2,1)}, bf16[8,4,4,64,128]{4,3,0,2,1:T(8,128)(2,1)}, u32[]{:S(2)}, u32[]{:S(2)}) collective-permute-start(bf16[8,4,4,64,128]{4,3,0,2,1:T(8,128)(2,1)} %bitcast.7), channel_id=1, source_target_pairs={{0,96},{1,97},{2,98},{3,99},{4,100},{5,101},{6,102},{7,103},{8,104... | collective-permute-start | bytes 6291464 | tf_op jit(solution)/shard_map/ppermute | solution.py:74
  78.3 6.7 %copy-start.8 = (s32[2,2]{1,0:T(2,128)S(1)}, s32[2,2]{1,0:T(2,128)}, u32[]{:S(2)}) copy-start(s32[2,2]{1,0:T(2,128)} %param.11) | copy-start | bytes 52
  78.3 90.2 %all-to-all-start.2 = ((bf16[32,6,64,128]{3,2,1,0:T(8,128)(2,1)}), bf16[32,6,64,128]{3,2,1,0:T(8,128)(2,1)}, u32[]{:S(2)}, u32[]{:S(2)}) async-start(bf16[32,6,64,128]{3,2,1,0:T(8,128)(2,1)} %pad_maximum_fusion.1), calls=%async_computation.2 | async-start | bytes 6291456 | tf_op jit(solution)/shard_map/all_to_all | solution.py:253
  129.0 36.8 %collective-permute-start.12 = (bf16[4,64,2048]{2,1,0:T(8,128)(2,1)S(1)}, bf16[4,64,2048]{2,1,0:T(8,128)(2,1)S(1)}, u32[]{:S(2)}, u32[]{:S(2)}) collective-permute-start(bf16[4,64,2048]{2,1,0:T(8,128)(2,1)S(1)} %slice.74), channel_id=1, source_target_pairs={{0,8},{1,9},{2,10},{3,11},{4,12},{5,13},{6,14},{7,15},{8,16},{9,17... | collective-permute-start | bytes 3145736 | tf_op jit(solution)/shard_map/ppermute | solution.py:74
  140.2 25.6 %collective-permute-start.13 = (bf16[4,64,2048]{2,1,0:T(8,128)(2,1)S(1)}, bf16[4,64,2048]{2,1,0:T(8,128)(2,1)S(1)}, u32[]{:S(2)}, u32[]{:S(2)}) collective-permute-start(bf16[4,64,2048]{2,1,0:T(8,128)(2,1)S(1)} %slice.75), channel_id=1, source_target_pairs={{0,24},{1,25},{2,26},{3,27},{4,28},{5,29},{6,30},{7,31},{8,0},{9,1... | collective-permute-start | bytes 3145736 | tf_op jit(solution)/shard_map/ppermute | solution.py:74
  145.8 31.9 %collective-permute-start.8 = (f32[2,3,64,128]{3,2,1,0:T(8,128)S(1)}, f32[2,3,64,128]{3,2,1,0:T(8,128)S(1)}, u32[]{:S(2)}, u32[]{:S(2)}) collective-permute-start(f32[2,3,64,128]{3,2,1,0:T(8,128)S(1)} %get-tuple-element.39), channel_id=1, source_target_pairs={{0,8},{1,9},{2,10},{3,11},{4,12},{5,13},{6,14},{7,15},{8,16},{9,17... | collective-permute-start | bytes 589832 | tf_op jit(solution)/shard_map/ppermute | solution.py:74
  148.9 28.9 %collective-permute-start.9 = (f32[2,3,64,128]{3,2,1,0:T(8,128)S(1)}, f32[2,3,64,128]{3,2,1,0:T(8,128)S(1)}, u32[]{:S(2)}, u32[]{:S(2)}) collective-permute-start(f32[2,3,64,128]{3,2,1,0:T(8,128)S(1)} %get-tuple-element.40), channel_id=1, source_target_pairs={{0,16},{1,17},{2,18},{3,19},{4,20},{5,21},{6,22},{7,23},{8,24},{9,... | collective-permute-start | bytes 589832 | tf_op jit(solution)/shard_map/ppermute | solution.py:74
  150.8 27.0 %collective-permute-start.10 = (f32[2,3,64,128]{3,2,1,0:T(8,128)S(1)}, f32[2,3,64,128]{3,2,1,0:T(8,128)S(1)}, u32[]{:S(2)}, u32[]{:S(2)}) collective-permute-start(f32[2,3,64,128]{3,2,1,0:T(8,128)S(1)} %get-tuple-element.37), channel_id=1, source_target_pairs={{0,24},{1,25},{2,26},{3,27},{4,28},{5,29},{6,30},{7,31},{8,0},{9,1... | collective-permute-start | bytes 589832 | tf_op jit(solution)/shard_map/ppermute | solution.py:74
  164.4 1.4 copy-start.3
  167.6 0.9 copy-start.2
  168.5 13.9 %copy-start.1 = (bf16[2,64,2048]{2,1,0:T(8,128)(2,1)S(1)}, bf16[2,64,2048]{2,1,0:T(8,128)(2,1)}, u32[]{:S(2)}) copy-start(bf16[2,64,2048]{2,1,0:T(8,128)(2,1)} %param.10) | copy-start | bytes 1572868
  175.7 5.0 %collective-permute-start.14 = (f32[3,64,128]{2,1,0:T(8,128)}, f32[3,64,128]{2,1,0:T(8,128)S(1)}, u32[]{:S(2)}, u32[]{:S(2)}) collective-permute-start(f32[3,64,128]{2,1,0:T(8,128)} %get-tuple-element.30), channel_id=1, source_target_pairs={{0,32},{1,33},{2,34},{3,35},{4,36},{5,37},{6,38},{7,39},{8,40},{9,... | collective-permute-start | bytes 294920 | tf_op jit(solution)/shard_map/ppermute | solution.py:74
  177.8 0.7 copy-start.5
  177.8 0.7 copy-start.6
  177.8 0.8 copy-start.7

commit v6 on v5

--- a/solution.py
+++ b/solution.py
@@ -139,9 +139,11 @@
             y_now = jnp.where(core == 0, b_now, a_now)
             places.append(y_now * 8 + z_now * 4 + x_now)
     lane = lax.broadcasted_iota(jnp.int32, (64, 128), 1)
-    for k in order:
-        for copy in copies(k):
-            copy.wait()
+    for position, k in enumerate(order):
+        if position % 3 == 0:
+            for later in order[position : position + 3]:
+                for copy in copies(later):
+                    copy.wait()
         gathered = jnp.concatenate([right[k, place] for place in places], axis=0)
         full = lax.dot_general(
             image[k], gathered, (((0,), (0,)), ((), ())), preferred_element_type=jnp.float32

time: 183 us -> 182 us (level)
  transfers between devices with their start and end apart: 18 -> 18, of which waited for: 7 -> 7; matrix products, arithmetic and copies ran while one was open for 22% -> 22% of each run, Pallas kernels for 10% -> 9%
where the time goes in v6:
time: 182 us; the launch traced here: 181 us
  starting transfers between devices  63.6 us (35%)
  waiting for transfers between devices  52.1 us (29%)
  local copies, waits for them, and re-layouts  30.2 us (17%)
  Pallas kernels  17 us (9%)
  other arithmetic  11.4 us (6%)
  matrix products  3.99 us (2%)
  between operations  2.62 us (1%)
    ppermute x15, waiting for transfers between devices, send(): return lax.ppermute(array, AXES, pairs)  48.1 us
    ppermute x15, starting transfers between devices, send(): return lax.ppermute(array, AXES, pairs)  42.7 us
    all_to_all x3, starting transfers between devices, spread(): lax.all_to_all(packed, 'ga', split_axis=0, concat_axis=0, tiled=True, axi...  20.9 us
    pallas_call x2, Pallas kernels, image_of(): pl.pallas_call(image_kernel, out_shape=jax.ShapeDtypeStruct((6, count, 12...  9.31 us
    unnamed x25, local copies, waits for them, and re-layouts  7.57 us
    pallas_call x1, Pallas kernels, direct_of(): pl.pallas_call(direct_kernel, out_shape=(shape, shape), in_specs=[pl.Bloc...  5.67 us
    dynamic_slice x2, local copies, waits for them, and re-layouts, both_cores(): mine = lax.dynamic_index_in_dim(dens, core, 0, keepdims=False)  5.15 us
    transpose x1, local copies, waits for them, and re-layouts, local(): valence = jnp.transpose(valence, (0, 2, 1, 3)).reshape(2048, 768)  4.8 us
  transfers between devices with their start and end apart: 18, of which 7 were waited for; matrix products, arithmetic and copies ran while one was open for 22% of the time, Pallas kernels for 9%

profile of v6, /device:TPU:35, one launch (start us, length us, event | category | flops | bytes accessed | tf_op | source)
XLA Modules:
  0.0 180.9 jit_solution(17118717118162562954)
XLA Ops:
  0.0 1.0 copy-done
  1.1 0.1 collective-permute-start
  1.2 1.2 slice.77
  2.3 0.9 slice.76
  3.2 0.7 fusion.24
  3.9 0.2 pad_maximum_fusion.3
  4.1 0.1 copy.23
  4.3 1.6 pad_maximum_fusion.2
  5.9 2.4 %collective-permute-done = bf16[1,64,2048]{2,1,0:T(8,128)(2,1)S(1)} collective-permute-done((bf16[1,64,2048]{2,1,0:T(8,128)(2,1)S(1)}, bf16[1,64,2048]{2,1,0:T(8,128)(2,1)S(1)}, u32[]{:S(2)}, u32[]{:S(2)}) %collective-permute-start) | collective-permute-done | bytes 262176 | tf_op jit(solution)/shard_map/ppermute | solution.py:74
  8.4 5.2 %all-to-all-start = ((bf16[8,17,64,128]{3,2,1,0:T(8,128)(2,1)}), bf16[8,17,64,128]{3,2,1,0:T(8,128)(2,1)}, u32[]{:S(2)}, u32[]{:S(2)}) async-start(bf16[8,17,64,128]{3,2,1,0:T(8,128)(2,1)} %pad_maximum_fusion.2), calls=%async_computation | async-start | bytes 4456448 | tf_op jit(solution)/shard_map/all_to_all | solution.py:255
  13.6 2.6 %constant_dynamic-slice_fusion.2 = (bf16[1,96,64,128]{3,2,1,0:T(8,128)(2,1)S(1)}, bf16[96,64,128]{2,1,0:T(8,128)(2,1)S(1)}) fusion(bf16[2,96,64,128]{3,2,1,0:T(8,128)(2,1)} %param.9, s32[]{:T(128)S(6)} %select_n.75, s32[]{:T(128)S(6)} %select_n.76), kind=kLoop, calls=%fused_computation.54 | loop fusion | bytes 6291464 | tf_op jit(solution)/shard_map/jit(dynamic_index_in_dim)/dynamic_slice | solution.py:248
  16.1 2.2 %collective-permute-start.2 = (bf16[96,64,128]{2,1,0:T(8,128)(2,1)S(1)}, bf16[96,64,128]{2,1,0:T(8,128)(2,1)S(1)}, u32[]{:S(2)}, u32[]{:S(2)}) collective-permute-start(bf16[96,64,128]{2,1,0:T(8,128)(2,1)S(1)} %get-tuple-element.34), channel_id=1, source_target_pairs={{0,32},{1,33},{2,34},{3,35},{4,36},{5,37},{6,38},{7,39},{8,40},{9,... | collective-permute-start | bytes 4718600 | tf_op jit(solution)/shard_map/ppermute | solution.py:74
  18.3 1.3 collective-permute-start.3
  19.6 1.4 collective-permute-start.4
  21.1 1.6 collective-permute-start.5
  22.7 2.0 %pad_maximum_fusion = bf16[32,6,64,128]{3,2,1,0:T(8,128)(2,1)} fusion(bf16[32,3,64,128]{3,2,1,0:T(8,128)(2,1)S(1)} %bitcast.70, bf16[32,3,64,128]{3,2,1,0:T(8,128)(2,1)S(1)} %bitcast.65), kind=kLoop, calls=%fused_computation.1 | loop fusion | flops 1572864 | bytes 6291456 | tf_op jit(solution)/shard_map/concatenate | solution.py:251
  24.7 3.2 %collective-permute-done.3 = bf16[2,64,2048]{2,1,0:T(8,128)(2,1)S(1)} collective-permute-done((bf16[2,64,2048]{2,1,0:T(8,128)(2,1)S(1)}, bf16[2,64,2048]{2,1,0:T(8,128)(2,1)S(1)}, u32[]{:S(2)}, u32[]{:S(2)}) %collective-permute-start.3) | collective-permute-done | bytes 524320 | tf_op jit(solution)/shard_map/ppermute | solution.py:74
  27.9 0.2 collective-permute-done.4
  28.0 6.5 %collective-permute-done.5 = bf16[2,64,2048]{2,1,0:T(8,128)(2,1)} collective-permute-done((bf16[2,64,2048]{2,1,0:T(8,128)(2,1)S(1)}, bf16[2,64,2048]{2,1,0:T(8,128)(2,1)}, u32[]{:S(2)}, u32[]{:S(2)}) %collective-permute-start.5) | collective-permute-done | bytes 524320 | tf_op jit(solution)/shard_map/ppermute | solution.py:74
  34.5 4.0 %all-to-all-done = bf16[8,17,64,128]{3,2,1,0:T(8,128)(2,1)} async-done(((bf16[8,17,64,128]{3,2,1,0:T(8,128)(2,1)}), bf16[8,17,64,128]{3,2,1,0:T(8,128)(2,1)}, u32[]{:S(2)}, u32[]{:S(2)}) %all-to-all-start) | async-done | bytes 2228256 | tf_op jit(solution)/shard_map/all_to_all | solution.py:255
  38.5 9.0 %all-to-all-start.1 = ((bf16[32,6,64,128]{3,2,1,0:T(8,128)(2,1)}), bf16[32,6,64,128]{3,2,1,0:T(8,128)(2,1)}, u32[]{:S(2)}, u32[]{:S(2)}) async-start(bf16[32,6,64,128]{3,2,1,0:T(8,128)(2,1)} %pad_maximum_fusion), calls=%async_computation.1 | async-start | bytes 6291456 | tf_op jit(solution)/shard_map/all_to_all | solution.py:255
  47.5 2.6 %constant_dynamic-slice_fusion = (bf16[1,96,64,128]{3,2,1,0:T(8,128)(2,1)S(1)}, bf16[96,64,128]{2,1,0:T(8,128)(2,1)S(1)}) fusion(bf16[2,96,64,128]{3,2,1,0:T(8,128)(2,1)} %param.8, s32[]{:T(128)S(6)} %select_n.75, s32[]{:T(128)S(6)} %select_n.76), kind=kLoop, calls=%fused_computation.51 | loop fusion | bytes 6291464 | tf_op jit(solution)/shard_map/jit(dynamic_index_in_dim)/dynamic_slice | solution.py:248
  50.1 15.2 %collective-permute-start.11 = (bf16[96,64,128]{2,1,0:T(8,128)(2,1)S(1)}, bf16[96,64,128]{2,1,0:T(8,128)(2,1)S(1)}, u32[]{:S(2)}, u32[]{:S(2)}) collective-permute-start(bf16[96,64,128]{2,1,0:T(8,128)(2,1)S(1)} %get-tuple-element.32), channel_id=1, source_target_pairs={{0,32},{1,33},{2,34},{3,35},{4,36},{5,37},{6,38},{7,39},{8,40},{9,... | collective-permute-start | bytes 4718600 | tf_op jit(solution)/shard_map/ppermute | solution.py:74
  65.4 0.8 constant_dynamic-update-slice_fusion.3
  66.2 0.8 constant_dynamic-update-slice_fusion.2
  67.0 0.8 constant_dynamic-update-slice_fusion.1
  67.9 1.9 %constant_dynamic-update-slice_fusion.refs_0_ = bf16[8,64,2048]{2,1,0:T(8,128)(2,1)} fusion(bf16[8,64,2048]{2,1,0:T(8,128)(2,1)} %constant_dynamic-update-slice_fusion.1, bf16[2,64,2048]{2,1,0:T(8,128)(2,1)} %collective-permute-done.5), kind=kLoop, calls=%fused_computation.47 | loop fusion | bytes 1048576 | tf_op jit(solution)/shard_map/concatenate | solution.py:277
  69.8 1.2 collective-permute-start.6
  70.9 0.3 collective-permute-start.7
  71.2 1.8 slice.79
  73.0 1.5 copy.18
  74.5 1.8 collective-permute-start.1
  76.3 2.0 %pad_maximum_fusion.1 = bf16[32,6,64,128]{3,2,1,0:T(8,128)(2,1)} fusion(bf16[32,3,64,128]{3,2,1,0:T(8,128)(2,1)S(1)} %bitcast.69, bf16[32,3,64,128]{3,2,1,0:T(8,128)(2,1)S(1)} %bitcast.64), kind=kLoop, calls=%fused_computation.4 | loop fusion | flops 1572864 | bytes 6291456 | tf_op jit(solution)/shard_map/concatenate | solution.py:251
  78.3 6.7 %all-to-all-start.2 = ((bf16[32,6,64,128]{3,2,1,0:T(8,128)(2,1)}), bf16[32,6,64,128]{3,2,1,0:T(8,128)(2,1)}, u32[]{:S(2)}, u32[]{:S(2)}) async-start(bf16[32,6,64,128]{3,2,1,0:T(8,128)(2,1)} %pad_maximum_fusion.1), calls=%async_computation.2 | async-start | bytes 6291456 | tf_op jit(solution)/shard_map/all_to_all | solution.py:255
  85.0 0.6 slice.58
  86.2 0.5 constant_dynamic-slice_fusion.1
  88.5 0.6 pad_add_fusion.pos_ref
  89.0 1.5 slice.80
  90.6 1.1 convert_reduce_fusion
  91.6 19.5 %collective-permute-done.6.refs_1_ = bf16[8,64,2048]{2,1,0:T(8,128)(2,1)S(1)} collective-permute-done((bf16[8,64,2048]{2,1,0:T(8,128)(2,1)}, bf16[8,64,2048]{2,1,0:T(8,128)(2,1)S(1)}, u32[]{:S(2)}, u32[]{:S(2)}) %collective-permute-start.6) | collective-permute-done | bytes 2097184 | tf_op jit(solution)/shard_map/ppermute | solution.py:74
  111.1 16.3 %collective-permute-done.1 = bf16[8,4,4,64,128]{4,3,0,2,1:T(8,128)(2,1)} collective-permute-done((bf16[8,4,4,64,128]{4,3,0,2,1:T(8,128)(2,1)}, bf16[8,4,4,64,128]{4,3,0,2,1:T(8,128)(2,1)}, u32[]{:S(2)}, u32[]{:S(2)}) %collective-permute-start.1) | collective-permute-done | bytes 2097184 | tf_op jit(solution)/shard_map/ppermute | solution.py:74
  127.4 1.5 slice.69
  129.0 9.9 %collective-permute-start.12 = (bf16[4,64,2048]{2,1,0:T(8,128)(2,1)S(1)}, bf16[4,64,2048]{2,1,0:T(8,128)(2,1)S(1)}, u32[]{:S(2)}, u32[]{:S(2)}) collective-permute-start(bf16[4,64,2048]{2,1,0:T(8,128)(2,1)S(1)} %slice.74), channel_id=1, source_target_pairs={{0,8},{1,9},{2,10},{3,11},{4,12},{5,13},{6,14},{7,15},{8,16},{9,17... | collective-permute-start | bytes 3145736 | tf_op jit(solution)/shard_map/ppermute | solution.py:74
  138.9 1.3 slice.75
  140.3 2.7 %fusion.5 = f32[4,3,128,128]{3,2,1,0:T(8,128)S(1)} fusion(bf16[8,4,4,64,128]{4,3,0,2,1:T(8,128)(2,1)} %collective-permute-done.1, f32[8,64]{1,0:T(8,128)S(1)} %convert_reduce_fusion, bf16[8,4,4,64,128]{4,3,0,2,1:T(8,128)(2,1)} %bitcast.7), kind=kOutput, calls=%fused_computation.14 | convolution fusion | flops 203685888 | bytes 3934208 | tf_op jit(solution)/shard_map/sabgp,sabgq->abpq/dot_general | solution.py:228
  143.0 1.3 fusion.8
  144.3 0.5 fusion.12
  144.8 0.3 broadcast_select_fusion
  145.1 0.8 fusion.16
  145.8 3.1 %collective-permute-start.8 = (f32[2,3,64,128]{3,2,1,0:T(8,128)S(1)}, f32[2,3,64,128]{3,2,1,0:T(8,128)S(1)}, u32[]{:S(2)}, u32[]{:S(2)}) collective-permute-start(f32[2,3,64,128]{3,2,1,0:T(8,128)S(1)} %get-tuple-element.39), channel_id=1, source_target_pairs={{0,8},{1,9},{2,10},{3,11},{4,12},{5,13},{6,14},{7,15},{8,16},{9,17... | collective-permute-start | bytes 589832 | tf_op jit(solution)/shard_map/ppermute | solution.py:74
  148.9 1.9 %collective-permute-start.9 = (f32[2,3,64,128]{3,2,1,0:T(8,128)S(1)}, f32[2,3,64,128]{3,2,1,0:T(8,128)S(1)}, u32[]{:S(2)}, u32[]{:S(2)}) collective-permute-start(f32[2,3,64,128]{3,2,1,0:T(8,128)S(1)} %get-tuple-element.40), channel_id=1, source_target_pairs={{0,16},{1,17},{2,18},{3,19},{4,20},{5,21},{6,22},{7,23},{8,24},{9,... | collective-permute-start | bytes 589832 | tf_op jit(solution)/shard_map/ppermute | solution.py:74
  150.8 0.5 collective-permute-start.10
  151.3 4.8 %copy.19 = bf16[32,64,6,128]{3,2,1,0:T(8,128)(2,1)S(1)} copy(bf16[32,64,6,128]{3,1,2,0:T(8,128)(2,1)} %bitcast.33) | data formatting | bytes 6291456 | tf_op jit(solution)/shard_map/transpose | solution.py:292
  156.1 0.8 copy.28
  156.9 7.5 %shard_map.65.near_ref = bf16[6,1536,128]{2,1,0:T(8,128)(2,1)S(1)} custom-call(bf16[8,64,2048]{2,1,0:T(8,128)(2,1)} %constant_dynamic-update-slice_fusion.refs_0_, bf16[8,64,2048]{2,1,0:T(8,128)(2,1)S(1)} %collective-permute-done.6.refs_1_, bf16[8,64,2048]{2,1,0:T(8,128)(2,1)} %collective-permute-done.7.refs_2_, bf16[2048,768]{1,0:T(8,128)(2,1)S(1)} %bitcast.60), custom_call_target="tpu_custom_call" | custom-call | flops 4831838208 | bytes 11796480 | tf_op jit(solution)/shard_map/pallas_call | solution.py:93
  164.4 1.4 copy-done.3
  165.8 1.8 %shard_map.66.far_ref = bf16[6,512,128]{2,1,0:T(8,128)(2,1)S(1)} custom-call(bf16[4,64,2048]{2,1,0:T(8,128)(2,1)S(1)} %collective-permute-done.12.refs_0_, bf16[4,64,2048]{2,1,0:T(8,128)(2,1)S(1)} %collective-permute-done.13.refs_1_, bf16[2048,768]{1,0:T(8,128)(2,1)S(1)} %bitcast.61), custom_call_target="tpu_custom_call" | custom-call | flops 1610612736 | bytes 6029312 | tf_op jit(solution)/shard_map/pallas_call | solution.py:93
  167.6 0.9 copy-done.2
  168.5 5.7 %shard_map.67 = (f32[3,64,128]{2,1,0:T(8,128)}, f32[3,64,128]{2,1,0:T(8,128)}) custom-call(s32[4]{0:T(128)} %pad_add_fusion.pos_ref, bf16[6,1536,128]{2,1,0:T(8,128)(2,1)} %copy-done.3, bf16[6,512,128]{2,1,0:T(8,128)(2,1)} %copy-done.2, bf16[32,6,64,128]{3,2,1,0:T(8,128)(2,1)} %all-to-all-done.2.conduction_ref), custom_call_target="tpu_custom_call" | custom-call | flops 402653184 | bytes 7340032 | tf_op jit(solution)/shard_map/pallas_call | solution.py:164
  174.2 2.1 %collective-permute-start.14 = (f32[3,64,128]{2,1,0:T(8,128)}, f32[3,64,128]{2,1,0:T(8,128)S(1)}, u32[]{:S(2)}, u32[]{:S(2)}) collective-permute-start(f32[3,64,128]{2,1,0:T(8,128)} %get-tuple-element.30), channel_id=1, source_target_pairs={{0,32},{1,33},{2,34},{3,35},{4,36},{5,37},{6,38},{7,39},{8,40},{9,... | collective-permute-start | bytes 294920 | tf_op jit(solution)/shard_map/ppermute | solution.py:74
  176.3 0.6 copy-done.5
  176.9 0.1 copy-done.6
  177.1 2.1 %shard_map.64 = f32[2,3,64,128]{3,2,1,0:T(8,128)} custom-call(f32[2,3,64,128]{3,2,1,0:T(8,128)} %get-tuple-element.38.first_ref, f32[2,3,64,128]{3,2,1,0:T(8,128)} %copy-done.5, f32[2,3,64,128]{3,2,1,0:T(8,128)} %copy-done.6, f32[2,3,64,128]{3,2,1,0:T(8,128)} %copy-done.7), custom_call_target="tpu_custom_call" | custom-call | tf_op jit(solution)/shard_map/pallas_call | solution.py:192
  179.2 1.8 select_subtract_fusion
  (34 shorter events, 0.4 us)
Async XLA Ops:
  0.0 1.0 copy-start
  1.0 2.8 %copy-start.4 = (bf16[96,64,128]{2,1,0:T(8,128)(2,1)S(1)}, bf16[96,64,128]{2,1,0:T(8,128)(2,1)}, u32[]{:S(2)}) copy-start(bf16[96,64,128]{2,1,0:T(8,128)(2,1)} %param.6) | copy-start | bytes 4718596
  1.1 7.3 %collective-permute-start = (bf16[1,64,2048]{2,1,0:T(8,128)(2,1)S(1)}, bf16[1,64,2048]{2,1,0:T(8,128)(2,1)S(1)}, u32[]{:S(2)}, u32[]{:S(2)}) collective-permute-start(bf16[1,64,2048]{2,1,0:T(8,128)(2,1)S(1)} %constant_dynamic-slice_fusion.3), channel_id=1, source_target_pairs={{0,4},{1,5},{2,6},{3,7},{4,0},{5,1},{6,2},{7,3},{8,12},{9,13},{10,... | collective-permute-start | bytes 786440 | tf_op jit(solution)/shard_map/ppermute | solution.py:74
  8.4 30.2 %all-to-all-start = ((bf16[8,17,64,128]{3,2,1,0:T(8,128)(2,1)}), bf16[8,17,64,128]{3,2,1,0:T(8,128)(2,1)}, u32[]{:S(2)}, u32[]{:S(2)}) async-start(bf16[8,17,64,128]{3,2,1,0:T(8,128)(2,1)} %pad_maximum_fusion.2), calls=%async_computation | async-start | bytes 4456448 | tf_op jit(solution)/shard_map/all_to_all | solution.py:255
  16.1 6.6 %collective-permute-start.2 = (bf16[96,64,128]{2,1,0:T(8,128)(2,1)S(1)}, bf16[96,64,128]{2,1,0:T(8,128)(2,1)S(1)}, u32[]{:S(2)}, u32[]{:S(2)}) collective-permute-start(bf16[96,64,128]{2,1,0:T(8,128)(2,1)S(1)} %get-tuple-element.34), channel_id=1, source_target_pairs={{0,32},{1,33},{2,34},{3,35},{4,36},{5,37},{6,38},{7,39},{8,40},{9,... | collective-permute-start | bytes 4718600 | tf_op jit(solution)/shard_map/ppermute | solution.py:74
  18.3 9.5 %collective-permute-start.3 = (bf16[2,64,2048]{2,1,0:T(8,128)(2,1)S(1)}, bf16[2,64,2048]{2,1,0:T(8,128)(2,1)S(1)}, u32[]{:S(2)}, u32[]{:S(2)}) collective-permute-start(bf16[2,64,2048]{2,1,0:T(8,128)(2,1)S(1)} %pad_maximum_fusion.4), channel_id=1, source_target_pairs={{0,1},{1,2},{2,3},{3,0},{4,5},{5,6},{6,7},{7,4},{8,9},{9,10},{10,1... | collective-permute-start | bytes 1572872 | tf_op jit(solution)/shard_map/ppermute | solution.py:74
  19.6 8.4 %collective-permute-start.4 = (bf16[2,64,2048]{2,1,0:T(8,128)(2,1)S(1)}, bf16[2,64,2048]{2,1,0:T(8,128)(2,1)S(1)}, u32[]{:S(2)}, u32[]{:S(2)}) collective-permute-start(bf16[2,64,2048]{2,1,0:T(8,128)(2,1)S(1)} %pad_maximum_fusion.4), channel_id=1, source_target_pairs={{0,3},{1,0},{2,1},{3,2},{4,7},{5,4},{6,5},{7,6},{8,11},{9,8},{10,9... | collective-permute-start | bytes 1572872 | tf_op jit(solution)/shard_map/ppermute | solution.py:74
  21.1 13.5 %collective-permute-start.5 = (bf16[2,64,2048]{2,1,0:T(8,128)(2,1)S(1)}, bf16[2,64,2048]{2,1,0:T(8,128)(2,1)}, u32[]{:S(2)}, u32[]{:S(2)}) collective-permute-start(bf16[2,64,2048]{2,1,0:T(8,128)(2,1)S(1)} %pad_maximum_fusion.4), channel_id=1, source_target_pairs={{0,2},{1,3},{2,0},{3,1},{4,6},{5,7},{6,4},{7,5},{8,10},{9,11},{10,... | collective-permute-start | bytes 1572872 | tf_op jit(solution)/shard_map/ppermute | solution.py:74
  38.5 39.8 %all-to-all-start.1 = ((bf16[32,6,64,128]{3,2,1,0:T(8,128)(2,1)}), bf16[32,6,64,128]{3,2,1,0:T(8,128)(2,1)}, u32[]{:S(2)}, u32[]{:S(2)}) async-start(bf16[32,6,64,128]{3,2,1,0:T(8,128)(2,1)} %pad_maximum_fusion), calls=%async_computation.1 | async-start | bytes 6291456 | tf_op jit(solution)/shard_map/all_to_all | solution.py:255
  50.1 26.2 %collective-permute-start.11 = (bf16[96,64,128]{2,1,0:T(8,128)(2,1)S(1)}, bf16[96,64,128]{2,1,0:T(8,128)(2,1)S(1)}, u32[]{:S(2)}, u32[]{:S(2)}) collective-permute-start(bf16[96,64,128]{2,1,0:T(8,128)(2,1)S(1)} %get-tuple-element.32), channel_id=1, source_target_pairs={{0,32},{1,33},{2,34},{3,35},{4,36},{5,37},{6,38},{7,39},{8,40},{9,... | collective-permute-start | bytes 4718600 | tf_op jit(solution)/shard_map/ppermute | solution.py:74
  69.8 41.3 %collective-permute-start.6 = (bf16[8,64,2048]{2,1,0:T(8,128)(2,1)}, bf16[8,64,2048]{2,1,0:T(8,128)(2,1)S(1)}, u32[]{:S(2)}, u32[]{:S(2)}) collective-permute-start(bf16[8,64,2048]{2,1,0:T(8,128)(2,1)} %constant_dynamic-update-slice_fusion.refs_0_), channel_id=1, source_target_pairs={{0,8},{1,9},{2,10},{3,11},{4,12},{5,13},{6,14},{7,15},{8,16},{9,17... | collective-permute-start | bytes 6291464 | tf_op jit(solution)/shard_map/ppermute | solution.py:74
  70.9 40.1 %collective-permute-start.7 = (bf16[8,64,2048]{2,1,0:T(8,128)(2,1)}, bf16[8,64,2048]{2,1,0:T(8,128)(2,1)}, u32[]{:S(2)}, u32[]{:S(2)}) collective-permute-start(bf16[8,64,2048]{2,1,0:T(8,128)(2,1)} %constant_dynamic-update-slice_fusion.refs_0_), channel_id=1, source_target_pairs={{0,24},{1,25},{2,26},{3,27},{4,28},{5,29},{6,30},{7,31},{8,0},{9,1... | collective-permute-start | bytes 6291464 | tf_op jit(solution)/shard_map/ppermute | solution.py:74
  74.5 52.9 %collective-permute-start.1 = (bf16[8,4,4,64,128]{4,3,0,2,1:T(8,128)(2,1)}, bf16[8,4,4,64,128]{4,3,0,2,1:T(8,128)(2,1)}, u32[]{:S(2)}, u32[]{:S(2)}) collective-permute-start(bf16[8,4,4,64,128]{4,3,0,2,1:T(8,128)(2,1)} %bitcast.7), channel_id=1, source_target_pairs={{0,96},{1,97},{2,98},{3,99},{4,100},{5,101},{6,102},{7,103},{8,104... | collective-permute-start | bytes 6291464 | tf_op jit(solution)/shard_map/ppermute | solution.py:74
  78.3 6.7 %copy-start.8 = (s32[2,2]{1,0:T(2,128)S(1)}, s32[2,2]{1,0:T(2,128)}, u32[]{:S(2)}) copy-start(s32[2,2]{1,0:T(2,128)} %param.11) | copy-start | bytes 52
  78.3 90.2 %all-to-all-start.2 = ((bf16[32,6,64,128]{3,2,1,0:T(8,128)(2,1)}), bf16[32,6,64,128]{3,2,1,0:T(8,128)(2,1)}, u32[]{:S(2)}, u32[]{:S(2)}) async-start(bf16[32,6,64,128]{3,2,1,0:T(8,128)(2,1)} %pad_maximum_fusion.1), calls=%async_computation.2 | async-start | bytes 6291456 | tf_op jit(solution)/shard_map/all_to_all | solution.py:255
  129.0 36.8 %collective-permute-start.12 = (bf16[4,64,2048]{2,1,0:T(8,128)(2,1)S(1)}, bf16[4,64,2048]{2,1,0:T(8,128)(2,1)S(1)}, u32[]{:S(2)}, u32[]{:S(2)}) collective-permute-start(bf16[4,64,2048]{2,1,0:T(8,128)(2,1)S(1)} %slice.74), channel_id=1, source_target_pairs={{0,8},{1,9},{2,10},{3,11},{4,12},{5,13},{6,14},{7,15},{8,16},{9,17... | collective-permute-start | bytes 3145736 | tf_op jit(solution)/shard_map/ppermute | solution.py:74
  140.2 25.6 %collective-permute-start.13 = (bf16[4,64,2048]{2,1,0:T(8,128)(2,1)S(1)}, bf16[4,64,2048]{2,1,0:T(8,128)(2,1)S(1)}, u32[]{:S(2)}, u32[]{:S(2)}) collective-permute-start(bf16[4,64,2048]{2,1,0:T(8,128)(2,1)S(1)} %slice.75), channel_id=1, source_target_pairs={{0,24},{1,25},{2,26},{3,27},{4,28},{5,29},{6,30},{7,31},{8,0},{9,1... | collective-permute-start | bytes 3145736 | tf_op jit(solution)/shard_map/ppermute | solution.py:74
  145.8 30.4 %collective-permute-start.8 = (f32[2,3,64,128]{3,2,1,0:T(8,128)S(1)}, f32[2,3,64,128]{3,2,1,0:T(8,128)S(1)}, u32[]{:S(2)}, u32[]{:S(2)}) collective-permute-start(f32[2,3,64,128]{3,2,1,0:T(8,128)S(1)} %get-tuple-element.39), channel_id=1, source_target_pairs={{0,8},{1,9},{2,10},{3,11},{4,12},{5,13},{6,14},{7,15},{8,16},{9,17... | collective-permute-start | bytes 589832 | tf_op jit(solution)/shard_map/ppermute | solution.py:74
  148.9 27.4 %collective-permute-start.9 = (f32[2,3,64,128]{3,2,1,0:T(8,128)S(1)}, f32[2,3,64,128]{3,2,1,0:T(8,128)S(1)}, u32[]{:S(2)}, u32[]{:S(2)}) collective-permute-start(f32[2,3,64,128]{3,2,1,0:T(8,128)S(1)} %get-tuple-element.40), channel_id=1, source_target_pairs={{0,16},{1,17},{2,18},{3,19},{4,20},{5,21},{6,22},{7,23},{8,24},{9,... | collective-permute-start | bytes 589832 | tf_op jit(solution)/shard_map/ppermute | solution.py:74
  150.8 25.5 %collective-permute-start.10 = (f32[2,3,64,128]{3,2,1,0:T(8,128)S(1)}, f32[2,3,64,128]{3,2,1,0:T(8,128)S(1)}, u32[]{:S(2)}, u32[]{:S(2)}) collective-permute-start(f32[2,3,64,128]{3,2,1,0:T(8,128)S(1)} %get-tuple-element.37), channel_id=1, source_target_pairs={{0,24},{1,25},{2,26},{3,27},{4,28},{5,29},{6,30},{7,31},{8,0},{9,1... | collective-permute-start | bytes 589832 | tf_op jit(solution)/shard_map/ppermute | solution.py:74
  164.4 1.4 copy-start.3
  167.6 0.9 copy-start.2
  168.5 12.4 %copy-start.1 = (bf16[2,64,2048]{2,1,0:T(8,128)(2,1)S(1)}, bf16[2,64,2048]{2,1,0:T(8,128)(2,1)}, u32[]{:S(2)}) copy-start(bf16[2,64,2048]{2,1,0:T(8,128)(2,1)} %param.10) | copy-start | bytes 1572868
  174.2 5.0 %collective-permute-start.14 = (f32[3,64,128]{2,1,0:T(8,128)}, f32[3,64,128]{2,1,0:T(8,128)S(1)}, u32[]{:S(2)}, u32[]{:S(2)}) collective-permute-start(f32[3,64,128]{2,1,0:T(8,128)} %get-tuple-element.30), channel_id=1, source_target_pairs={{0,32},{1,33},{2,34},{3,35},{4,36},{5,37},{6,38},{7,39},{8,40},{9,... | collective-permute-start | bytes 294920 | tf_op jit(solution)/shard_map/ppermute | solution.py:74
  176.3 0.7 copy-start.5
  176.3 0.7 copy-start.6
  176.3 0.8 copy-start.7

commit v7 on v6

--- a/solution.py
+++ b/solution.py
@@ -285,8 +285,8 @@
 
     conduction = both_cores(dens_cc, core)
     conduction, valence = after((conduction, valence))
+    far_low, far_high = send(behind[:4], along_second(1)), send(ahead[4:], along_second(-1))
     next_rows, behind, ahead = after((next_rows, behind, ahead))
-    far_low, far_high = send(behind[:4], along_second(1)), send(ahead[4:], along_second(-1))
     conduction = spread(conduction)
 
     valence = jnp.transpose(valence, (0, 2, 1, 3)).reshape(2048, 768)

time: 182 us -> 180 us (0.989)
  starting transfers between devices: 63.6 us -> 60.5 us
    ppermute x15, starting transfers between devices: 42.7 us -> 39.7 us  [send(): return lax.ppermute(array, AXES, pairs)]
  transfers between devices with their start and end apart: 18 -> 18, of which waited for: 7 -> 8; matrix products, arithmetic and copies ran while one was open for 22% -> 22% of each run, Pallas kernels for 9% -> 9%
where the time goes in v7:
time: 180 us
  starting transfers between devices  60.5 us (34%)
  waiting for transfers between devices  53.8 us (30%)
  local copies, waits for them, and re-layouts  30.2 us (17%)
  Pallas kernels  17 us (9%)
  other arithmetic  11.4 us (6%)
  matrix products  3.99 us (2%)
  between operations  2.62 us (1%)
    ppermute x15, waiting for transfers between devices, send(): return lax.ppermute(array, AXES, pairs)  49.8 us
    ppermute x15, starting transfers between devices, send(): return lax.ppermute(array, AXES, pairs)  39.7 us
    all_to_all x3, starting transfers between devices, spread(): lax.all_to_all(packed, 'ga', split_axis=0, concat_axis=0, tiled=True, axi...  20.9 us
    pallas_call x2, Pallas kernels, image_of(): pl.pallas_call(image_kernel, out_shape=jax.ShapeDtypeStruct((6, count, 12...  9.3 us
    unnamed x25, local copies, waits for them, and re-layouts  7.57 us
    pallas_call x1, Pallas kernels, direct_of(): pl.pallas_call(direct_kernel, out_shape=(shape, shape), in_specs=[pl.Bloc...  5.67 us
    dynamic_slice x2, local copies, waits for them, and re-layouts, both_cores(): mine = lax.dynamic_index_in_dim(dens, core, 0, keepdims=False)  5.15 us
    transpose x1, local copies, waits for them, and re-layouts, local(): valence = jnp.transpose(valence, (0, 2, 1, 3)).reshape(2048, 768)  4.8 us
  transfers between devices with their start and end apart: 18, of which 8 were waited for; matrix products, arithmetic and copies ran while one was open for 22% of the time, Pallas kernels for 9%

profile of v7, /device:TPU:35, one launch (start us, length us, event | category | flops | bytes accessed | tf_op | source)
XLA Modules:
  0.0 179.6 jit_solution(14716081463068589843)
XLA Ops:
  0.0 1.0 copy-done
  1.1 0.1 collective-permute-start
  1.2 1.2 slice.77
  2.3 0.9 slice.76
  3.2 0.7 fusion.24
  3.9 0.2 pad_maximum_fusion.3
  4.1 0.1 copy.23
  4.3 1.6 pad_maximum_fusion.2
  5.9 2.4 %collective-permute-done = bf16[1,64,2048]{2,1,0:T(8,128)(2,1)S(1)} collective-permute-done((bf16[1,64,2048]{2,1,0:T(8,128)(2,1)S(1)}, bf16[1,64,2048]{2,1,0:T(8,128)(2,1)S(1)}, u32[]{:S(2)}, u32[]{:S(2)}) %collective-permute-start) | collective-permute-done | bytes 262176 | tf_op jit(solution)/shard_map/ppermute | solution.py:74
  8.4 5.2 %all-to-all-start = ((bf16[8,17,64,128]{3,2,1,0:T(8,128)(2,1)}), bf16[8,17,64,128]{3,2,1,0:T(8,128)(2,1)}, u32[]{:S(2)}, u32[]{:S(2)}) async-start(bf16[8,17,64,128]{3,2,1,0:T(8,128)(2,1)} %pad_maximum_fusion.2), calls=%async_computation | async-start | bytes 4456448 | tf_op jit(solution)/shard_map/all_to_all | solution.py:255
  13.6 2.6 %constant_dynamic-slice_fusion.2 = (bf16[1,96,64,128]{3,2,1,0:T(8,128)(2,1)S(1)}, bf16[96,64,128]{2,1,0:T(8,128)(2,1)S(1)}) fusion(bf16[2,96,64,128]{3,2,1,0:T(8,128)(2,1)} %param.9, s32[]{:T(128)S(6)} %select_n.75, s32[]{:T(128)S(6)} %select_n.76), kind=kLoop, calls=%fused_computation.54 | loop fusion | bytes 6291464 | tf_op jit(solution)/shard_map/jit(dynamic_index_in_dim)/dynamic_slice | solution.py:248
  16.1 2.2 %collective-permute-start.2 = (bf16[96,64,128]{2,1,0:T(8,128)(2,1)S(1)}, bf16[96,64,128]{2,1,0:T(8,128)(2,1)S(1)}, u32[]{:S(2)}, u32[]{:S(2)}) collective-permute-start(bf16[96,64,128]{2,1,0:T(8,128)(2,1)S(1)} %get-tuple-element.34), channel_id=1, source_target_pairs={{0,32},{1,33},{2,34},{3,35},{4,36},{5,37},{6,38},{7,39},{8,40},{9,... | collective-permute-start | bytes 4718600 | tf_op jit(solution)/shard_map/ppermute | solution.py:74
  18.3 1.3 collective-permute-start.3
  19.6 1.4 collective-permute-start.4
  21.1 1.6 collective-permute-start.5
  22.7 2.0 %pad_maximum_fusion = bf16[32,6,64,128]{3,2,1,0:T(8,128)(2,1)} fusion(bf16[32,3,64,128]{3,2,1,0:T(8,128)(2,1)S(1)} %bitcast.70, bf16[32,3,64,128]{3,2,1,0:T(8,128)(2,1)S(1)} %bitcast.65), kind=kLoop, calls=%fused_computation.1 | loop fusion | flops 1572864 | bytes 6291456 | tf_op jit(solution)/shard_map/concatenate | solution.py:251
  24.7 3.2 %collective-permute-done.3 = bf16[2,64,2048]{2,1,0:T(8,128)(2,1)S(1)} collective-permute-done((bf16[2,64,2048]{2,1,0:T(8,128)(2,1)S(1)}, bf16[2,64,2048]{2,1,0:T(8,128)(2,1)S(1)}, u32[]{:S(2)}, u32[]{:S(2)}) %collective-permute-start.3) | collective-permute-done | bytes 524320 | tf_op jit(solution)/shard_map/ppermute | solution.py:74
  27.9 0.2 collective-permute-done.4
  28.0 6.5 %collective-permute-done.5 = bf16[2,64,2048]{2,1,0:T(8,128)(2,1)} collective-permute-done((bf16[2,64,2048]{2,1,0:T(8,128)(2,1)S(1)}, bf16[2,64,2048]{2,1,0:T(8,128)(2,1)}, u32[]{:S(2)}, u32[]{:S(2)}) %collective-permute-start.5) | collective-permute-done | bytes 524320 | tf_op jit(solution)/shard_map/ppermute | solution.py:74
  34.5 4.0 %all-to-all-done = bf16[8,17,64,128]{3,2,1,0:T(8,128)(2,1)} async-done(((bf16[8,17,64,128]{3,2,1,0:T(8,128)(2,1)}), bf16[8,17,64,128]{3,2,1,0:T(8,128)(2,1)}, u32[]{:S(2)}, u32[]{:S(2)}) %all-to-all-start) | async-done | bytes 2228256 | tf_op jit(solution)/shard_map/all_to_all | solution.py:255
  38.5 9.0 %all-to-all-start.1 = ((bf16[32,6,64,128]{3,2,1,0:T(8,128)(2,1)}), bf16[32,6,64,128]{3,2,1,0:T(8,128)(2,1)}, u32[]{:S(2)}, u32[]{:S(2)}) async-start(bf16[32,6,64,128]{3,2,1,0:T(8,128)(2,1)} %pad_maximum_fusion), calls=%async_computation.1 | async-start | bytes 6291456 | tf_op jit(solution)/shard_map/all_to_all | solution.py:255
  47.5 2.6 %constant_dynamic-slice_fusion = (bf16[1,96,64,128]{3,2,1,0:T(8,128)(2,1)S(1)}, bf16[96,64,128]{2,1,0:T(8,128)(2,1)S(1)}) fusion(bf16[2,96,64,128]{3,2,1,0:T(8,128)(2,1)} %param.8, s32[]{:T(128)S(6)} %select_n.75, s32[]{:T(128)S(6)} %select_n.76), kind=kLoop, calls=%fused_computation.51 | loop fusion | bytes 6291464 | tf_op jit(solution)/shard_map/jit(dynamic_index_in_dim)/dynamic_slice | solution.py:248
  50.1 15.2 %collective-permute-start.11 = (bf16[96,64,128]{2,1,0:T(8,128)(2,1)S(1)}, bf16[96,64,128]{2,1,0:T(8,128)(2,1)S(1)}, u32[]{:S(2)}, u32[]{:S(2)}) collective-permute-start(bf16[96,64,128]{2,1,0:T(8,128)(2,1)S(1)} %get-tuple-element.32), channel_id=1, source_target_pairs={{0,32},{1,33},{2,34},{3,35},{4,36},{5,37},{6,38},{7,39},{8,40},{9,... | collective-permute-start | bytes 4718600 | tf_op jit(solution)/shard_map/ppermute | solution.py:74
  65.4 0.8 constant_dynamic-update-slice_fusion.3
  66.2 0.8 constant_dynamic-update-slice_fusion.2
  67.0 0.8 constant_dynamic-update-slice_fusion.1
  67.9 1.9 %constant_dynamic-update-slice_fusion.refs_0_ = bf16[8,64,2048]{2,1,0:T(8,128)(2,1)} fusion(bf16[8,64,2048]{2,1,0:T(8,128)(2,1)} %constant_dynamic-update-slice_fusion.1, bf16[2,64,2048]{2,1,0:T(8,128)(2,1)} %collective-permute-done.5), kind=kLoop, calls=%fused_computation.47 | loop fusion | bytes 1048576 | tf_op jit(solution)/shard_map/concatenate | solution.py:277
  69.8 1.2 collective-permute-start.6
  70.9 0.3 collective-permute-start.7
  71.2 1.8 slice.79
  73.0 1.5 copy.18
  74.5 1.8 collective-permute-start.1
  76.3 2.0 %pad_maximum_fusion.1 = bf16[32,6,64,128]{3,2,1,0:T(8,128)(2,1)} fusion(bf16[32,3,64,128]{3,2,1,0:T(8,128)(2,1)S(1)} %bitcast.69, bf16[32,3,64,128]{3,2,1,0:T(8,128)(2,1)S(1)} %bitcast.64), kind=kLoop, calls=%fused_computation.4 | loop fusion | flops 1572864 | bytes 6291456 | tf_op jit(solution)/shard_map/concatenate | solution.py:251
  78.3 6.7 %all-to-all-start.2 = ((bf16[32,6,64,128]{3,2,1,0:T(8,128)(2,1)}), bf16[32,6,64,128]{3,2,1,0:T(8,128)(2,1)}, u32[]{:S(2)}, u32[]{:S(2)}) async-start(bf16[32,6,64,128]{3,2,1,0:T(8,128)(2,1)} %pad_maximum_fusion.1), calls=%async_computation.2 | async-start | bytes 6291456 | tf_op jit(solution)/shard_map/all_to_all | solution.py:255
  85.0 0.6 slice.58
  86.2 0.5 constant_dynamic-slice_fusion.1
  88.5 0.6 pad_add_fusion.pos_ref
  89.0 1.5 slice.80
  90.6 1.1 convert_reduce_fusion
  91.6 19.5 %collective-permute-done.6.refs_1_ = bf16[8,64,2048]{2,1,0:T(8,128)(2,1)S(1)} collective-permute-done((bf16[8,64,2048]{2,1,0:T(8,128)(2,1)}, bf16[8,64,2048]{2,1,0:T(8,128)(2,1)S(1)}, u32[]{:S(2)}, u32[]{:S(2)}) %collective-permute-start.6) | collective-permute-done | bytes 2097184 | tf_op jit(solution)/shard_map/ppermute | solution.py:74
  111.2 1.3 slice.90
  112.5 1.5 collective-permute-start.13
  114.1 13.3 %collective-permute-done.1 = bf16[8,4,4,64,128]{4,3,0,2,1:T(8,128)(2,1)} collective-permute-done((bf16[8,4,4,64,128]{4,3,0,2,1:T(8,128)(2,1)}, bf16[8,4,4,64,128]{4,3,0,2,1:T(8,128)(2,1)}, u32[]{:S(2)}, u32[]{:S(2)}) %collective-permute-start.1) | collective-permute-done | bytes 2097184 | tf_op jit(solution)/shard_map/ppermute | solution.py:74
  127.4 1.5 slice.69
  128.9 2.7 %fusion.5 = f32[4,3,128,128]{3,2,1,0:T(8,128)S(1)} fusion(bf16[8,4,4,64,128]{4,3,0,2,1:T(8,128)(2,1)} %collective-permute-done.1, f32[8,64]{1,0:T(8,128)S(1)} %convert_reduce_fusion, bf16[8,4,4,64,128]{4,3,0,2,1:T(8,128)(2,1)} %bitcast.7), kind=kOutput, calls=%fused_computation.14 | convolution fusion | flops 203685888 | bytes 3934208 | tf_op jit(solution)/shard_map/sabgp,sabgq->abpq/dot_general | solution.py:228
  131.6 1.3 fusion.8
  132.9 0.5 fusion.12
  133.4 0.3 broadcast_select_fusion
  133.7 0.8 fusion.16
  134.4 0.9 collective-permute-start.8
  135.3 1.7 collective-permute-start.9
  137.0 1.1 collective-permute-start.10
  138.1 4.8 %copy.19 = bf16[32,64,6,128]{3,2,1,0:T(8,128)(2,1)S(1)} copy(bf16[32,64,6,128]{3,1,2,0:T(8,128)(2,1)} %bitcast.33) | data formatting | bytes 6291456 | tf_op jit(solution)/shard_map/transpose | solution.py:292
  142.9 0.8 copy.28
  143.7 7.5 %shard_map.65.near_ref = bf16[6,1536,128]{2,1,0:T(8,128)(2,1)S(1)} custom-call(bf16[8,64,2048]{2,1,0:T(8,128)(2,1)} %constant_dynamic-update-slice_fusion.refs_0_, bf16[8,64,2048]{2,1,0:T(8,128)(2,1)S(1)} %collective-permute-done.6.refs_1_, bf16[8,64,2048]{2,1,0:T(8,128)(2,1)} %collective-permute-done.7.refs_2_, bf16[2048,768]{1,0:T(8,128)(2,1)S(1)} %bitcast.60), custom_call_target="tpu_custom_call" | custom-call | flops 4831838208 | bytes 11796480 | tf_op jit(solution)/shard_map/pallas_call | solution.py:93
  151.2 1.4 copy-done.3
  152.6 4.7 %collective-permute-done.12.refs_0_ = bf16[4,64,2048]{2,1,0:T(8,128)(2,1)S(1)} collective-permute-done((bf16[4,64,2048]{2,1,0:T(8,128)(2,1)S(1)}, bf16[4,64,2048]{2,1,0:T(8,128)(2,1)S(1)}, u32[]{:S(2)}, u32[]{:S(2)}) %collective-permute-start.12) | collective-permute-done | bytes 1048608 | tf_op jit(solution)/shard_map/ppermute | solution.py:74
  157.3 1.8 %shard_map.66.far_ref = bf16[6,512,128]{2,1,0:T(8,128)(2,1)S(1)} custom-call(bf16[4,64,2048]{2,1,0:T(8,128)(2,1)S(1)} %collective-permute-done.12.refs_0_, bf16[4,64,2048]{2,1,0:T(8,128)(2,1)S(1)} %collective-permute-done.13.refs_1_, bf16[2048,768]{1,0:T(8,128)(2,1)S(1)} %bitcast.61), custom_call_target="tpu_custom_call" | custom-call | flops 1610612736 | bytes 6029312 | tf_op jit(solution)/shard_map/pallas_call | solution.py:93
  159.2 0.9 copy-done.2
  160.0 5.7 %shard_map.67 = (f32[3,64,128]{2,1,0:T(8,128)}, f32[3,64,128]{2,1,0:T(8,128)}) custom-call(s32[4]{0:T(128)} %pad_add_fusion.pos_ref, bf16[6,1536,128]{2,1,0:T(8,128)(2,1)} %copy-done.3, bf16[6,512,128]{2,1,0:T(8,128)(2,1)} %copy-done.2, bf16[32,6,64,128]{3,2,1,0:T(8,128)(2,1)} %all-to-all-done.2.conduction_ref), custom_call_target="tpu_custom_call" | custom-call | flops 402653184 | bytes 7340032 | tf_op jit(solution)/shard_map/pallas_call | solution.py:164
  165.7 9.2 %collective-permute-start.14 = (f32[3,64,128]{2,1,0:T(8,128)}, f32[3,64,128]{2,1,0:T(8,128)S(1)}, u32[]{:S(2)}, u32[]{:S(2)}) collective-permute-start(f32[3,64,128]{2,1,0:T(8,128)} %get-tuple-element.30), channel_id=1, source_target_pairs={{0,32},{1,33},{2,34},{3,35},{4,36},{5,37},{6,38},{7,39},{8,40},{9,... | collective-permute-start | bytes 294920 | tf_op jit(solution)/shard_map/ppermute | solution.py:74
  175.0 0.6 copy-done.5
  175.8 2.1 %shard_map.64 = f32[2,3,64,128]{3,2,1,0:T(8,128)} custom-call(f32[2,3,64,128]{3,2,1,0:T(8,128)} %get-tuple-element.38.first_ref, f32[2,3,64,128]{3,2,1,0:T(8,128)} %copy-done.5, f32[2,3,64,128]{3,2,1,0:T(8,128)} %copy-done.6, f32[2,3,64,128]{3,2,1,0:T(8,128)} %copy-done.7), custom_call_target="tpu_custom_call" | custom-call | tf_op jit(solution)/shard_map/pallas_call | solution.py:192
  177.9 1.8 select_subtract_fusion
  (34 shorter events, 0.5 us)
Async XLA Ops:
  0.0 1.0 copy-start
  1.0 2.8 %copy-start.4 = (bf16[96,64,128]{2,1,0:T(8,128)(2,1)S(1)}, bf16[96,64,128]{2,1,0:T(8,128)(2,1)}, u32[]{:S(2)}) copy-start(bf16[96,64,128]{2,1,0:T(8,128)(2,1)} %param.6) | copy-start | bytes 4718596
  1.1 7.3 %collective-permute-start = (bf16[1,64,2048]{2,1,0:T(8,128)(2,1)S(1)}, bf16[1,64,2048]{2,1,0:T(8,128)(2,1)S(1)}, u32[]{:S(2)}, u32[]{:S(2)}) collective-permute-start(bf16[1,64,2048]{2,1,0:T(8,128)(2,1)S(1)} %constant_dynamic-slice_fusion.3), channel_id=1, source_target_pairs={{0,4},{1,5},{2,6},{3,7},{4,0},{5,1},{6,2},{7,3},{8,12},{9,13},{10,... | collective-permute-start | bytes 786440 | tf_op jit(solution)/shard_map/ppermute | solution.py:74
  8.4 30.2 %all-to-all-start = ((bf16[8,17,64,128]{3,2,1,0:T(8,128)(2,1)}), bf16[8,17,64,128]{3,2,1,0:T(8,128)(2,1)}, u32[]{:S(2)}, u32[]{:S(2)}) async-start(bf16[8,17,64,128]{3,2,1,0:T(8,128)(2,1)} %pad_maximum_fusion.2), calls=%async_computation | async-start | bytes 4456448 | tf_op jit(solution)/shard_map/all_to_all | solution.py:255
  16.1 6.6 %collective-permute-start.2 = (bf16[96,64,128]{2,1,0:T(8,128)(2,1)S(1)}, bf16[96,64,128]{2,1,0:T(8,128)(2,1)S(1)}, u32[]{:S(2)}, u32[]{:S(2)}) collective-permute-start(bf16[96,64,128]{2,1,0:T(8,128)(2,1)S(1)} %get-tuple-element.34), channel_id=1, source_target_pairs={{0,32},{1,33},{2,34},{3,35},{4,36},{5,37},{6,38},{7,39},{8,40},{9,... | collective-permute-start | bytes 4718600 | tf_op jit(solution)/shard_map/ppermute | solution.py:74
  18.3 9.5 %collective-permute-start.3 = (bf16[2,64,2048]{2,1,0:T(8,128)(2,1)S(1)}, bf16[2,64,2048]{2,1,0:T(8,128)(2,1)S(1)}, u32[]{:S(2)}, u32[]{:S(2)}) collective-permute-start(bf16[2,64,2048]{2,1,0:T(8,128)(2,1)S(1)} %pad_maximum_fusion.4), channel_id=1, source_target_pairs={{0,1},{1,2},{2,3},{3,0},{4,5},{5,6},{6,7},{7,4},{8,9},{9,10},{10,1... | collective-permute-start | bytes 1572872 | tf_op jit(solution)/shard_map/ppermute | solution.py:74
  19.6 8.4 %collective-permute-start.4 = (bf16[2,64,2048]{2,1,0:T(8,128)(2,1)S(1)}, bf16[2,64,2048]{2,1,0:T(8,128)(2,1)S(1)}, u32[]{:S(2)}, u32[]{:S(2)}) collective-permute-start(bf16[2,64,2048]{2,1,0:T(8,128)(2,1)S(1)} %pad_maximum_fusion.4), channel_id=1, source_target_pairs={{0,3},{1,0},{2,1},{3,2},{4,7},{5,4},{6,5},{7,6},{8,11},{9,8},{10,9... | collective-permute-start | bytes 1572872 | tf_op jit(solution)/shard_map/ppermute | solution.py:74
  21.1 13.5 %collective-permute-start.5 = (bf16[2,64,2048]{2,1,0:T(8,128)(2,1)S(1)}, bf16[2,64,2048]{2,1,0:T(8,128)(2,1)}, u32[]{:S(2)}, u32[]{:S(2)}) collective-permute-start(bf16[2,64,2048]{2,1,0:T(8,128)(2,1)S(1)} %pad_maximum_fusion.4), channel_id=1, source_target_pairs={{0,2},{1,3},{2,0},{3,1},{4,6},{5,7},{6,4},{7,5},{8,10},{9,11},{10,... | collective-permute-start | bytes 1572872 | tf_op jit(solution)/shard_map/ppermute | solution.py:74
  38.5 39.8 %all-to-all-start.1 = ((bf16[32,6,64,128]{3,2,1,0:T(8,128)(2,1)}), bf16[32,6,64,128]{3,2,1,0:T(8,128)(2,1)}, u32[]{:S(2)}, u32[]{:S(2)}) async-start(bf16[32,6,64,128]{3,2,1,0:T(8,128)(2,1)} %pad_maximum_fusion), calls=%async_computation.1 | async-start | bytes 6291456 | tf_op jit(solution)/shard_map/all_to_all | solution.py:255
  50.1 26.2 %collective-permute-start.11 = (bf16[96,64,128]{2,1,0:T(8,128)(2,1)S(1)}, bf16[96,64,128]{2,1,0:T(8,128)(2,1)S(1)}, u32[]{:S(2)}, u32[]{:S(2)}) collective-permute-start(bf16[96,64,128]{2,1,0:T(8,128)(2,1)S(1)} %get-tuple-element.32), channel_id=1, source_target_pairs={{0,32},{1,33},{2,34},{3,35},{4,36},{5,37},{6,38},{7,39},{8,40},{9,... | collective-permute-start | bytes 4718600 | tf_op jit(solution)/shard_map/ppermute | solution.py:74
  69.8 41.3 %collective-permute-start.6 = (bf16[8,64,2048]{2,1,0:T(8,128)(2,1)}, bf16[8,64,2048]{2,1,0:T(8,128)(2,1)S(1)}, u32[]{:S(2)}, u32[]{:S(2)}) collective-permute-start(bf16[8,64,2048]{2,1,0:T(8,128)(2,1)} %constant_dynamic-update-slice_fusion.refs_0_), channel_id=1, source_target_pairs={{0,8},{1,9},{2,10},{3,11},{4,12},{5,13},{6,14},{7,15},{8,16},{9,17... | collective-permute-start | bytes 6291464 | tf_op jit(solution)/shard_map/ppermute | solution.py:74
  70.9 40.3 %collective-permute-start.7 = (bf16[8,64,2048]{2,1,0:T(8,128)(2,1)}, bf16[8,64,2048]{2,1,0:T(8,128)(2,1)}, u32[]{:S(2)}, u32[]{:S(2)}) collective-permute-start(bf16[8,64,2048]{2,1,0:T(8,128)(2,1)} %constant_dynamic-update-slice_fusion.refs_0_), channel_id=1, source_target_pairs={{0,24},{1,25},{2,26},{3,27},{4,28},{5,29},{6,30},{7,31},{8,0},{9,1... | collective-permute-start | bytes 6291464 | tf_op jit(solution)/shard_map/ppermute | solution.py:74
  74.5 52.9 %collective-permute-start.1 = (bf16[8,4,4,64,128]{4,3,0,2,1:T(8,128)(2,1)}, bf16[8,4,4,64,128]{4,3,0,2,1:T(8,128)(2,1)}, u32[]{:S(2)}, u32[]{:S(2)}) collective-permute-start(bf16[8,4,4,64,128]{4,3,0,2,1:T(8,128)(2,1)} %bitcast.7), channel_id=1, source_target_pairs={{0,96},{1,97},{2,98},{3,99},{4,100},{5,101},{6,102},{7,103},{8,104... | collective-permute-start | bytes 6291464 | tf_op jit(solution)/shard_map/ppermute | solution.py:74
  78.3 6.7 %copy-start.8 = (s32[2,2]{1,0:T(2,128)S(1)}, s32[2,2]{1,0:T(2,128)}, u32[]{:S(2)}) copy-start(s32[2,2]{1,0:T(2,128)} %param.11) | copy-start | bytes 52
  78.3 81.8 %all-to-all-start.2 = ((bf16[32,6,64,128]{3,2,1,0:T(8,128)(2,1)}), bf16[32,6,64,128]{3,2,1,0:T(8,128)(2,1)}, u32[]{:S(2)}, u32[]{:S(2)}) async-start(bf16[32,6,64,128]{3,2,1,0:T(8,128)(2,1)} %pad_maximum_fusion.1), calls=%async_computation.2 | async-start | bytes 6291456 | tf_op jit(solution)/shard_map/all_to_all | solution.py:255
  111.2 46.2 %collective-permute-start.12 = (bf16[4,64,2048]{2,1,0:T(8,128)(2,1)S(1)}, bf16[4,64,2048]{2,1,0:T(8,128)(2,1)S(1)}, u32[]{:S(2)}, u32[]{:S(2)}) collective-permute-start(bf16[4,64,2048]{2,1,0:T(8,128)(2,1)S(1)} %slice.89), channel_id=1, source_target_pairs={{0,8},{1,9},{2,10},{3,11},{4,12},{5,13},{6,14},{7,15},{8,16},{9,17... | collective-permute-start | bytes 3145736 | tf_op jit(solution)/shard_map/ppermute | solution.py:74
  112.5 44.8 %collective-permute-start.13 = (bf16[4,64,2048]{2,1,0:T(8,128)(2,1)S(1)}, bf16[4,64,2048]{2,1,0:T(8,128)(2,1)S(1)}, u32[]{:S(2)}, u32[]{:S(2)}) collective-permute-start(bf16[4,64,2048]{2,1,0:T(8,128)(2,1)S(1)} %slice.90), channel_id=1, source_target_pairs={{0,24},{1,25},{2,26},{3,27},{4,28},{5,29},{6,30},{7,31},{8,0},{9,1... | collective-permute-start | bytes 3145736 | tf_op jit(solution)/shard_map/ppermute | solution.py:74
  134.4 40.5 %collective-permute-start.8 = (f32[2,3,64,128]{3,2,1,0:T(8,128)S(1)}, f32[2,3,64,128]{3,2,1,0:T(8,128)S(1)}, u32[]{:S(2)}, u32[]{:S(2)}) collective-permute-start(f32[2,3,64,128]{3,2,1,0:T(8,128)S(1)} %get-tuple-element.39), channel_id=1, source_target_pairs={{0,8},{1,9},{2,10},{3,11},{4,12},{5,13},{6,14},{7,15},{8,16},{9,17... | collective-permute-start | bytes 589832 | tf_op jit(solution)/shard_map/ppermute | solution.py:74
  135.3 39.7 %collective-permute-start.9 = (f32[2,3,64,128]{3,2,1,0:T(8,128)S(1)}, f32[2,3,64,128]{3,2,1,0:T(8,128)S(1)}, u32[]{:S(2)}, u32[]{:S(2)}) collective-permute-start(f32[2,3,64,128]{3,2,1,0:T(8,128)S(1)} %get-tuple-element.40), channel_id=1, source_target_pairs={{0,16},{1,17},{2,18},{3,19},{4,20},{5,21},{6,22},{7,23},{8,24},{9,... | collective-permute-start | bytes 589832 | tf_op jit(solution)/shard_map/ppermute | solution.py:74
  137.0 38.0 %collective-permute-start.10 = (f32[2,3,64,128]{3,2,1,0:T(8,128)S(1)}, f32[2,3,64,128]{3,2,1,0:T(8,128)S(1)}, u32[]{:S(2)}, u32[]{:S(2)}) collective-permute-start(f32[2,3,64,128]{3,2,1,0:T(8,128)S(1)} %get-tuple-element.37), channel_id=1, source_target_pairs={{0,24},{1,25},{2,26},{3,27},{4,28},{5,29},{6,30},{7,31},{8,0},{9,1... | collective-permute-start | bytes 589832 | tf_op jit(solution)/shard_map/ppermute | solution.py:74
  151.2 1.4 copy-start.3
  159.2 0.9 copy-start.2
  160.0 19.6 %copy-start.1 = (bf16[2,64,2048]{2,1,0:T(8,128)(2,1)S(1)}, bf16[2,64,2048]{2,1,0:T(8,128)(2,1)}, u32[]{:S(2)}) copy-start(bf16[2,64,2048]{2,1,0:T(8,128)(2,1)} %param.10) | copy-start | bytes 1572868
  165.7 12.1 %collective-permute-start.14 = (f32[3,64,128]{2,1,0:T(8,128)}, f32[3,64,128]{2,1,0:T(8,128)S(1)}, u32[]{:S(2)}, u32[]{:S(2)}) collective-permute-start(f32[3,64,128]{2,1,0:T(8,128)} %get-tuple-element.30), channel_id=1, source_target_pairs={{0,32},{1,33},{2,34},{3,35},{4,36},{5,37},{6,38},{7,39},{8,40},{9,... | collective-permute-start | bytes 294920 | tf_op jit(solution)/shard_map/ppermute | solution.py:74
  175.0 0.7 copy-start.5
  175.0 0.7 copy-start.6
  175.0 0.8 copy-start.7
